TPU v7x, 32 devices: a whole 2x2x4 slice. The times are simulated.
32 devices in a mesh: grp: 4 (over z), wide: 4 (over x, core), blk: 2 (over y).
Axes of the slice: x: 2, y: 2, z: 4, core: 2. Of those that a mesh axis runs over, the one named last changes fastest.
Arguments:
- activations: bfloat16 [2048, 8192], P('blk', ('grp', 'wide')), may hold values from -6 to 6
- out_grads: bfloat16 [2048, 8192], P('blk', ('grp', 'wide')), may hold values from -6 to 6
- in_projection: bfloat16 [8192, 32], P(('grp', 'wide')), may hold values from -0.0625 to 0.0625
- out_projection: bfloat16 [8192, 64], P(('grp', 'wide')), may hold values from -0.0625 to 0.0625
- in_inverse: float32 [32, 32], replicated, may hold values from -1 to 1
- out_inverse: float32 [64, 64], replicated, may hold values from -0.75 to 0.75
- grad_store: bfloat16 [49152, 2048], P(('grp', 'wide', 'blk')), may hold values from -0.0234375 to 0.0234375
Outputs:
- influence: float32 [64, 49152], P(None, ('grp', 'wide', 'blk'))
All inputs are finite; a program needn't handle non-finite values.
Results may differ from a plain program's by a relative error of at most 0.0029.
Values may be sent and summed in bfloat16 or wider, within the bound.
No kernel may reach another device: no remote copies, remote signals or barrier semaphores. Data moves between devices by JAX's collectives and lax.ppermute only.
A program may use at most 64 MiB of HBM per device.

v0:
```python
import jax
import jax.numpy as jnp
from jax import lax
from jax.sharding import PartitionSpec as P

SEQ = 32


highest = lax.Precision.HIGHEST


def partial_projection(activations, out_grads, in_projection, out_projection):
    contract = (((0,), (1,)), ((), ()))
    part_input = lax.dot_general(
        in_projection, activations, contract, preferred_element_type=jnp.float32
    )
    part_output = lax.dot_general(
        out_projection, out_grads, contract, preferred_element_type=jnp.float32
    )
    return jnp.concatenate([part_input, part_output], axis=0)


def build_queries(summed, in_inverse, out_inverse):
    width_in = in_inverse.shape[0]
    query_count = summed.shape[1] // SEQ
    low_input = summed[:width_in].reshape(width_in, query_count, SEQ)
    low_output = summed[width_in:].reshape(out_inverse.shape[0], query_count, SEQ)
    gradient = jnp.einsum("oqs,iqs->qoi", low_output, low_input, precision=highest)
    shaped = jnp.einsum("ao,qoi->qai", out_inverse, gradient, precision=highest)
    shaped = jnp.einsum("qai,ib->qab", shaped, in_inverse, precision=highest)
    return shaped.reshape(query_count, -1).astype(jnp.bfloat16)


def on_device(
    activations, out_grads, in_projection, out_projection, in_inverse, out_inverse, grad_store
):
    partial_sum = partial_projection(activations, out_grads, in_projection, out_projection)
    summed = lax.psum(partial_sum, ("grp", "wide"))
    queries = build_queries(summed, in_inverse, out_inverse)
    return lax.dot_general(
        lax.all_gather(queries, "blk", axis=0, tiled=True),
        grad_store,
        (((1,), (1,)), ((), ())),
        preferred_element_type=jnp.float32,
    )


def solution(mesh):
    return jax.shard_map(
        on_device,
        mesh=mesh,
        in_specs=(
            P("blk", ("grp", "wide")),
            P("blk", ("grp", "wide")),
            P(("grp", "wide"), None),
            P(("grp", "wide"), None),
            P(),
            P(),
            P(("grp", "wide", "blk"), None),
        ),
        out_specs=P(None, ("grp", "wide", "blk")),
        check_vma=False,
    )
```

profile of v0, /device:TPU:0, one launch (start us, length us, event | category | flops | bytes accessed | tf_op | source)
XLA Modules:
  0.0 129.4 jit_solution(3321797975777232962)
XLA Ops:
  6.5 0.0 copy-start
  6.5 0.0 copy-start.1
  6.5 0.0 copy-start.2
  6.5 0.0 all-reduce.2.cloned.1.call-start
  6.5 1.7 %fusion.2 = f32[32,1024]{1,0:T(8,128)S(1)} fusion(bf16[512,32]{0,1:T(8,128)(2,1)} %param.9, bf16[1024,512]{1,0:T(8,128)(2,1)} %param.7), kind=kOutput, calls=%fused_computation.5 | convolution fusion | flops 33554432 | bytes 1212416 | tf_op jit(solution)/shard_map/dot_general | solution.py:14
  8.3 0.0 copy-done
  8.3 1.3 fusion.3
  9.6 0.8 pad_maximum_fusion
  10.4 0.0 all-reduce.2.cloned.1.call-update
  10.4 93.4 %all-reduce.2.cloned.1.call-done = f32[96,1024]{1,0:T(8,128)} async-done(((f32[96,1024]{1,0:T(8,128)}), f32[96,1024]{1,0:T(8,128)}) %all-reduce.2.cloned.1.call-update) | async-done | bytes 393232 | tf_op jit(solution)/shard_map/psum | solution.py:38
  103.8 1.0 slice.8
  104.8 0.2 copy.9
  105.0 0.9 slice.9
  105.9 0.2 copy.14
  106.1 1.9 %fusion.4 = f32[32,64,32]{2,1,0:T(8,128)S(1)} fusion(f32[64,32,32]{0,2,1:T(8,128)S(1)} %bitcast.21, f32[32,32,32]{0,2,1:T(8,128)S(1)} %bitcast.20), kind=kOutput, calls=%fused_computation.7 | convolution fusion | flops 25165824 | bytes 655360 | tf_op jit(solution)/shard_map/oqs,iqs->qoi/dot_general | solution.py:28
  108.0 0.0 copy-done.1
  108.1 1.8 %convolution_bitcast_fusion = f32[32,64,32]{1,2,0:T(8,128)S(1)} fusion(f32[32,64,32]{2,1,0:T(8,128)S(1)} %fusion.4, f32[64,64]{1,0:T(8,128)S(1)} %copy-done.1), kind=kOutput, calls=%fused_computation | convolution fusion | flops 50331648 | bytes 540672 | tf_op jit(solution)/shard_map/ao,qoi->qai/dot_general | solution.py:29
  109.9 0.0 copy-done.2
  109.9 0.6 convolution_convert_fusion
  110.5 0.3 copy.11
  110.8 0.5 convert_element_type.7
  111.3 5.6 %all_gather.3 = bf16[64,2048]{1,0:T(8,128)(2,1)S(1)} all-gather(bf16[32,2048]{1,0:T(8,128)(2,1)S(1)} %convert_element_type.7), channel_id=1, replica_groups=mesh['grp'=4,'wide'=4,'blk'=2] {'blk'}, dimensions={0}, use_global_device_ids=true | all-gather | bytes 393216 | tf_op jit(solution)/shard_map/all_gather | solution.py:41
  117.0 5.6 %fusion.5 = f32[64,1536]{1,0:T(8,128)} fusion(bf16[64,2048]{1,0:T(8,128)(2,1)S(1)} %all_gather.3, bf16[1536,2048]{1,0:T(8,128)(2,1)} %param.13), kind=kOutput, calls=%fused_computation.8 | convolution fusion | flops 402653184 | bytes 6946816 | tf_op jit(solution)/shard_map/dot_general | solution.py:40
Async XLA Ops:
  6.5 1.8 %copy-start = (bf16[1024,512]{1,0:T(8,128)(2,1)S(1)}, bf16[1024,512]{1,0:T(8,128)(2,1)}, u32[]{:S(2)}) copy-start(bf16[1024,512]{1,0:T(8,128)(2,1)} %param.8) | copy-start | bytes 3145732
  6.5 101.5 %copy-start.1 = (f32[64,64]{1,0:T(8,128)S(1)}, f32[64,64]{1,0:T(8,128)}, u32[]{:S(2)}) copy-start(f32[64,64]{1,0:T(8,128)} %param.12) | copy-start | bytes 49156
  6.5 103.3 %copy-start.2 = (f32[32,32]{1,0:T(8,128)S(1)}, f32[32,32]{1,0:T(8,128)}, u32[]{:S(2)}) copy-start(f32[32,32]{1,0:T(8,128)} %param.11) | copy-start | bytes 12292
  6.5 97.3 %all-reduce.2.cloned.1.call-start = ((), (), s32[]{:S(2)}) async-start(), calls=%async_computation | async-start | bytes 786432 | tf_op jit(solution)/shard_map/psum | solution.py:38
Sparse Core Ops, SparseCore 0:
  10.7 93.0 all-reduce.1
where the time goes:
time: 130 us; the launch traced here: 129 us
  waiting for transfers between devices  93.4 us (72%)
  between operations  13.5 us (10%)
  matrix products  12.9 us (10%)
  blocking collectives  5.64 us (4%)
  local copies, waits for them, and re-layouts  3.11 us (2%)
    psum x1, waiting for transfers between devices, on_device(): summed = lax.psum(partial_sum, ('grp', 'wide'))  93.4 us
    all_gather x1, blocking collectives, on_device(): lax.all_gather(queries, 'blk', axis=0, tiled=True)  5.64 us
    dot_general x1, matrix products, on_device(): lax.dot_general(lax.all_gather(queries, 'blk', axis=0, tiled=True), grad_...  5.55 us
  transfers between devices with their start and end apart: 1, of which 1 were waited for; matrix products, arithmetic and copies ran while one was open for 0% of the time, Pallas kernels for 0%

commit v1 on v0

v1 whole, which is shorter than its diff:
```python
import functools

import jax
import jax.numpy as jnp
from jax import lax
from jax.experimental import pallas as pl
from jax.experimental.pallas import tpu as pltpu
from jax.sharding import PartitionSpec as P

SEQ = 32
VMEM = pl.BlockSpec(memory_space=pltpu.VMEM)
HBM = pl.BlockSpec(memory_space=pl.ANY)
MIB = 1 << 20


def contract(lhs, rhs, left, right):
    return lax.dot_general(
        lhs, rhs, (((left,), (right,)), ((), ())), preferred_element_type=jnp.float32
    )


def two_parts(value):
    high = value.astype(jnp.bfloat16)
    return high, (value - high.astype(jnp.float32)).astype(jnp.bfloat16)


def project_kernel(flip, acts, grads, in_proj, out_proj, out, act_buf, grad_buf, sems):
    slices, tokens = act_buf.shape[0], act_buf.shape[1]
    width_in = in_proj.shape[0]
    mine = lax.axis_index("wide")
    copies = []
    for k in range(slices):
        rows = pl.ds(pl.multiple_of((mine ^ (flip + 2 * k)) * tokens, tokens), tokens)
        for source, target, part in ((acts, act_buf, 0), (grads, grad_buf, 1)):
            copy = pltpu.make_async_copy(source.at[rows], target.at[k], sems.at[k, part])
            copy.start()
            copies.append(copy)
    for k in range(slices):
        copies[2 * k].wait()
        out[k, :width_in] = contract(in_proj[...], act_buf[k], 1, 1)
        copies[2 * k + 1].wait()
        out[k, width_in:] = contract(out_proj[...], grad_buf[k], 1, 1)


def project(flip, shards, acts, grads, in_proj, out_proj):
    tokens, features = acts.shape[0] // shards, acts.shape[1]
    slices = shards // 2
    width = in_proj.shape[0] + out_proj.shape[0]
    return pl.pallas_call(
        functools.partial(project_kernel, flip),
        out_shape=jax.ShapeDtypeStruct((slices, width, tokens), jnp.float32),
        in_specs=[HBM, HBM, VMEM, VMEM],
        out_specs=VMEM,
        scratch_shapes=[
            pltpu.VMEM((slices, tokens, features), jnp.bfloat16),
            pltpu.VMEM((slices, tokens, features), jnp.bfloat16),
            pltpu.SemaphoreType.DMA((slices, 2)),
        ],
        compiler_params=pltpu.CompilerParams(vmem_limit_bytes=8 * MIB),
        cost_estimate=pl.CostEstimate(
            flops=2 * slices * tokens * features * width,
            bytes_accessed=4 * slices * tokens * features,
            transcendentals=0,
        ),
    )(acts, grads, in_proj, out_proj)


def spread_kernel(in_inverse, out_inverse, spread_out, spread_in):
    width_out, width_in = out_inverse.shape[0], in_inverse.shape[0]
    columns, lanes = spread_out.shape[1], spread_in.shape[1]
    row = lax.broadcasted_iota(jnp.int32, (width_out, columns), 0)
    column = lax.broadcasted_iota(jnp.int32, (width_out, columns), 1)
    start = row * width_in
    repeat = ((column >= start) & (column < start + width_in)).astype(jnp.bfloat16)
    high, low = two_parts(out_inverse[...])
    high = contract(high, repeat, 0, 0).astype(jnp.bfloat16)
    low = contract(low, repeat, 0, 0).astype(jnp.bfloat16)
    spread_out[...] = jnp.concatenate([high, low, high, low], axis=0)
    row = lax.broadcasted_iota(jnp.int32, (width_in, lanes), 0)
    column = lax.broadcasted_iota(jnp.int32, (width_in, lanes), 1)
    tile = (lax.rem(column, width_in) == row).astype(jnp.bfloat16)
    high, low = two_parts(in_inverse[...])
    high = contract(high, tile, 1, 0).astype(jnp.bfloat16)
    low = contract(low, tile, 1, 0).astype(jnp.bfloat16)
    spread_in[...] = jnp.concatenate([high, low, high, low], axis=0)


def spread_inverses(in_inverse, out_inverse):
    width_in, width_out = in_inverse.shape[0], out_inverse.shape[0]
    return pl.pallas_call(
        spread_kernel,
        out_shape=(
            jax.ShapeDtypeStruct((4 * width_out, width_out * width_in), jnp.bfloat16),
            jax.ShapeDtypeStruct((4 * width_in, 128), jnp.bfloat16),
        ),
        in_specs=[VMEM, VMEM],
        out_specs=(VMEM, VMEM),
        compiler_params=pltpu.CompilerParams(vmem_limit_bytes=8 * MIB),
    )(in_inverse, out_inverse)


def query_kernel(held, got, spread_out, spread_in, out):
    width_in = spread_in.shape[0] // 4
    tokens = held.shape[1]
    queries, columns = out.shape
    lanes = spread_in.shape[1]
    low = (held[...] + got[...]).T
    in_high, in_low = two_parts(low[:, :width_in])
    out_high, out_low = two_parts(low[:, width_in:])
    side_in = jnp.concatenate([in_high, in_high, in_low, in_low], axis=1)
    side_out = jnp.concatenate([out_high, out_high, out_low, out_low], axis=1)
    spread_in_low = contract(side_in, spread_in[...], 1, 0)
    step = 256
    wide = jnp.concatenate([spread_in_low] * (step // lanes), axis=1)
    for start in range(0, columns, step):
        part = contract(side_out, spread_out[:, start : start + step], 1, 0) * wide
        part = jnp.sum(part.reshape(queries, tokens // queries, step), axis=1)
        out[:, start : start + step] = part.astype(out.dtype)


def build_queries(held, got, spread_out, spread_in):
    tokens = held.shape[1]
    return pl.pallas_call(
        query_kernel,
        out_shape=jax.ShapeDtypeStruct((tokens // SEQ, spread_out.shape[1]), jnp.bfloat16),
        in_specs=[VMEM] * 4,
        out_specs=VMEM,
        compiler_params=pltpu.CompilerParams(vmem_limit_bytes=12 * MIB),
    )(held, got, spread_out, spread_in)


def score_kernel(wide, blocks, queries, store, out):
    mine = lax.axis_index("blk")
    group = out.shape[0] // (blocks * wide)
    step = 256
    for start in range(0, out.shape[1], step):
        part = contract(queries[...], store[start : start + step], 1, 1)
        for w in range(wide):
            for s in range(blocks):
                source = (w * blocks + s) * group
                target = pl.multiple_of(((mine ^ s) * wide + w) * group, group)
                out[pl.ds(target, group), start : start + step] = part[source : source + group]


def scores(wide, blocks, queries, store):
    return pl.pallas_call(
        functools.partial(score_kernel, wide, blocks),
        out_shape=jax.ShapeDtypeStruct((queries.shape[0], store.shape[0]), jnp.float32),
        in_specs=[VMEM, VMEM],
        out_specs=VMEM,
        compiler_params=pltpu.CompilerParams(vmem_limit_bytes=20 * MIB),
    )(queries, store)


def exchange(value, axis, bit, size):
    return lax.ppermute(value, axis, [(i, i ^ bit) for i in range(size)])


def on_device(
    sizes, activations, out_grads, in_projection, out_projection, in_inverse, out_inverse, grad_store
):
    wide, groups, blocks = sizes["wide"], sizes["grp"], sizes["blk"]
    in_proj, out_proj = in_projection.T, out_projection.T
    given = project(1, wide, activations, out_grads, in_proj, out_proj)
    got = exchange(given, "wide", 1, wide)
    held = project(0, wide, activations, out_grads, in_proj, out_proj)
    held = held + got
    bit = 2
    while bit < wide:
        half = held.shape[0] // 2
        held = held[:half] + exchange(held[half:], "wide", bit, wide)
        bit *= 2
    held = held[0]
    bit = 1
    got = jnp.zeros_like(held)
    while bit < groups:
        if bit > 1:
            held = held + got
        got = exchange(held, "grp", bit, groups)
        bit *= 2
    spread_out, spread_in = spread_inverses(in_inverse, out_inverse)
    queries = build_queries(held, got, spread_out, spread_in)
    bit = 1
    while bit < blocks:
        queries = jnp.concatenate([queries, exchange(queries, "blk", bit, blocks)], axis=0)
        bit *= 2
    queries = lax.all_gather(queries, "wide", axis=0, tiled=True)
    return scores(wide, blocks, queries, grad_store)


def solution(mesh):
    return jax.shard_map(
        functools.partial(on_device, dict(mesh.shape)),
        mesh=mesh,
        in_specs=(
            P("blk", ("grp", "wide")),
            P("blk", ("grp", "wide")),
            P(("grp", "wide"), None),
            P(("grp", "wide"), None),
            P(),
            P(),
            P(("grp", "wide", "blk"), None),
        ),
        out_specs=P(None, ("grp", "wide", "blk")),
        check_vma=False,
    )
```

time: 130 us -> 37.4 us (0.29)
  waiting for transfers between devices: 93.4 us -> 8.94 us
  between operations: 13.5 us -> 0.07 us
  matrix products: 12.9 us -> 0 us
  starting transfers between devices: 0.01 us -> 9.97 us
  Pallas kernels: 0 us -> 6.06 us
  local copies, waits for them, and re-layouts: 3.11 us -> 5.92 us
    psum x1 -> x0, waiting for transfers between devices: 93.4 us -> none  [on_device(): summed = lax.psum(partial_sum, ('grp', 'wide'))]
    dot_general x6 -> x0, matrix products: 12.9 us -> none  [the longest x1 5.55 us: on_device(): lax.dot_general(lax.all_gather(queries, 'blk', axis=0, tiled=True), grad_...]
    ppermute x0 -> x5, starting transfers between devices: none -> 9.97 us  [exchange(): return lax.ppermute(value, axis, [(i, i ^ bit) for i in range(size)])]
    ppermute x0 -> x5, waiting for transfers between devices: none -> 8.94 us  [exchange(): return lax.ppermute(value, axis, [(i, i ^ bit) for i in range(size)])]
    pallas_call x0 -> x5, Pallas kernels: none -> 6.06 us  [the longest x1 2.77 us: scores(): pl.pallas_call(functools.partial(score_kernel, wide, blocks), out_shape=j...]
    unnamed x6 -> x14, local copies, waits for them, and re-layouts: 0.02 us -> 5.92 us
    slice x3 -> x1, local copies, waits for them, and re-layouts: 2.08 us -> 0.01 us  [on_device(): held = held[:half] + exchange(held[half:], 'wide', bit, wide)]
  transfers between devices with their start and end apart: 1 -> 5, of which waited for: 1 -> 4; matrix products, arithmetic and copies ran while one was open for 0% -> 0% of each run, Pallas kernels for 0% -> 4%
where the time goes in v1:
time: 37.4 us; the launch traced here: 37 us
  starting transfers between devices  9.97 us (27%)
  waiting for transfers between devices  8.94 us (24%)
  Pallas kernels  6.06 us (16%)
  blocking collectives  5.99 us (16%)
  local copies, waits for them, and re-layouts  5.92 us (16%)
    ppermute x5, starting transfers between devices, exchange(): return lax.ppermute(value, axis, [(i, i ^ bit) for i in range(size)])  9.97 us
    ppermute x5, waiting for transfers between devices, exchange(): return lax.ppermute(value, axis, [(i, i ^ bit) for i in range(size)])  8.94 us
    all_gather x1, blocking collectives, on_device(): queries = lax.all_gather(queries, 'wide', axis=0, tiled=True)  5.99 us
    unnamed x14, local copies, waits for them, and re-layouts  5.92 us
    pallas_call x1, Pallas kernels, scores(): pl.pallas_call(functools.partial(score_kernel, wide, blocks), out_shape=j...  2.77 us
    pallas_call x2, Pallas kernels, project(): pl.pallas_call(functools.partial(project_kernel, flip), out_shape=jax.Sha...  2.3 us
  transfers between devices with their start and end apart: 5, of which 4 were waited for; matrix products, arithmetic and copies ran while one was open for 0% of the time, Pallas kernels for 4%

profile of v1, /device:TPU:0, one launch (start us, length us, event | category | flops | bytes accessed | tf_op | source)
XLA Modules:
  0.0 37.0 jit_solution(13116289379509564775)
XLA Ops:
  0.0 0.0 copy-start
  0.0 0.0 copy-start.1
  0.0 1.4 %copy-done.1 = bf16[1024,512]{1,0:T(8,128)(2,1)S(1)} copy-done((bf16[1024,512]{1,0:T(8,128)(2,1)S(1)}, bf16[1024,512]{1,0:T(8,128)(2,1)}, u32[]{:S(2)}) %copy-start.1) | copy-done | bytes 1048600
  1.4 0.0 copy-start.2
  1.4 1.5 %copy-done.2 = bf16[1024,512]{1,0:T(8,128)(2,1)S(1)} copy-done((bf16[1024,512]{1,0:T(8,128)(2,1)S(1)}, bf16[1024,512]{1,0:T(8,128)(2,1)}, u32[]{:S(2)}) %copy-start.2) | copy-done | bytes 1048600
  2.8 0.0 copy-start.3
  2.8 0.8 %copy-done.3 = bf16[512,64]{0,1:T(8,128)(2,1)S(1)} copy-done((bf16[512,64]{0,1:T(8,128)(2,1)S(1)}, bf16[512,64]{0,1:T(8,128)(2,1)}, u32[]{:S(2)}) %copy-start.3) | copy-done | bytes 65560
  3.7 0.0 copy-start.4
  3.7 0.8 %copy-done.4 = bf16[512,32]{0,1:T(8,128)(2,1)S(1)} copy-done((bf16[512,32]{0,1:T(8,128)(2,1)S(1)}, bf16[512,32]{0,1:T(8,128)(2,1)}, u32[]{:S(2)}) %copy-start.4) | copy-done | bytes 32792
  4.4 1.2 %shard_map.74 = f32[2,96,256]{2,1,0:T(8,128)S(1)} custom-call(bf16[1024,512]{1,0:T(8,128)(2,1)S(1)} %copy-done.1, bf16[1024,512]{1,0:T(8,128)(2,1)S(1)} %copy-done.2, bf16[32,512]{1,0:T(8,128)(2,1)S(1)} %bitcast.6, bf16[64,512]{1,0:T(8,128)(2,1)S(1)} %bitcast.4), custom_call_target="tpu_custom_call" | custom-call | flops 50331648 | bytes 1048576 | tf_op jit(solution)/shard_map/pallas_call | solution.py:49
  5.6 0.5 %collective-permute-start = (f32[2,96,256]{2,1,0:T(8,128)S(1)}, f32[2,96,256]{2,1,0:T(8,128)S(1)}, u32[]{:S(2)}, u32[]{:S(2)}) collective-permute-start(f32[2,96,256]{2,1,0:T(8,128)S(1)} %shard_map.74), channel_id=1, source_target_pairs={{0,2},{2,0},{4,6},{6,4},{1,3},{3,1},{5,7},{7,5},{8,10},{10,8},{12,... | collective-permute-start | bytes 589832 | tf_op jit(solution)/shard_map/ppermute | solution.py:156
  6.1 1.2 %shard_map.73 = f32[2,96,256]{2,1,0:T(8,128)S(1)} custom-call(bf16[1024,512]{1,0:T(8,128)(2,1)S(1)} %copy-done.1, bf16[1024,512]{1,0:T(8,128)(2,1)S(1)} %copy-done.2, bf16[32,512]{1,0:T(8,128)(2,1)S(1)} %bitcast.7, bf16[64,512]{1,0:T(8,128)(2,1)S(1)} %bitcast.5), custom_call_target="tpu_custom_call" | custom-call | flops 50331648 | bytes 1048576 | tf_op jit(solution)/shard_map/pallas_call | solution.py:49
  7.3 0.0 collective-permute-done
  7.3 2.8 %collective-permute-start.1 = (f32[1,96,256]{2,1,0:T(8,128)S(1)}, f32[1,96,256]{2,1,0:T(8,128)S(1)}, u32[]{:S(2)}, u32[]{:S(2)}) collective-permute-start(f32[1,96,256]{2,1,0:T(8,128)S(1)} %slice.9), channel_id=1, source_target_pairs={{0,4},{2,6},{4,0},{6,2},{1,5},{3,7},{5,1},{7,3},{8,12},{10,14},{12... | collective-permute-start | bytes 294920 | tf_op jit(solution)/shard_map/ppermute | solution.py:156
  10.2 3.2 %collective-permute-done.1 = f32[1,96,256]{2,1,0:T(8,128)S(1)} collective-permute-done((f32[1,96,256]{2,1,0:T(8,128)S(1)}, f32[1,96,256]{2,1,0:T(8,128)S(1)}, u32[]{:S(2)}, u32[]{:S(2)}) %collective-permute-start.1) | collective-permute-done | bytes 98336 | tf_op jit(solution)/shard_map/ppermute | solution.py:156
  13.4 1.9 %collective-permute-start.2 = (f32[96,256]{1,0:T(8,128)S(1)}, f32[96,256]{1,0:T(8,128)S(1)}, u32[]{:S(2)}, u32[]{:S(2)}) collective-permute-start(f32[96,256]{1,0:T(8,128)S(1)} %fusion), channel_id=1, source_target_pairs={{0,8},{8,0},{16,24},{24,16},{1,9},{9,1},{17,25},{25,17},{2,10},{10... | collective-permute-start | bytes 294920 | tf_op jit(solution)/shard_map/ppermute | solution.py:156
  15.3 2.8 %collective-permute-done.2 = f32[96,256]{1,0:T(8,128)S(1)} collective-permute-done((f32[96,256]{1,0:T(8,128)S(1)}, f32[96,256]{1,0:T(8,128)S(1)}, u32[]{:S(2)}, u32[]{:S(2)}) %collective-permute-start.2) | collective-permute-done | bytes 98336 | tf_op jit(solution)/shard_map/ppermute | solution.py:156
  18.1 2.9 %collective-permute-start.3 = (f32[96,256]{1,0:T(8,128)S(1)}, f32[96,256]{1,0:T(8,128)S(1)}, u32[]{:S(2)}, u32[]{:S(2)}) collective-permute-start(f32[96,256]{1,0:T(8,128)S(1)} %add.11.held), channel_id=1, source_target_pairs={{0,16},{8,24},{16,0},{24,8},{1,17},{9,25},{17,1},{25,9},{2,18},{10... | collective-permute-start | bytes 294920 | tf_op jit(solution)/shard_map/ppermute | solution.py:156
  21.0 0.0 copy-start.5
  21.0 0.8 %copy-done.5 = f32[64,64]{1,0:T(8,128)S(1)} copy-done((f32[64,64]{1,0:T(8,128)S(1)}, f32[64,64]{1,0:T(8,128)}, u32[]{:S(2)}) %copy-start.5) | copy-done | bytes 16408
  21.7 0.0 copy-start.6
  21.7 0.7 %copy-done.6 = f32[32,32]{1,0:T(8,128)S(1)} copy-done((f32[32,32]{1,0:T(8,128)S(1)}, f32[32,32]{1,0:T(8,128)}, u32[]{:S(2)}) %copy-start.6) | copy-done | bytes 4120
  22.5 0.4 %shard_map.75 = (bf16[256,2048]{1,0:T(8,128)(2,1)S(1)}, bf16[128,128]{1,0:T(8,128)(2,1)S(1)}) custom-call(f32[32,32]{1,0:T(8,128)S(1)} %copy-done.6, f32[64,64]{1,0:T(8,128)S(1)} %copy-done.5), custom_call_target="tpu_custom_call" | custom-call | tf_op jit(solution)/shard_map/pallas_call | solution.py:90
  22.9 0.8 %collective-permute-done.3.got = f32[96,256]{1,0:T(8,128)S(1)} collective-permute-done((f32[96,256]{1,0:T(8,128)S(1)}, f32[96,256]{1,0:T(8,128)S(1)}, u32[]{:S(2)}, u32[]{:S(2)}) %collective-permute-start.3) | collective-permute-done | bytes 98336 | tf_op jit(solution)/shard_map/ppermute | solution.py:156
  23.7 0.6 %shard_map.76 = bf16[8,2048]{1,0:T(8,128)(2,1)S(1)} custom-call(f32[96,256]{1,0:T(8,128)S(1)} %add.11.held, f32[96,256]{1,0:T(8,128)S(1)} %collective-permute-done.3.got, bf16[256,2048]{1,0:T(8,128)(2,1)S(1)} %get-tuple-element.7.spread_out, bf16[128,128]{1,0:T(8,128)(2,1)S(1)} %get-tuple-element.8.spread_in), custom_call_target="tpu_custom_call" | custom-call | tf_op jit(solution)/shard_map/pallas_call | solution.py:123
  24.3 1.8 %collective-permute-start.4 = (bf16[8,2048]{1,0:T(8,128)(2,1)S(1)}, bf16[8,2048]{1,0:T(8,128)(2,1)S(1)}, u32[]{:S(2)}, u32[]{:S(2)}) collective-permute-start(bf16[8,2048]{1,0:T(8,128)(2,1)S(1)} %shard_map.76), channel_id=1, source_target_pairs={{0,1},{1,0},{2,3},{3,2},{4,5},{5,4},{6,7},{7,6},{8,9},{9,8},{10,11... | collective-permute-start | bytes 98312 | tf_op jit(solution)/shard_map/ppermute | solution.py:156
  26.1 2.1 %collective-permute-done.4 = bf16[8,2048]{1,0:T(8,128)(2,1)S(1)} collective-permute-done((bf16[8,2048]{1,0:T(8,128)(2,1)S(1)}, bf16[8,2048]{1,0:T(8,128)(2,1)S(1)}, u32[]{:S(2)}, u32[]{:S(2)}) %collective-permute-start.4) | collective-permute-done | bytes 32800 | tf_op jit(solution)/shard_map/ppermute | solution.py:156
  28.3 6.0 %all_gather.3.queries = bf16[64,2048]{1,0:T(8,128)(2,1)S(1)} all-gather(bf16[16,2048]{1,0:T(8,128)(2,1)S(1)} %pad_maximum_fusion), channel_id=1, replica_groups=mesh['grp'=4,'wide'=4,'blk'=2] {'wide'}, dimensions={0}, use_global_device_ids=true | all-gather | bytes 327680 | tf_op jit(solution)/shard_map/all_gather | solution.py:187
  34.3 0.0 copy-done
  34.3 2.8 %shard_map.77 = f32[64,1536]{1,0:T(8,128)} custom-call(bf16[64,2048]{1,0:T(8,128)(2,1)S(1)} %all_gather.3.queries, bf16[1536,2048]{1,0:T(8,128)(2,1)S(1)} %copy-done), custom_call_target="tpu_custom_call" | custom-call | tf_op jit(solution)/shard_map/pallas_call | solution.py:146
  (5 shorter events, 0.1 us)
Async XLA Ops:
  0.0 34.3 %copy-start = (bf16[1536,2048]{1,0:T(8,128)(2,1)S(1)}, bf16[1536,2048]{1,0:T(8,128)(2,1)}, u32[]{:S(2)}) copy-start(bf16[1536,2048]{1,0:T(8,128)(2,1)} %store.1) | copy-start | bytes 18874372
  0.0 1.4 %copy-start.1 = (bf16[1024,512]{1,0:T(8,128)(2,1)S(1)}, bf16[1024,512]{1,0:T(8,128)(2,1)}, u32[]{:S(2)}) copy-start(bf16[1024,512]{1,0:T(8,128)(2,1)} %acts.3) | copy-start | bytes 3145732
  1.4 1.5 %copy-start.2 = (bf16[1024,512]{1,0:T(8,128)(2,1)S(1)}, bf16[1024,512]{1,0:T(8,128)(2,1)}, u32[]{:S(2)}) copy-start(bf16[1024,512]{1,0:T(8,128)(2,1)} %grads.3) | copy-start | bytes 3145732
  2.8 0.8 %copy-start.3 = (bf16[512,64]{0,1:T(8,128)(2,1)S(1)}, bf16[512,64]{0,1:T(8,128)(2,1)}, u32[]{:S(2)}) copy-start(bf16[512,64]{0,1:T(8,128)(2,1)} %param.10) | copy-start | bytes 196612
  3.7 0.8 %copy-start.4 = (bf16[512,32]{0,1:T(8,128)(2,1)S(1)}, bf16[512,32]{0,1:T(8,128)(2,1)}, u32[]{:S(2)}) copy-start(bf16[512,32]{0,1:T(8,128)(2,1)} %param.9) | copy-start | bytes 98308
  5.6 1.7 %collective-permute-start = (f32[2,96,256]{2,1,0:T(8,128)S(1)}, f32[2,96,256]{2,1,0:T(8,128)S(1)}, u32[]{:S(2)}, u32[]{:S(2)}) collective-permute-start(f32[2,96,256]{2,1,0:T(8,128)S(1)} %shard_map.74), channel_id=1, source_target_pairs={{0,2},{2,0},{4,6},{6,4},{1,3},{3,1},{5,7},{7,5},{8,10},{10,8},{12,... | collective-permute-start | bytes 589832 | tf_op jit(solution)/shard_map/ppermute | solution.py:156
  7.3 6.0 %collective-permute-start.1 = (f32[1,96,256]{2,1,0:T(8,128)S(1)}, f32[1,96,256]{2,1,0:T(8,128)S(1)}, u32[]{:S(2)}, u32[]{:S(2)}) collective-permute-start(f32[1,96,256]{2,1,0:T(8,128)S(1)} %slice.9), channel_id=1, source_target_pairs={{0,4},{2,6},{4,0},{6,2},{1,5},{3,7},{5,1},{7,3},{8,12},{10,14},{12... | collective-permute-start | bytes 294920 | tf_op jit(solution)/shard_map/ppermute | solution.py:156
  13.4 4.7 %collective-permute-start.2 = (f32[96,256]{1,0:T(8,128)S(1)}, f32[96,256]{1,0:T(8,128)S(1)}, u32[]{:S(2)}, u32[]{:S(2)}) collective-permute-start(f32[96,256]{1,0:T(8,128)S(1)} %fusion), channel_id=1, source_target_pairs={{0,8},{8,0},{16,24},{24,16},{1,9},{9,1},{17,25},{25,17},{2,10},{10... | collective-permute-start | bytes 294920 | tf_op jit(solution)/shard_map/ppermute | solution.py:156
  18.1 5.6 %collective-permute-start.3 = (f32[96,256]{1,0:T(8,128)S(1)}, f32[96,256]{1,0:T(8,128)S(1)}, u32[]{:S(2)}, u32[]{:S(2)}) collective-permute-start(f32[96,256]{1,0:T(8,128)S(1)} %add.11.held), channel_id=1, source_target_pairs={{0,16},{8,24},{16,0},{24,8},{1,17},{9,25},{17,1},{25,9},{2,18},{10... | collective-permute-start | bytes 294920 | tf_op jit(solution)/shard_map/ppermute | solution.py:156
  21.0 0.8 %copy-start.5 = (f32[64,64]{1,0:T(8,128)S(1)}, f32[64,64]{1,0:T(8,128)}, u32[]{:S(2)}) copy-start(f32[64,64]{1,0:T(8,128)} %out_inverse.1) | copy-start | bytes 49156
  21.7 0.7 %copy-start.6 = (f32[32,32]{1,0:T(8,128)S(1)}, f32[32,32]{1,0:T(8,128)}, u32[]{:S(2)}) copy-start(f32[32,32]{1,0:T(8,128)} %in_inverse.1) | copy-start | bytes 12292
  24.3 4.0 %collective-permute-start.4 = (bf16[8,2048]{1,0:T(8,128)(2,1)S(1)}, bf16[8,2048]{1,0:T(8,128)(2,1)S(1)}, u32[]{:S(2)}, u32[]{:S(2)}) collective-permute-start(bf16[8,2048]{1,0:T(8,128)(2,1)S(1)} %shard_map.76), channel_id=1, source_target_pairs={{0,1},{1,0},{2,3},{3,2},{4,5},{5,4},{6,7},{7,6},{8,9},{9,8},{10,11... | collective-permute-start | bytes 98312 | tf_op jit(solution)/shard_map/ppermute | solution.py:156

commit v2 on v1

v2 whole, which is shorter than its diff:
```python
import functools
import itertools

import jax
import jax.numpy as jnp
from jax import lax
from jax.experimental import pallas as pl
from jax.experimental.pallas import tpu as pltpu
from jax.sharding import PartitionSpec as P

SEQ = 32
VMEM = pl.BlockSpec(memory_space=pltpu.VMEM)
HBM = pl.BlockSpec(memory_space=pltpu.HBM)
MIB = 1 << 20


def contract(lhs, rhs, left, right):
    return lax.dot_general(
        lhs, rhs, (((left,), (right,)), ((), ())), preferred_element_type=jnp.float32
    )


def two_parts(value):
    high = value.astype(jnp.bfloat16)
    return high, (value - high.astype(jnp.float32)).astype(jnp.bfloat16)


def odd_bits(value):
    for shift in (16, 8, 4, 2, 1):
        value = value ^ (value >> shift)
    return value & 1


def exchange(value, sizes, wide=0, grp=0, blk=0):
    flip = odd_bits(wide) ^ odd_bits(grp >> 1)
    return swap(value, sizes, {"wide": 2 * wide + flip, "grp": grp, "blk": blk})


def swap(value, sizes, far):
    axes = tuple(sizes)
    coordinates = list(itertools.product(*(range(sizes[a]) for a in axes)))
    index = {c: i for i, c in enumerate(coordinates)}
    pairs = [
        (i, index[tuple(p ^ far.get(a, 0) for p, a in zip(c, axes))])
        for c, i in index.items()
    ]
    return lax.ppermute(value, axes, pairs)


def own_half():
    slot, group = lax.axis_index("wide"), lax.axis_index("grp")
    return lax.rem(slot, 2) ^ odd_bits(slot // 2) ^ odd_bits(group // 2)


def project_kernel(
    lows, width_in, acts, grads, proj, given, kept, act_buf, grad_buf, sems
):
    slices, spans = given.shape[0], given.shape[0] // lows
    tokens = given.shape[2]
    half = own_half()
    x, low = lax.axis_index("wide") // 2, lax.rem(lax.axis_index("grp"), lows)
    copies = []
    for k in range(2 * spans):
        first = ((x ^ (k % spans)) * 2 + (half ^ (k < spans))) * lows * tokens
        rows = pl.ds(pl.multiple_of(first, lows * tokens), lows * tokens)
        for source, target, part in ((acts, act_buf, 0), (grads, grad_buf, 1)):
            copy = pltpu.make_async_copy(source.at[rows], target.at[k], sems.at[k, part])
            copy.start()
            copies.append(copy)
    for k in range(2 * spans):
        copies[2 * k].wait()
        copies[2 * k + 1].wait()
        low_in = contract(proj[:width_in], act_buf[k], 1, 1)
        low_out = contract(proj[width_in:], grad_buf[k], 1, 1)
        out = given if k < spans else kept
        for place in range(lows):
            slot = (k % spans) * lows + (low ^ place)
            lanes = slice(place * tokens, (place + 1) * tokens)
            out[slot, :width_in] = low_in[:, lanes]
            out[slot, width_in:] = low_out[:, lanes]


def project(slices, lows, acts, grads, proj, width_in):
    tokens, features = acts.shape[0] // (2 * slices), acts.shape[1]
    width = proj.shape[0]
    spans = slices // lows
    out = jax.ShapeDtypeStruct((slices, width, tokens), jnp.float32)
    return pl.pallas_call(
        functools.partial(project_kernel, lows, width_in),
        out_shape=(out, out),
        in_specs=[HBM] * 2 + [VMEM],
        out_specs=(VMEM, VMEM),
        scratch_shapes=[
            pltpu.VMEM((2 * spans, tokens * lows, features), jnp.bfloat16),
            pltpu.VMEM((2 * spans, tokens * lows, features), jnp.bfloat16),
            pltpu.SemaphoreType.DMA((2 * spans + 1, 2)),
        ],
        compiler_params=pltpu.CompilerParams(vmem_limit_bytes=55885824),
        cost_estimate=pl.CostEstimate(
            flops=4 * slices * tokens * features * width,
            bytes_accessed=8 * slices * tokens * features,
            transcendentals=0,
        ),
    )(acts, grads, proj)


def spread_kernel(in_inverse, out_inverse, spread_out, spread_in):
    width_out, width_in = out_inverse.shape[0], in_inverse.shape[0]
    columns, lanes = spread_out.shape[1], spread_in.shape[1]
    row = lax.broadcasted_iota(jnp.int32, (width_out, columns), 0)
    column = lax.broadcasted_iota(jnp.int32, (width_out, columns), 1)
    start = row * width_in
    repeat = ((column >= start) & (column < start + width_in)).astype(jnp.bfloat16)
    high, low = two_parts(out_inverse[...])
    high = contract(high, repeat, 0, 0).astype(jnp.bfloat16)
    low = contract(low, repeat, 0, 0).astype(jnp.bfloat16)
    spread_out[...] = jnp.concatenate([high, low, high, low], axis=0)
    row = lax.broadcasted_iota(jnp.int32, (width_in, lanes), 0)
    column = lax.broadcasted_iota(jnp.int32, (width_in, lanes), 1)
    tile = (lax.rem(column, width_in) == row).astype(jnp.bfloat16)
    high, low = two_parts(in_inverse[...])
    high = contract(high, tile, 1, 0).astype(jnp.bfloat16)
    low = contract(low, tile, 1, 0).astype(jnp.bfloat16)
    spread_in[...] = jnp.concatenate([high, low, high, low], axis=0)


def spread_inverses(in_inverse, out_inverse):
    width_in, width_out = in_inverse.shape[0], out_inverse.shape[0]
    return pl.pallas_call(
        spread_kernel,
        out_shape=(
            jax.ShapeDtypeStruct((4 * width_out, width_out * width_in), jnp.bfloat16),
            jax.ShapeDtypeStruct((4 * width_in, 128), jnp.bfloat16),
        ),
        in_specs=[VMEM, VMEM],
        out_specs=(VMEM, VMEM),
        compiler_params=pltpu.CompilerParams(vmem_limit_bytes=8 * MIB),
        cost_estimate=pl.CostEstimate(flops=1 << 33, bytes_accessed=16 * MIB, transcendentals=0),
    )(in_inverse, out_inverse)


def query_kernel(held, got, spread_out, spread_in, out):
    width_in = spread_in.shape[0] // 4
    tokens = held.shape[1]
    queries, columns = out.shape
    lanes = spread_in.shape[1]
    low = (held[...] + got[...]).T
    in_high, in_low = two_parts(low[:, :width_in])
    out_high, out_low = two_parts(low[:, width_in:])
    side_in = jnp.concatenate([in_high, in_high, in_low, in_low], axis=1)
    side_out = jnp.concatenate([out_high, out_high, out_low, out_low], axis=1)
    spread_in_low = contract(side_in, spread_in[...], 1, 0)
    step = 256
    wide = jnp.concatenate([spread_in_low] * (step // lanes), axis=1)
    for start in range(0, columns, step):
        part = contract(side_out, spread_out[:, start : start + step], 1, 0) * wide
        part = jnp.sum(part.reshape(queries, tokens // queries, step), axis=1)
        out[:, start : start + step] = part.astype(out.dtype)


def build_queries(held, got, spread_out, spread_in):
    tokens = held.shape[1]
    return pl.pallas_call(
        query_kernel,
        out_shape=jax.ShapeDtypeStruct((tokens // SEQ, spread_out.shape[1]), jnp.bfloat16),
        in_specs=[VMEM] * 4,
        out_specs=VMEM,
        compiler_params=pltpu.CompilerParams(vmem_limit_bytes=12 * MIB),
        cost_estimate=pl.CostEstimate(flops=1 << 33, bytes_accessed=16 * MIB, transcendentals=0),
    )(held, got, spread_out, spread_in)


def score_kernel(order, wide, lows, held, got, store, out):
    blk, x, half = lax.axis_index("blk"), lax.axis_index("wide") // 2, own_half()
    queries = jnp.concatenate([held[...], got[...]], axis=0)
    rows = out.shape[0] // len(order)
    targets = [
        pl.multiple_of((((blk ^ far_blk) * (wide // 2) + (x ^ far_x)) * 2 + (half ^ flip)) * rows, rows)
        for far_blk, far_x, flip in order
    ]
    step = 512
    swapped = lax.rem(lax.axis_index("grp"), lows) == 1
    for start in range(0, out.shape[1], step):
        part = contract(queries, store[start : start + step], 1, 1)
        part = part.reshape(len(order), rows, step)
        if lows > 1:
            part = jnp.where(swapped, jnp.roll(part, rows // 2, axis=1), part)
        for r, row in enumerate(targets):
            out[pl.ds(row, rows), start : start + step] = part[r]


def scores(order, wide, lows, held, got, store):
    return pl.pallas_call(
        functools.partial(score_kernel, order, wide, lows),
        out_shape=jax.ShapeDtypeStruct((2 * held.shape[0], store.shape[0]), jnp.float32),
        in_specs=[VMEM] * 3,
        out_specs=VMEM,
        compiler_params=pltpu.CompilerParams(vmem_limit_bytes=20 * MIB),
    )(held, got, store)


def stack(pieces):
    rows = pieces[0].shape[0]
    zero = jnp.zeros((), pieces[0].dtype)
    return sum(
        lax.pad(piece, zero, ((n * rows, (len(pieces) - 1 - n) * rows, 0), (0, 0, 0)))
        for n, piece in enumerate(pieces)
    )


def on_device(
    sizes, activations, out_grads, in_projection, out_projection, in_inverse, out_inverse, grad_store
):
    wide, groups, blocks = sizes["wide"], sizes["grp"], sizes["blk"]
    spans, lows = wide // 2, min(groups, 2)
    slices = spans * lows
    given, kept = project(
        slices, lows, activations, out_grads, jnp.concatenate([in_projection.T, out_projection.T], axis=0), in_inverse.shape[0]
    )
    both = kept + swap(given, sizes, {"wide": 1})
    held = both[0]
    for k in range(slices - 1, 0, -1):
        held = held + exchange(both[k], sizes, wide=k // lows, grp=k % lows)
    last = jnp.zeros_like(held)
    bit = lows
    while bit < groups:
        if bit > lows:
            held = held + last
        last = exchange(held, sizes, grp=bit)
        bit *= 2
    spread_out, spread_in = spread_inverses(in_inverse, out_inverse)
    queries = build_queries(held, last, spread_out, spread_in)
    if lows > 1:
        other = exchange(queries, sizes, grp=1)
        queries = jnp.concatenate([queries, other], axis=0)
    order = [(0, 0)]
    bit = 2
    while bit < blocks:
        queries = jnp.concatenate([queries, exchange(queries, sizes, blk=bit)], axis=0)
        order += [(b ^ bit, x) for b, x in order]
        bit *= 2
    near = [(b, x) for x in range(spans) for b in range(min(blocks, 2))]
    others = [exchange(queries, sizes, blk=b, wide=x) for b, x in near[:0:-1]]
    queries = stack([queries] + others[::-1])
    order = [(b ^ c, x ^ y) for c, y in near for b, x in order]
    order = tuple((b, x, flip) for flip in range(2) for b, x in order)
    return scores(order, wide, lows, queries, swap(queries, sizes, {"wide": 1}), grad_store)


def solution(mesh):
    return jax.shard_map(
        functools.partial(on_device, dict(mesh.shape)),
        mesh=mesh,
        in_specs=(
            P("blk", ("grp", "wide")),
            P("blk", ("grp", "wide")),
            P(("grp", "wide"), None),
            P(("grp", "wide"), None),
            P(),
            P(),
            P(("grp", "wide", "blk"), None),
        ),
        out_specs=P(None, ("grp", "wide", "blk")),
        check_vma=False,
    )
```

time: 37.4 us -> 33 us (0.88)
  blocking collectives: 5.99 us -> 0 us
  local copies, waits for them, and re-layouts: 5.92 us -> 1.49 us
  waiting for transfers between devices: 8.94 us -> 11.7 us
  starting transfers between devices: 9.97 us -> 12.5 us
  other arithmetic: 0.06 us -> 0.93 us
    all_gather x1 -> x0, blocking collectives: 5.99 us -> none  [on_device(): queries = lax.all_gather(queries, 'wide', axis=0, tiled=True)]
    unnamed x14 -> x8, local copies, waits for them, and re-layouts: 5.92 us -> 1.48 us
    ppermute x5 -> x10, waiting for transfers between devices: 8.94 us -> 11.7 us  [swap(): return lax.ppermute(value, axes, pairs)]
    ppermute x5 -> x10, starting transfers between devices: 9.97 us -> 12.5 us  [swap(): return lax.ppermute(value, axes, pairs)]
    concatenate x1 -> x2, other arithmetic: 0.01 us -> 0.87 us  [the longest x1 0.85 us: on_device(): jnp.concatenate([in_projection.T, out_projection.T], axis=0)]
    pallas_call x3 -> x2, Pallas kernels: 5.07 us -> 5.02 us  [the longest x1 2.76 us: scores(): pl.pallas_call(functools.partial(score_kernel, order, wide, lows), out_sh...]
  transfers between devices with their start and end apart: 5 -> 10, of which waited for: 4 -> 10; matrix products, arithmetic and copies ran while one was open for 0% -> 0% of each run, Pallas kernels for 4% -> 1%
where the time goes in v2:
time: 33 us; the launch traced here: 32.6 us
  starting transfers between devices  12.5 us (38%)
  waiting for transfers between devices  11.7 us (35%)
  Pallas kernels  5.86 us (18%)
  local copies, waits for them, and re-layouts  1.49 us (5%)
  other arithmetic  0.93 us (3%)
    ppermute x10, starting transfers between devices, swap(): return lax.ppermute(value, axes, pairs)  12.5 us
    ppermute x10, waiting for transfers between devices, swap(): return lax.ppermute(value, axes, pairs)  11.7 us
    pallas_call x1, Pallas kernels, scores(): pl.pallas_call(functools.partial(score_kernel, order, wide, lows), out_sh...  2.76 us
    pallas_call x1, Pallas kernels, project(): pl.pallas_call(functools.partial(project_kernel, lows, width_in), out_sha...  2.26 us
    unnamed x8, local copies, waits for them, and re-layouts  1.48 us
    concatenate x1, other arithmetic, on_device(): jnp.concatenate([in_projection.T, out_projection.T], axis=0)  0.85 us
  transfers between devices with their start and end apart: 10, of which 10 were waited for; matrix products, arithmetic and copies ran while one was open for 0% of the time, Pallas kernels for 1%

profile of v2, /device:TPU:0, one launch (start us, length us, event | category | flops | bytes accessed | tf_op | source)
XLA Modules:
  0.0 32.6 jit_solution(11752383607537329422)
XLA Ops:
  0.0 0.8 %pad_maximum_fusion.proj = bf16[96,512]{1,0:T(8,128)(2,1)S(1)} fusion(bf16[64,512]{1,0:T(8,128)(2,1)} %bitcast.18, bf16[32,512]{1,0:T(8,128)(2,1)} %bitcast.19), kind=kLoop, calls=%fused_computation.1 | loop fusion | flops 196608 | bytes 196608 | tf_op jit(solution)/shard_map/concatenate | solution.py:218
  0.8 2.3 %shard_map.73 = (f32[4,96,128]{2,1,0:T(8,128)S(1)}, f32[4,96,128]{2,1,0:T(8,128)S(1)}) custom-call(bf16[1024,512]{1,0:T(8,128)(2,1)} %acts.1, bf16[1024,512]{1,0:T(8,128)(2,1)} %grads.1, bf16[96,512]{1,0:T(8,128)(2,1)S(1)} %pad_maximum_fusion.proj), custom_call_target="tpu_custom_call" | custom-call | flops 100663296 | bytes 2097152 | tf_op jit(solution)/shard_map/pallas_call | solution.py:88
  3.1 0.5 %collective-permute-start = (f32[4,96,128]{2,1,0:T(8,128)S(1)}, f32[4,96,128]{2,1,0:T(8,128)S(1)}, u32[]{:S(2)}, u32[]{:S(2)}) collective-permute-start(f32[4,96,128]{2,1,0:T(8,128)S(1)} %get-tuple-element.10), channel_id=1, source_target_pairs={{0,2},{1,3},{2,0},{3,1},{4,6},{5,7},{6,4},{7,5},{8,10},{9,11},{10,... | collective-permute-start | bytes 589832 | tf_op jit(solution)/shard_map/ppermute | solution.py:47
  3.6 1.1 %collective-permute-done = f32[4,96,128]{2,1,0:T(8,128)S(1)} collective-permute-done((f32[4,96,128]{2,1,0:T(8,128)S(1)}, f32[4,96,128]{2,1,0:T(8,128)S(1)}, u32[]{:S(2)}, u32[]{:S(2)}) %collective-permute-start) | collective-permute-done | bytes 196640 | tf_op jit(solution)/shard_map/ppermute | solution.py:47
  4.8 3.7 %collective-permute-start.1 = (f32[96,128]{1,0:T(8,128)S(1)}, f32[96,128]{1,0:T(8,128)S(1)}, u32[]{:S(2)}, u32[]{:S(2)}) collective-permute-start(f32[96,128]{1,0:T(8,128)S(1)} %get-tuple-element.13), channel_id=1, source_target_pairs={{0,14},{1,15},{2,12},{3,13},{4,10},{5,11},{6,8},{7,9},{8,6},{9,7},... | collective-permute-start | bytes 147464 | tf_op jit(solution)/shard_map/ppermute | solution.py:47
  8.4 0.5 %collective-permute-start.3 = (f32[96,128]{1,0:T(8,128)S(1)}, f32[96,128]{1,0:T(8,128)S(1)}, u32[]{:S(2)}, u32[]{:S(2)}) collective-permute-start(f32[96,128]{1,0:T(8,128)S(1)} %get-tuple-element.14), channel_id=1, source_target_pairs={{0,8},{1,9},{2,10},{3,11},{4,12},{5,13},{6,14},{7,15},{8,0},{9,1},... | collective-permute-start | bytes 147464 | tf_op jit(solution)/shard_map/ppermute | solution.py:47
  8.9 0.1 collective-permute-start.2
  9.0 1.6 %collective-permute-done.1 = f32[96,128]{1,0:T(8,128)S(1)} collective-permute-done((f32[96,128]{1,0:T(8,128)S(1)}, f32[96,128]{1,0:T(8,128)S(1)}, u32[]{:S(2)}, u32[]{:S(2)}) %collective-permute-start.1) | collective-permute-done | bytes 49184 | tf_op jit(solution)/shard_map/ppermute | solution.py:47
  10.6 2.0 %collective-permute-done.3 = f32[96,128]{1,0:T(8,128)S(1)} collective-permute-done((f32[96,128]{1,0:T(8,128)S(1)}, f32[96,128]{1,0:T(8,128)S(1)}, u32[]{:S(2)}, u32[]{:S(2)}) %collective-permute-start.3) | collective-permute-done | bytes 49184 | tf_op jit(solution)/shard_map/ppermute | solution.py:47
  12.5 0.1 collective-permute-done.2
  12.7 2.4 %collective-permute-start.4 = (f32[96,128]{1,0:T(8,128)S(1)}, f32[96,128]{1,0:T(8,128)S(1)}, u32[]{:S(2)}, u32[]{:S(2)}) collective-permute-start(f32[96,128]{1,0:T(8,128)S(1)} %fusion.2.held), channel_id=1, source_target_pairs={{0,18},{1,19},{2,16},{3,17},{4,22},{5,23},{6,20},{7,21},{8,26},{9,... | collective-permute-start | bytes 147464 | tf_op jit(solution)/shard_map/ppermute | solution.py:47
  15.1 0.0 copy-start
  15.1 0.8 %copy-done = f32[64,64]{1,0:T(8,128)S(1)} copy-done((f32[64,64]{1,0:T(8,128)S(1)}, f32[64,64]{1,0:T(8,128)}, u32[]{:S(2)}) %copy-start) | copy-done | bytes 16408
  15.8 0.0 copy-start.1
  15.8 0.7 %copy-done.1 = f32[32,32]{1,0:T(8,128)S(1)} copy-done((f32[32,32]{1,0:T(8,128)S(1)}, f32[32,32]{1,0:T(8,128)}, u32[]{:S(2)}) %copy-start.1) | copy-done | bytes 4120
  16.6 0.0 slice-start
  16.6 0.4 %shard_map.74 = (bf16[256,2048]{1,0:T(8,128)(2,1)S(1)}, bf16[128,128]{1,0:T(8,128)(2,1)S(1)}) custom-call(f32[32,32]{1,0:T(8,128)S(1)} %copy-done.1, f32[64,64]{1,0:T(8,128)S(1)} %copy-done), custom_call_target="tpu_custom_call" | custom-call | flops 8589934592 | bytes 16777216 | tf_op jit(solution)/shard_map/pallas_call | solution.py:129
  16.9 0.5 %collective-permute-done.4.got = f32[96,128]{1,0:T(8,128)S(1)} collective-permute-done((f32[96,128]{1,0:T(8,128)S(1)}, f32[96,128]{1,0:T(8,128)S(1)}, u32[]{:S(2)}, u32[]{:S(2)}) %collective-permute-start.4) | collective-permute-done | bytes 49184 | tf_op jit(solution)/shard_map/ppermute | solution.py:47
  17.4 0.0 slice-start.1
  17.4 0.5 %shard_map.75 = bf16[4,2048]{1,0:T(4,128)(2,1)S(1)} custom-call(f32[96,128]{1,0:T(8,128)S(1)} %fusion.2.held, f32[96,128]{1,0:T(8,128)S(1)} %collective-permute-done.4.got, bf16[256,2048]{1,0:T(8,128)(2,1)S(1)} %get-tuple-element.11.spread_out, bf16[128,128]{1,0:T(8,128)(2,1)S(1)} %get-tuple-element.12.spread_in), custom_call_target="tpu_custom_call" | custom-call | flops 8589934592 | bytes 16777216 | tf_op jit(solution)/shard_map/pallas_call | solution.py:163
  17.9 2.1 %collective-permute-start.5 = (bf16[4,2048]{1,0:T(4,128)(2,1)S(1)}, bf16[4,2048]{1,0:T(4,128)(2,1)S(1)}, u32[]{:S(2)}, u32[]{:S(2)}) collective-permute-start(bf16[4,2048]{1,0:T(4,128)(2,1)S(1)} %shard_map.75), channel_id=1, source_target_pairs={{0,8},{1,9},{2,10},{3,11},{4,12},{5,13},{6,14},{7,15},{8,0},{9,1},... | collective-permute-start | bytes 49160 | tf_op jit(solution)/shard_map/ppermute | solution.py:47
  20.0 1.7 %collective-permute-done.5 = bf16[4,2048]{1,0:T(4,128)(2,1)S(1)} collective-permute-done((bf16[4,2048]{1,0:T(4,128)(2,1)S(1)}, bf16[4,2048]{1,0:T(4,128)(2,1)S(1)}, u32[]{:S(2)}, u32[]{:S(2)}) %collective-permute-start.5) | collective-permute-done | bytes 16416 | tf_op jit(solution)/shard_map/ppermute | solution.py:47
  21.7 0.7 %collective-permute-start.8 = (bf16[8,2048]{1,0:T(8,128)(2,1)S(1)}, bf16[8,2048]{1,0:T(8,128)(2,1)S(1)}, u32[]{:S(2)}, u32[]{:S(2)}) collective-permute-start(bf16[8,2048]{1,0:T(8,128)(2,1)S(1)} %pad_maximum_fusion.1), channel_id=1, source_target_pairs={{0,7},{1,6},{2,5},{3,4},{4,3},{5,2},{6,1},{7,0},{8,15},{9,14},{10,... | collective-permute-start | bytes 98312 | tf_op jit(solution)/shard_map/ppermute | solution.py:47
  22.5 2.0 %collective-permute-start.7 = (bf16[8,2048]{1,0:T(8,128)(2,1)S(1)}, bf16[8,2048]{1,0:T(8,128)(2,1)S(1)}, u32[]{:S(2)}, u32[]{:S(2)}) collective-permute-start(bf16[8,2048]{1,0:T(8,128)(2,1)S(1)} %pad_maximum_fusion.1), channel_id=1, source_target_pairs={{0,6},{1,7},{2,4},{3,5},{4,2},{5,3},{6,0},{7,1},{8,14},{9,15},{10,... | collective-permute-start | bytes 98312 | tf_op jit(solution)/shard_map/ppermute | solution.py:47
  24.5 0.5 %collective-permute-start.6 = (bf16[8,2048]{1,0:T(8,128)(2,1)S(1)}, bf16[8,2048]{1,0:T(8,128)(2,1)S(1)}, u32[]{:S(2)}, u32[]{:S(2)}) collective-permute-start(bf16[8,2048]{1,0:T(8,128)(2,1)S(1)} %pad_maximum_fusion.1), channel_id=1, source_target_pairs={{0,1},{1,0},{2,3},{3,2},{4,5},{5,4},{6,7},{7,6},{8,9},{9,8},{10,11... | collective-permute-start | bytes 98312 | tf_op jit(solution)/shard_map/ppermute | solution.py:47
  25.0 1.0 %collective-permute-done.8 = bf16[8,2048]{1,0:T(8,128)(2,1)S(1)} collective-permute-done((bf16[8,2048]{1,0:T(8,128)(2,1)S(1)}, bf16[8,2048]{1,0:T(8,128)(2,1)S(1)}, u32[]{:S(2)}, u32[]{:S(2)}) %collective-permute-start.8) | collective-permute-done | bytes 32800 | tf_op jit(solution)/shard_map/ppermute | solution.py:47
  26.0 0.4 %collective-permute-done.7 = bf16[8,2048]{1,0:T(8,128)(2,1)S(1)} collective-permute-done((bf16[8,2048]{1,0:T(8,128)(2,1)S(1)}, bf16[8,2048]{1,0:T(8,128)(2,1)S(1)}, u32[]{:S(2)}, u32[]{:S(2)}) %collective-permute-start.7) | collective-permute-done | bytes 32800 | tf_op jit(solution)/shard_map/ppermute | solution.py:47
  26.5 2.0 %collective-permute-done.6 = bf16[8,2048]{1,0:T(8,128)(2,1)S(1)} collective-permute-done((bf16[8,2048]{1,0:T(8,128)(2,1)S(1)}, bf16[8,2048]{1,0:T(8,128)(2,1)S(1)}, u32[]{:S(2)}, u32[]{:S(2)}) %collective-permute-start.6) | collective-permute-done | bytes 32800 | tf_op jit(solution)/shard_map/ppermute | solution.py:47
  28.4 0.1 collective-permute-start.9
  28.5 1.3 %collective-permute-done.9.got = bf16[32,2048]{1,0:T(8,128)(2,1)S(1)} collective-permute-done((bf16[32,2048]{1,0:T(8,128)(2,1)S(1)}, bf16[32,2048]{1,0:T(8,128)(2,1)S(1)}, u32[]{:S(2)}, u32[]{:S(2)}) %collective-permute-start.9) | collective-permute-done | bytes 131104 | tf_op jit(solution)/shard_map/ppermute | solution.py:47
  29.9 0.0 slice-done
  29.9 0.0 slice-done.1
  29.9 2.8 %shard_map.76 = f32[64,1536]{1,0:T(8,128)} custom-call(bf16[32,2048]{1,0:T(8,128)(2,1)S(1)} %pad_add_fusion.held, bf16[32,2048]{1,0:T(8,128)(2,1)S(1)} %collective-permute-done.9.got, bf16[1536,2048]{1,0:T(8,128)(2,1)S(1)} %bitcast.17), custom_call_target="tpu_custom_call" | custom-call | tf_op jit(solution)/shard_map/pallas_call | solution.py:193
  (6 shorter events, 0.1 us)
Async XLA Ops:
  3.1 1.6 %collective-permute-start = (f32[4,96,128]{2,1,0:T(8,128)S(1)}, f32[4,96,128]{2,1,0:T(8,128)S(1)}, u32[]{:S(2)}, u32[]{:S(2)}) collective-permute-start(f32[4,96,128]{2,1,0:T(8,128)S(1)} %get-tuple-element.10), channel_id=1, source_target_pairs={{0,2},{1,3},{2,0},{3,1},{4,6},{5,7},{6,4},{7,5},{8,10},{9,11},{10,... | collective-permute-start | bytes 589832 | tf_op jit(solution)/shard_map/ppermute | solution.py:47
  4.8 5.8 %collective-permute-start.1 = (f32[96,128]{1,0:T(8,128)S(1)}, f32[96,128]{1,0:T(8,128)S(1)}, u32[]{:S(2)}, u32[]{:S(2)}) collective-permute-start(f32[96,128]{1,0:T(8,128)S(1)} %get-tuple-element.13), channel_id=1, source_target_pairs={{0,14},{1,15},{2,12},{3,13},{4,10},{5,11},{6,8},{7,9},{8,6},{9,7},... | collective-permute-start | bytes 147464 | tf_op jit(solution)/shard_map/ppermute | solution.py:47
  8.4 4.1 %collective-permute-start.3 = (f32[96,128]{1,0:T(8,128)S(1)}, f32[96,128]{1,0:T(8,128)S(1)}, u32[]{:S(2)}, u32[]{:S(2)}) collective-permute-start(f32[96,128]{1,0:T(8,128)S(1)} %get-tuple-element.14), channel_id=1, source_target_pairs={{0,8},{1,9},{2,10},{3,11},{4,12},{5,13},{6,14},{7,15},{8,0},{9,1},... | collective-permute-start | bytes 147464 | tf_op jit(solution)/shard_map/ppermute | solution.py:47
  8.9 3.8 %collective-permute-start.2 = (f32[96,128]{1,0:T(8,128)S(1)}, f32[96,128]{1,0:T(8,128)S(1)}, u32[]{:S(2)}, u32[]{:S(2)}) collective-permute-start(f32[96,128]{1,0:T(8,128)S(1)} %get-tuple-element.15), channel_id=1, source_target_pairs={{0,6},{1,7},{2,4},{3,5},{4,2},{5,3},{6,0},{7,1},{8,14},{9,15},{10,... | collective-permute-start | bytes 147464 | tf_op jit(solution)/shard_map/ppermute | solution.py:47
  12.7 4.7 %collective-permute-start.4 = (f32[96,128]{1,0:T(8,128)S(1)}, f32[96,128]{1,0:T(8,128)S(1)}, u32[]{:S(2)}, u32[]{:S(2)}) collective-permute-start(f32[96,128]{1,0:T(8,128)S(1)} %fusion.2.held), channel_id=1, source_target_pairs={{0,18},{1,19},{2,16},{3,17},{4,22},{5,23},{6,20},{7,21},{8,26},{9,... | collective-permute-start | bytes 147464 | tf_op jit(solution)/shard_map/ppermute | solution.py:47
  15.1 0.8 %copy-start = (f32[64,64]{1,0:T(8,128)S(1)}, f32[64,64]{1,0:T(8,128)}, u32[]{:S(2)}) copy-start(f32[64,64]{1,0:T(8,128)} %out_inverse.1) | copy-start | bytes 49156
  15.8 0.7 %copy-start.1 = (f32[32,32]{1,0:T(8,128)S(1)}, f32[32,32]{1,0:T(8,128)}, u32[]{:S(2)}) copy-start(f32[32,32]{1,0:T(8,128)} %in_inverse.1) | copy-start | bytes 12292
  16.6 13.3 %slice-start = ((s8[6291456]{0:T(1024)(128)(4,1)}), s8[4194304]{0:T(1024)(128)(4,1)S(1)}, s32[]{:S(2)}) async-start(s8[6291456]{0:T(1024)(128)(4,1)} %bitcast.16), calls=%async_computation | async-start | bytes 8388608
  17.4 12.4 %slice-start.1 = ((s8[6291456]{0:T(1024)(128)(4,1)}), s8[2097152]{0:T(1024)(128)(4,1)S(1)}, s32[]{:S(2)}) async-start(s8[6291456]{0:T(1024)(128)(4,1)} %bitcast.16), calls=%async_computation.1 | async-start | bytes 4194304
  17.9 3.8 %collective-permute-start.5 = (bf16[4,2048]{1,0:T(4,128)(2,1)S(1)}, bf16[4,2048]{1,0:T(4,128)(2,1)S(1)}, u32[]{:S(2)}, u32[]{:S(2)}) collective-permute-start(bf16[4,2048]{1,0:T(4,128)(2,1)S(1)} %shard_map.75), channel_id=1, source_target_pairs={{0,8},{1,9},{2,10},{3,11},{4,12},{5,13},{6,14},{7,15},{8,0},{9,1},... | collective-permute-start | bytes 49160 | tf_op jit(solution)/shard_map/ppermute | solution.py:47
  21.7 4.3 %collective-permute-start.8 = (bf16[8,2048]{1,0:T(8,128)(2,1)S(1)}, bf16[8,2048]{1,0:T(8,128)(2,1)S(1)}, u32[]{:S(2)}, u32[]{:S(2)}) collective-permute-start(bf16[8,2048]{1,0:T(8,128)(2,1)S(1)} %pad_maximum_fusion.1), channel_id=1, source_target_pairs={{0,7},{1,6},{2,5},{3,4},{4,3},{5,2},{6,1},{7,0},{8,15},{9,14},{10,... | collective-permute-start | bytes 98312 | tf_op jit(solution)/shard_map/ppermute | solution.py:47
  22.5 4.0 %collective-permute-start.7 = (bf16[8,2048]{1,0:T(8,128)(2,1)S(1)}, bf16[8,2048]{1,0:T(8,128)(2,1)S(1)}, u32[]{:S(2)}, u32[]{:S(2)}) collective-permute-start(bf16[8,2048]{1,0:T(8,128)(2,1)S(1)} %pad_maximum_fusion.1), channel_id=1, source_target_pairs={{0,6},{1,7},{2,4},{3,5},{4,2},{5,3},{6,0},{7,1},{8,14},{9,15},{10,... | collective-permute-start | bytes 98312 | tf_op jit(solution)/shard_map/ppermute | solution.py:47
  24.5 3.9 %collective-permute-start.6 = (bf16[8,2048]{1,0:T(8,128)(2,1)S(1)}, bf16[8,2048]{1,0:T(8,128)(2,1)S(1)}, u32[]{:S(2)}, u32[]{:S(2)}) collective-permute-start(bf16[8,2048]{1,0:T(8,128)(2,1)S(1)} %pad_maximum_fusion.1), channel_id=1, source_target_pairs={{0,1},{1,0},{2,3},{3,2},{4,5},{5,4},{6,7},{7,6},{8,9},{9,8},{10,11... | collective-permute-start | bytes 98312 | tf_op jit(solution)/shard_map/ppermute | solution.py:47
  28.4 1.4 %collective-permute-start.9 = (bf16[32,2048]{1,0:T(8,128)(2,1)S(1)}, bf16[32,2048]{1,0:T(8,128)(2,1)S(1)}, u32[]{:S(2)}, u32[]{:S(2)}) collective-permute-start(bf16[32,2048]{1,0:T(8,128)(2,1)S(1)} %pad_add_fusion.held), channel_id=1, source_target_pairs={{0,2},{1,3},{2,0},{3,1},{4,6},{5,7},{6,4},{7,5},{8,10},{9,11},{10,... | collective-permute-start | bytes 393224 | tf_op jit(solution)/shard_map/ppermute | solution.py:47

commit v3 on v2

--- a/solution.py
+++ b/solution.py
@@ -12,6 +12,8 @@
 VMEM = pl.BlockSpec(memory_space=pltpu.VMEM)
 HBM = pl.BlockSpec(memory_space=pltpu.HBM)
 MIB = 1 << 20
+PROJECT_VMEM = 55_889_920
+HIGH = 12
 
 
 def contract(lhs, rhs, left, right):
@@ -52,50 +54,40 @@
     return lax.rem(slot, 2) ^ odd_bits(slot // 2) ^ odd_bits(group // 2)
 
 
-def project_kernel(
-    lows, width_in, acts, grads, proj, given, kept, act_buf, grad_buf, sems
-):
-    slices, spans = given.shape[0], given.shape[0] // lows
-    tokens = given.shape[2]
-    half = own_half()
-    x, low = lax.axis_index("wide") // 2, lax.rem(lax.axis_index("grp"), lows)
+def project_kernel(width_in, acts, grads, proj, given, kept, act_buf, grad_buf, sems):
+    slices, tokens = given.shape[0], given.shape[2]
+    half, x = own_half(), lax.axis_index("wide") // 2
     copies = []
-    for k in range(2 * spans):
-        first = ((x ^ (k % spans)) * 2 + (half ^ (k < spans))) * lows * tokens
-        rows = pl.ds(pl.multiple_of(first, lows * tokens), lows * tokens)
+    for k in range(2 * slices):
+        first = ((x ^ (k % slices)) * 2 + (half ^ (k < slices))) * tokens
+        rows = pl.ds(pl.multiple_of(first, tokens), tokens)
         for source, target, part in ((acts, act_buf, 0), (grads, grad_buf, 1)):
             copy = pltpu.make_async_copy(source.at[rows], target.at[k], sems.at[k, part])
             copy.start()
             copies.append(copy)
-    for k in range(2 * spans):
+    for k in range(2 * slices):
         copies[2 * k].wait()
         copies[2 * k + 1].wait()
-        low_in = contract(proj[:width_in], act_buf[k], 1, 1)
-        low_out = contract(proj[width_in:], grad_buf[k], 1, 1)
-        out = given if k < spans else kept
-        for place in range(lows):
-            slot = (k % spans) * lows + (low ^ place)
-            lanes = slice(place * tokens, (place + 1) * tokens)
-            out[slot, :width_in] = low_in[:, lanes]
-            out[slot, width_in:] = low_out[:, lanes]
-
-
-def project(slices, lows, acts, grads, proj, width_in):
+        out = given if k < slices else kept
+        out[k % slices, :width_in] = contract(proj[:width_in], act_buf[k], 1, 1)
+        out[k % slices, width_in:] = contract(proj[width_in:], grad_buf[k], 1, 1)
+
+
+def project(slices, acts, grads, proj, width_in):
     tokens, features = acts.shape[0] // (2 * slices), acts.shape[1]
     width = proj.shape[0]
-    spans = slices // lows
     out = jax.ShapeDtypeStruct((slices, width, tokens), jnp.float32)
     return pl.pallas_call(
-        functools.partial(project_kernel, lows, width_in),
+        functools.partial(project_kernel, width_in),
         out_shape=(out, out),
         in_specs=[HBM] * 2 + [VMEM],
         out_specs=(VMEM, VMEM),
         scratch_shapes=[
-            pltpu.VMEM((2 * spans, tokens * lows, features), jnp.bfloat16),
-            pltpu.VMEM((2 * spans, tokens * lows, features), jnp.bfloat16),
-            pltpu.SemaphoreType.DMA((2 * spans + 1, 2)),
+            pltpu.VMEM((2 * slices, tokens, features), jnp.bfloat16),
+            pltpu.VMEM((2 * slices, tokens, features), jnp.bfloat16),
+            pltpu.SemaphoreType.DMA((2 * slices, 2)),
         ],
-        compiler_params=pltpu.CompilerParams(vmem_limit_bytes=55885824),
+        compiler_params=pltpu.CompilerParams(vmem_limit_bytes=PROJECT_VMEM),
         cost_estimate=pl.CostEstimate(
             flops=4 * slices * tokens * features * width,
             bytes_accessed=8 * slices * tokens * features,
@@ -139,12 +131,12 @@
     )(in_inverse, out_inverse)
 
 
-def query_kernel(held, got, spread_out, spread_in, out):
+def query_kernel(summed, spread_out, spread_in, out):
     width_in = spread_in.shape[0] // 4
-    tokens = held.shape[1]
+    tokens = summed.shape[1]
     queries, columns = out.shape
     lanes = spread_in.shape[1]
-    low = (held[...] + got[...]).T
+    low = summed[...].T
     in_high, in_low = two_parts(low[:, :width_in])
     out_high, out_low = two_parts(low[:, width_in:])
     side_in = jnp.concatenate([in_high, in_high, in_low, in_low], axis=1)
@@ -158,19 +150,19 @@
         out[:, start : start + step] = part.astype(out.dtype)
 
 
-def build_queries(held, got, spread_out, spread_in):
-    tokens = held.shape[1]
+def build_queries(summed, spread_out, spread_in):
+    tokens = summed.shape[1]
     return pl.pallas_call(
         query_kernel,
         out_shape=jax.ShapeDtypeStruct((tokens // SEQ, spread_out.shape[1]), jnp.bfloat16),
-        in_specs=[VMEM] * 4,
+        in_specs=[VMEM] * 3,
         out_specs=VMEM,
         compiler_params=pltpu.CompilerParams(vmem_limit_bytes=12 * MIB),
         cost_estimate=pl.CostEstimate(flops=1 << 33, bytes_accessed=16 * MIB, transcendentals=0),
-    )(held, got, spread_out, spread_in)
-
-
-def score_kernel(order, wide, lows, held, got, store, out):
+    )(summed, spread_out, spread_in)
+
+
+def score_kernel(order, wide, held, got, store, out):
     blk, x, half = lax.axis_index("blk"), lax.axis_index("wide") // 2, own_half()
     queries = jnp.concatenate([held[...], got[...]], axis=0)
     rows = out.shape[0] // len(order)
@@ -179,19 +171,15 @@
         for far_blk, far_x, flip in order
     ]
     step = 512
-    swapped = lax.rem(lax.axis_index("grp"), lows) == 1
     for start in range(0, out.shape[1], step):
         part = contract(queries, store[start : start + step], 1, 1)
-        part = part.reshape(len(order), rows, step)
-        if lows > 1:
-            part = jnp.where(swapped, jnp.roll(part, rows // 2, axis=1), part)
         for r, row in enumerate(targets):
-            out[pl.ds(row, rows), start : start + step] = part[r]
-
-
-def scores(order, wide, lows, held, got, store):
-    return pl.pallas_call(
-        functools.partial(score_kernel, order, wide, lows),
+            out[pl.ds(row, rows), start : start + step] = part[r * rows : (r + 1) * rows]
+
+
+def scores(order, wide, held, got, store):
+    return pl.pallas_call(
+        functools.partial(score_kernel, order, wide),
         out_shape=jax.ShapeDtypeStruct((2 * held.shape[0], store.shape[0]), jnp.float32),
         in_specs=[VMEM] * 3,
         out_specs=VMEM,
@@ -208,43 +196,58 @@
     )
 
 
+def encode(value, width_in):
+    exponents = [
+        jnp.clip(jnp.ceil(jnp.log2(jnp.max(jnp.abs(part), axis=0, keepdims=True))), -100, 100)
+        for part in (value[:width_in], value[width_in:])
+    ]
+    rows = value.shape[0]
+    row = lax.broadcasted_iota(jnp.int32, (rows + 2, 1), 0)
+    exponent = jnp.where(row < width_in, *exponents)
+    scaled = lax.pad(value, jnp.float32(0), ((0, 2, 0), (0, 0, 0))) * jnp.exp2(HIGH - exponent)
+    scaled = jnp.where(row == rows, exponents[0], jnp.where(row > rows, exponents[1], scaled))
+    return scaled.astype(jnp.float16)
+
+
+def decode(value, width_in):
+    rows = value.shape[0] - 2
+    value = value.astype(jnp.float32)
+    row = lax.broadcasted_iota(jnp.int32, (rows, 1), 0)
+    exponent = jnp.where(row < width_in, value[rows : rows + 1], value[rows + 1 :])
+    return value[:rows] * jnp.exp2(exponent - HIGH)
+
+
 def on_device(
     sizes, activations, out_grads, in_projection, out_projection, in_inverse, out_inverse, grad_store
 ):
     wide, groups, blocks = sizes["wide"], sizes["grp"], sizes["blk"]
-    spans, lows = wide // 2, min(groups, 2)
-    slices = spans * lows
-    given, kept = project(
-        slices, lows, activations, out_grads, jnp.concatenate([in_projection.T, out_projection.T], axis=0), in_inverse.shape[0]
-    )
+    slices, lows, width_in = wide // 2, min(groups, 2), in_inverse.shape[0]
+    proj = jnp.concatenate([in_projection.T, out_projection.T], axis=0)
+    given, kept = project(slices, activations, out_grads, proj, width_in)
     both = kept + swap(given, sizes, {"wide": 1})
     held = both[0]
-    for k in range(slices - 1, 0, -1):
-        held = held + exchange(both[k], sizes, wide=k // lows, grp=k % lows)
-    last = jnp.zeros_like(held)
+    coded = [encode(part, width_in) for part in both]
+    for k in range(slices * lows - 1, 0, -1):
+        got = exchange(coded[k // lows], sizes, wide=k // lows, grp=k % lows)
+        held = held + decode(got, width_in)
     bit = lows
     while bit < groups:
-        if bit > lows:
-            held = held + last
-        last = exchange(held, sizes, grp=bit)
+        held = held + decode(exchange(encode(held, width_in), sizes, grp=bit), width_in)
         bit *= 2
     spread_out, spread_in = spread_inverses(in_inverse, out_inverse)
-    queries = build_queries(held, last, spread_out, spread_in)
-    if lows > 1:
-        other = exchange(queries, sizes, grp=1)
-        queries = jnp.concatenate([queries, other], axis=0)
+    queries = build_queries(held, spread_out, spread_in)
     order = [(0, 0)]
     bit = 2
     while bit < blocks:
-        queries = jnp.concatenate([queries, exchange(queries, sizes, blk=bit)], axis=0)
+        queries = stack([queries, exchange(queries, sizes, blk=bit)])
         order += [(b ^ bit, x) for b, x in order]
         bit *= 2
-    near = [(b, x) for x in range(spans) for b in range(min(blocks, 2))]
+    near = [(b, x) for x in range(slices) for b in range(min(blocks, 2))]
     others = [exchange(queries, sizes, blk=b, wide=x) for b, x in near[:0:-1]]
     queries = stack([queries] + others[::-1])
     order = [(b ^ c, x ^ y) for c, y in near for b, x in order]
     order = tuple((b, x, flip) for flip in range(2) for b, x in order)
-    return scores(order, wide, lows, queries, swap(queries, sizes, {"wide": 1}), grad_store)
+    return scores(order, wide, queries, swap(queries, sizes, {"wide": 1}), grad_store)
 
 
 def solution(mesh):

time: 33 us -> 32 us (0.970)
  starting transfers between devices: 12.5 us -> 11.1 us
  other arithmetic: 0.93 us -> 1.56 us
    ppermute x10 -> x9, starting transfers between devices: 12.5 us -> 11.1 us  [swap(): return lax.ppermute(value, axes, pairs)]
    ppermute x10 -> x9, waiting for transfers between devices: 11.7 us -> 11.4 us  [swap(): return lax.ppermute(value, axes, pairs)]
    concatenate x2 -> x1, other arithmetic: 0.87 us -> 0.85 us  [on_device(): proj = jnp.concatenate([in_projection.T, out_projection.T], axis=0)]
  transfers between devices with their start and end apart: 10 -> 9, of which waited for: 10 -> 9; matrix products, arithmetic and copies ran while one was open for 0% -> 0% of each run, Pallas kernels for 1% -> 1%
where the time goes in v3:
time: 32 us; the launch traced here: 31.7 us
  waiting for transfers between devices  11.4 us (36%)
  starting transfers between devices  11.1 us (35%)
  Pallas kernels  5.98 us (19%)
  other arithmetic  1.56 us (5%)
  local copies, waits for them, and re-layouts  1.52 us (5%)
    ppermute x9, waiting for transfers between devices, swap(): return lax.ppermute(value, axes, pairs)  11.4 us
    ppermute x9, starting transfers between devices, swap(): return lax.ppermute(value, axes, pairs)  11.1 us
    pallas_call x1, Pallas kernels, scores(): pl.pallas_call(functools.partial(score_kernel, order, wide), out_shape=ja...  2.77 us
    pallas_call x1, Pallas kernels, project(): pl.pallas_call(functools.partial(project_kernel, width_in), out_shape=(ou...  2.24 us
    unnamed x8, local copies, waits for them, and re-layouts  1.49 us
    concatenate x1, other arithmetic, on_device(): proj = jnp.concatenate([in_projection.T, out_projection.T], axis=0)  0.85 us
  transfers between devices with their start and end apart: 9, of which 9 were waited for; matrix products, arithmetic and copies ran while one was open for 0% of the time, Pallas kernels for 1%

profile of v3, /device:TPU:0, one launch (start us, length us, event | category | flops | bytes accessed | tf_op | source)
XLA Modules:
  0.0 31.7 jit_solution(11815104232081021186)
XLA Ops:
  0.0 0.8 %pad_maximum_fusion.proj = bf16[96,512]{1,0:T(8,128)(2,1)S(1)} fusion(bf16[64,512]{1,0:T(8,128)(2,1)} %bitcast.18, bf16[32,512]{1,0:T(8,128)(2,1)} %bitcast.19), kind=kLoop, calls=%fused_computation.14 | loop fusion | flops 196608 | bytes 196608 | tf_op jit(solution)/shard_map/concatenate | solution.py:225
  0.8 2.2 %shard_map.73 = (f32[2,96,256]{2,1,0:T(8,128)S(1)}, f32[2,96,256]{2,1,0:T(8,128)S(1)}) custom-call(bf16[1024,512]{1,0:T(8,128)(2,1)} %acts.1, bf16[1024,512]{1,0:T(8,128)(2,1)} %grads.1, bf16[96,512]{1,0:T(8,128)(2,1)S(1)} %pad_maximum_fusion.proj), custom_call_target="tpu_custom_call" | custom-call | flops 100663296 | bytes 2097152 | tf_op jit(solution)/shard_map/pallas_call | solution.py:80
  3.1 0.5 %collective-permute-start = (f32[2,96,256]{2,1,0:T(8,128)S(1)}, f32[2,96,256]{2,1,0:T(8,128)S(1)}, u32[]{:S(2)}, u32[]{:S(2)}) collective-permute-start(f32[2,96,256]{2,1,0:T(8,128)S(1)} %get-tuple-element.10), channel_id=1, source_target_pairs={{0,2},{1,3},{2,0},{3,1},{4,6},{5,7},{6,4},{7,5},{8,10},{9,11},{10,... | collective-permute-start | bytes 589832 | tf_op jit(solution)/shard_map/ppermute | solution.py:49
  3.6 1.1 %collective-permute-done = f32[2,96,256]{2,1,0:T(8,128)S(1)} collective-permute-done((f32[2,96,256]{2,1,0:T(8,128)S(1)}, f32[2,96,256]{2,1,0:T(8,128)S(1)}, u32[]{:S(2)}, u32[]{:S(2)}) %collective-permute-start) | collective-permute-done | bytes 196640 | tf_op jit(solution)/shard_map/ppermute | solution.py:49
  4.8 0.1 select_convert_fusion.2
  5.0 3.0 %collective-permute-start.3 = (f16[98,256]{1,0:T(8,128)(2,1)S(1)}, f16[98,256]{1,0:T(8,128)(2,1)S(1)}, u32[]{:S(2)}, u32[]{:S(2)}) collective-permute-start(f16[98,256]{1,0:T(8,128)(2,1)S(1)} %get-tuple-element.28), channel_id=1, source_target_pairs={{0,8},{1,9},{2,10},{3,11},{4,12},{5,13},{6,14},{7,15},{8,0},{9,1},... | collective-permute-start | bytes 150536 | tf_op jit(solution)/shard_map/ppermute | solution.py:49
  8.0 1.0 %collective-permute-start.2 = (f16[98,256]{1,0:T(8,128)(2,1)S(1)}, f16[98,256]{1,0:T(8,128)(2,1)S(1)}, u32[]{:S(2)}, u32[]{:S(2)}) collective-permute-start(f16[98,256]{1,0:T(8,128)(2,1)S(1)} %get-tuple-element.27), channel_id=1, source_target_pairs={{0,6},{1,7},{2,4},{3,5},{4,2},{5,3},{6,0},{7,1},{8,14},{9,15},{10,... | collective-permute-start | bytes 150536 | tf_op jit(solution)/shard_map/ppermute | solution.py:49
  8.9 0.3 collective-permute-start.1
  9.3 0.9 %collective-permute-done.3 = f16[98,256]{1,0:T(8,128)(2,1)S(1)} collective-permute-done((f16[98,256]{1,0:T(8,128)(2,1)S(1)}, f16[98,256]{1,0:T(8,128)(2,1)S(1)}, u32[]{:S(2)}, u32[]{:S(2)}) %collective-permute-start.3) | collective-permute-done | bytes 50208 | tf_op jit(solution)/shard_map/ppermute | solution.py:49
  10.1 1.9 %collective-permute-done.2 = f16[98,256]{1,0:T(8,128)(2,1)S(1)} collective-permute-done((f16[98,256]{1,0:T(8,128)(2,1)S(1)}, f16[98,256]{1,0:T(8,128)(2,1)S(1)}, u32[]{:S(2)}, u32[]{:S(2)}) %collective-permute-start.2) | collective-permute-done | bytes 50208 | tf_op jit(solution)/shard_map/ppermute | solution.py:49
  12.1 1.3 %collective-permute-done.1 = f16[98,256]{1,0:T(8,128)(2,1)S(1)} collective-permute-done((f16[98,256]{1,0:T(8,128)(2,1)S(1)}, f16[98,256]{1,0:T(8,128)(2,1)S(1)}, u32[]{:S(2)}, u32[]{:S(2)}) %collective-permute-start.1) | collective-permute-done | bytes 50208 | tf_op jit(solution)/shard_map/ppermute | solution.py:49
  13.4 0.1 fusion.1
  13.6 0.1 select_convert_fusion
  13.8 2.9 %collective-permute-start.4 = (f16[98,256]{1,0:T(8,128)(2,1)S(1)}, f16[98,256]{1,0:T(8,128)(2,1)S(1)}, u32[]{:S(2)}, u32[]{:S(2)}) collective-permute-start(f16[98,256]{1,0:T(8,128)(2,1)S(1)} %select_convert_fusion), channel_id=1, source_target_pairs={{0,18},{1,19},{2,16},{3,17},{4,22},{5,23},{6,20},{7,21},{8,26},{9,... | collective-permute-start | bytes 150536 | tf_op jit(solution)/shard_map/ppermute | solution.py:49
  16.7 0.0 copy-start
  16.7 0.8 %copy-done = f32[64,64]{1,0:T(8,128)S(1)} copy-done((f32[64,64]{1,0:T(8,128)S(1)}, f32[64,64]{1,0:T(8,128)}, u32[]{:S(2)}) %copy-start) | copy-done | bytes 16408
  17.4 0.0 copy-start.1
  17.4 0.7 %copy-done.1 = f32[32,32]{1,0:T(8,128)S(1)} copy-done((f32[32,32]{1,0:T(8,128)S(1)}, f32[32,32]{1,0:T(8,128)}, u32[]{:S(2)}) %copy-start.1) | copy-done | bytes 4120
  18.2 0.0 slice-start
  18.2 0.4 %shard_map.74 = (bf16[256,2048]{1,0:T(8,128)(2,1)S(1)}, bf16[128,128]{1,0:T(8,128)(2,1)S(1)}) custom-call(f32[32,32]{1,0:T(8,128)S(1)} %copy-done.1, f32[64,64]{1,0:T(8,128)S(1)} %copy-done), custom_call_target="tpu_custom_call" | custom-call | flops 8589934592 | bytes 16777216 | tf_op jit(solution)/shard_map/pallas_call | solution.py:121
  18.5 1.5 %collective-permute-done.4 = f16[98,256]{1,0:T(8,128)(2,1)S(1)} collective-permute-done((f16[98,256]{1,0:T(8,128)(2,1)S(1)}, f16[98,256]{1,0:T(8,128)(2,1)S(1)}, u32[]{:S(2)}, u32[]{:S(2)}) %collective-permute-start.4) | collective-permute-done | bytes 50208 | tf_op jit(solution)/shard_map/ppermute | solution.py:49
  20.1 0.0 slice-start.1
  20.1 0.1 fusion.summed
  20.2 0.6 %shard_map.75 = bf16[8,2048]{1,0:T(8,128)(2,1)S(1)} custom-call(f32[96,256]{1,0:T(8,128)S(1)} %fusion.summed, bf16[256,2048]{1,0:T(8,128)(2,1)S(1)} %get-tuple-element.11.spread_out, bf16[128,128]{1,0:T(8,128)(2,1)S(1)} %get-tuple-element.12.spread_in), custom_call_target="tpu_custom_call" | custom-call | flops 8589934592 | bytes 16777216 | tf_op jit(solution)/shard_map/pallas_call | solution.py:155
  20.8 1.3 %collective-permute-start.7 = (bf16[8,2048]{1,0:T(8,128)(2,1)S(1)}, bf16[8,2048]{1,0:T(8,128)(2,1)S(1)}, u32[]{:S(2)}, u32[]{:S(2)}) collective-permute-start(bf16[8,2048]{1,0:T(8,128)(2,1)S(1)} %shard_map.75), channel_id=1, source_target_pairs={{0,7},{1,6},{2,5},{3,4},{4,3},{5,2},{6,1},{7,0},{8,15},{9,14},{10,... | collective-permute-start | bytes 98312 | tf_op jit(solution)/shard_map/ppermute | solution.py:49
  22.1 1.5 %collective-permute-start.6 = (bf16[8,2048]{1,0:T(8,128)(2,1)S(1)}, bf16[8,2048]{1,0:T(8,128)(2,1)S(1)}, u32[]{:S(2)}, u32[]{:S(2)}) collective-permute-start(bf16[8,2048]{1,0:T(8,128)(2,1)S(1)} %shard_map.75), channel_id=1, source_target_pairs={{0,6},{1,7},{2,4},{3,5},{4,2},{5,3},{6,0},{7,1},{8,14},{9,15},{10,... | collective-permute-start | bytes 98312 | tf_op jit(solution)/shard_map/ppermute | solution.py:49
  23.6 0.5 %collective-permute-start.5 = (bf16[8,2048]{1,0:T(8,128)(2,1)S(1)}, bf16[8,2048]{1,0:T(8,128)(2,1)S(1)}, u32[]{:S(2)}, u32[]{:S(2)}) collective-permute-start(bf16[8,2048]{1,0:T(8,128)(2,1)S(1)} %shard_map.75), channel_id=1, source_target_pairs={{0,1},{1,0},{2,3},{3,2},{4,5},{5,4},{6,7},{7,6},{8,9},{9,8},{10,11... | collective-permute-start | bytes 98312 | tf_op jit(solution)/shard_map/ppermute | solution.py:49
  24.1 1.1 %collective-permute-done.7 = bf16[8,2048]{1,0:T(8,128)(2,1)S(1)} collective-permute-done((bf16[8,2048]{1,0:T(8,128)(2,1)S(1)}, bf16[8,2048]{1,0:T(8,128)(2,1)S(1)}, u32[]{:S(2)}, u32[]{:S(2)}) %collective-permute-start.7) | collective-permute-done | bytes 32800 | tf_op jit(solution)/shard_map/ppermute | solution.py:49
  25.1 0.8 %collective-permute-done.6 = bf16[8,2048]{1,0:T(8,128)(2,1)S(1)} collective-permute-done((bf16[8,2048]{1,0:T(8,128)(2,1)S(1)}, bf16[8,2048]{1,0:T(8,128)(2,1)S(1)}, u32[]{:S(2)}, u32[]{:S(2)}) %collective-permute-start.6) | collective-permute-done | bytes 32800 | tf_op jit(solution)/shard_map/ppermute | solution.py:49
  25.9 1.6 %collective-permute-done.5 = bf16[8,2048]{1,0:T(8,128)(2,1)S(1)} collective-permute-done((bf16[8,2048]{1,0:T(8,128)(2,1)S(1)}, bf16[8,2048]{1,0:T(8,128)(2,1)S(1)}, u32[]{:S(2)}, u32[]{:S(2)}) %collective-permute-start.5) | collective-permute-done | bytes 32800 | tf_op jit(solution)/shard_map/ppermute | solution.py:49
  27.5 0.1 collective-permute-start.8
  27.6 1.3 %collective-permute-done.8.got = bf16[32,2048]{1,0:T(8,128)(2,1)S(1)} collective-permute-done((bf16[32,2048]{1,0:T(8,128)(2,1)S(1)}, bf16[32,2048]{1,0:T(8,128)(2,1)S(1)}, u32[]{:S(2)}, u32[]{:S(2)}) %collective-permute-start.8) | collective-permute-done | bytes 131104 | tf_op jit(solution)/shard_map/ppermute | solution.py:49
  28.9 0.0 slice-done
  28.9 0.0 slice-done.1
  28.9 2.8 %shard_map.76 = f32[64,1536]{1,0:T(8,128)} custom-call(bf16[32,2048]{1,0:T(8,128)(2,1)S(1)} %pad_add_fusion.held, bf16[32,2048]{1,0:T(8,128)(2,1)S(1)} %collective-permute-done.8.got, bf16[1536,2048]{1,0:T(8,128)(2,1)S(1)} %bitcast.17), custom_call_target="tpu_custom_call" | custom-call | tf_op jit(solution)/shard_map/pallas_call | solution.py:181
  (23 shorter events, 0.2 us)
Async XLA Ops:
  3.1 1.6 %collective-permute-start = (f32[2,96,256]{2,1,0:T(8,128)S(1)}, f32[2,96,256]{2,1,0:T(8,128)S(1)}, u32[]{:S(2)}, u32[]{:S(2)}) collective-permute-start(f32[2,96,256]{2,1,0:T(8,128)S(1)} %get-tuple-element.10), channel_id=1, source_target_pairs={{0,2},{1,3},{2,0},{3,1},{4,6},{5,7},{6,4},{7,5},{8,10},{9,11},{10,... | collective-permute-start | bytes 589832 | tf_op jit(solution)/shard_map/ppermute | solution.py:49
  5.0 5.1 %collective-permute-start.3 = (f16[98,256]{1,0:T(8,128)(2,1)S(1)}, f16[98,256]{1,0:T(8,128)(2,1)S(1)}, u32[]{:S(2)}, u32[]{:S(2)}) collective-permute-start(f16[98,256]{1,0:T(8,128)(2,1)S(1)} %get-tuple-element.28), channel_id=1, source_target_pairs={{0,8},{1,9},{2,10},{3,11},{4,12},{5,13},{6,14},{7,15},{8,0},{9,1},... | collective-permute-start | bytes 150536 | tf_op jit(solution)/shard_map/ppermute | solution.py:49
  8.0 4.1 %collective-permute-start.2 = (f16[98,256]{1,0:T(8,128)(2,1)S(1)}, f16[98,256]{1,0:T(8,128)(2,1)S(1)}, u32[]{:S(2)}, u32[]{:S(2)}) collective-permute-start(f16[98,256]{1,0:T(8,128)(2,1)S(1)} %get-tuple-element.27), channel_id=1, source_target_pairs={{0,6},{1,7},{2,4},{3,5},{4,2},{5,3},{6,0},{7,1},{8,14},{9,15},{10,... | collective-permute-start | bytes 150536 | tf_op jit(solution)/shard_map/ppermute | solution.py:49
  8.9 4.5 %collective-permute-start.1 = (f16[98,256]{1,0:T(8,128)(2,1)S(1)}, f16[98,256]{1,0:T(8,128)(2,1)S(1)}, u32[]{:S(2)}, u32[]{:S(2)}) collective-permute-start(f16[98,256]{1,0:T(8,128)(2,1)S(1)} %get-tuple-element.27), channel_id=1, source_target_pairs={{0,14},{1,15},{2,12},{3,13},{4,10},{5,11},{6,8},{7,9},{8,6},{9,7},... | collective-permute-start | bytes 150536 | tf_op jit(solution)/shard_map/ppermute | solution.py:49
  13.8 6.3 %collective-permute-start.4 = (f16[98,256]{1,0:T(8,128)(2,1)S(1)}, f16[98,256]{1,0:T(8,128)(2,1)S(1)}, u32[]{:S(2)}, u32[]{:S(2)}) collective-permute-start(f16[98,256]{1,0:T(8,128)(2,1)S(1)} %select_convert_fusion), channel_id=1, source_target_pairs={{0,18},{1,19},{2,16},{3,17},{4,22},{5,23},{6,20},{7,21},{8,26},{9,... | collective-permute-start | bytes 150536 | tf_op jit(solution)/shard_map/ppermute | solution.py:49
  16.7 0.8 %copy-start = (f32[64,64]{1,0:T(8,128)S(1)}, f32[64,64]{1,0:T(8,128)}, u32[]{:S(2)}) copy-start(f32[64,64]{1,0:T(8,128)} %out_inverse.1) | copy-start | bytes 49156
  17.4 0.7 %copy-start.1 = (f32[32,32]{1,0:T(8,128)S(1)}, f32[32,32]{1,0:T(8,128)}, u32[]{:S(2)}) copy-start(f32[32,32]{1,0:T(8,128)} %in_inverse.1) | copy-start | bytes 12292
  18.2 10.7 %slice-start = ((s8[6291456]{0:T(1024)(128)(4,1)}), s8[4194304]{0:T(1024)(128)(4,1)S(1)}, s32[]{:S(2)}) async-start(s8[6291456]{0:T(1024)(128)(4,1)} %bitcast.16), calls=%async_computation | async-start | bytes 8388608
  20.1 8.8 %slice-start.1 = ((s8[6291456]{0:T(1024)(128)(4,1)}), s8[2097152]{0:T(1024)(128)(4,1)S(1)}, s32[]{:S(2)}) async-start(s8[6291456]{0:T(1024)(128)(4,1)} %bitcast.16), calls=%async_computation.1 | async-start | bytes 4194304
  20.8 4.4 %collective-permute-start.7 = (bf16[8,2048]{1,0:T(8,128)(2,1)S(1)}, bf16[8,2048]{1,0:T(8,128)(2,1)S(1)}, u32[]{:S(2)}, u32[]{:S(2)}) collective-permute-start(bf16[8,2048]{1,0:T(8,128)(2,1)S(1)} %shard_map.75), channel_id=1, source_target_pairs={{0,7},{1,6},{2,5},{3,4},{4,3},{5,2},{6,1},{7,0},{8,15},{9,14},{10,... | collective-permute-start | bytes 98312 | tf_op jit(solution)/shard_map/ppermute | solution.py:49
  22.1 3.8 %collective-permute-start.6 = (bf16[8,2048]{1,0:T(8,128)(2,1)S(1)}, bf16[8,2048]{1,0:T(8,128)(2,1)S(1)}, u32[]{:S(2)}, u32[]{:S(2)}) collective-permute-start(bf16[8,2048]{1,0:T(8,128)(2,1)S(1)} %shard_map.75), channel_id=1, source_target_pairs={{0,6},{1,7},{2,4},{3,5},{4,2},{5,3},{6,0},{7,1},{8,14},{9,15},{10,... | collective-permute-start | bytes 98312 | tf_op jit(solution)/shard_map/ppermute | solution.py:49
  23.6 3.9 %collective-permute-start.5 = (bf16[8,2048]{1,0:T(8,128)(2,1)S(1)}, bf16[8,2048]{1,0:T(8,128)(2,1)S(1)}, u32[]{:S(2)}, u32[]{:S(2)}) collective-permute-start(bf16[8,2048]{1,0:T(8,128)(2,1)S(1)} %shard_map.75), channel_id=1, source_target_pairs={{0,1},{1,0},{2,3},{3,2},{4,5},{5,4},{6,7},{7,6},{8,9},{9,8},{10,11... | collective-permute-start | bytes 98312 | tf_op jit(solution)/shard_map/ppermute | solution.py:49
  27.5 1.4 %collective-permute-start.8 = (bf16[32,2048]{1,0:T(8,128)(2,1)S(1)}, bf16[32,2048]{1,0:T(8,128)(2,1)S(1)}, u32[]{:S(2)}, u32[]{:S(2)}) collective-permute-start(bf16[32,2048]{1,0:T(8,128)(2,1)S(1)} %pad_add_fusion.held), channel_id=1, source_target_pairs={{0,2},{1,3},{2,0},{3,1},{4,6},{5,7},{6,4},{7,5},{8,10},{9,11},{10,... | collective-permute-start | bytes 393224 | tf_op jit(solution)/shard_map/ppermute | solution.py:49

commit v4 on v3

--- a/solution.py
+++ b/solution.py
@@ -13,6 +13,7 @@
 HBM = pl.BlockSpec(memory_space=pltpu.HBM)
 MIB = 1 << 20
 PROJECT_VMEM = 55_889_920
+CROSS = (-1, -2, -1)
 HIGH = 12
 
 
@@ -34,7 +35,7 @@
 
 
 def exchange(value, sizes, wide=0, grp=0, blk=0):
-    flip = odd_bits(wide) ^ odd_bits(grp >> 1)
+    flip = odd_bits(wide & CROSS[0]) ^ odd_bits(grp & CROSS[1]) ^ odd_bits(blk & CROSS[2])
     return swap(value, sizes, {"wide": 2 * wide + flip, "grp": grp, "blk": blk})
 
 
@@ -50,8 +51,11 @@
 
 
 def own_half():
-    slot, group = lax.axis_index("wide"), lax.axis_index("grp")
-    return lax.rem(slot, 2) ^ odd_bits(slot // 2) ^ odd_bits(group // 2)
+    slot = lax.axis_index("wide")
+    half = lax.rem(slot, 2)
+    for value, mask in zip((slot // 2, lax.axis_index("grp"), lax.axis_index("blk")), CROSS):
+        half = half ^ odd_bits(value & mask)
+    return half
 
 
 def project_kernel(width_in, acts, grads, proj, given, kept, act_buf, grad_buf, sems):
@@ -162,7 +166,7 @@
     )(summed, spread_out, spread_in)
 
 
-def score_kernel(order, wide, held, got, store, out):
+def score_kernel(order, wide, held, got, store, out, part, sems):
     blk, x, half = lax.axis_index("blk"), lax.axis_index("wide") // 2, own_half()
     queries = jnp.concatenate([held[...], got[...]], axis=0)
     rows = out.shape[0] // len(order)
@@ -171,10 +175,16 @@
         for far_blk, far_x, flip in order
     ]
     step = 512
-    for start in range(0, out.shape[1], step):
-        part = contract(queries, store[start : start + step], 1, 1)
+    stores = []
+    for n, start in enumerate(range(0, out.shape[1], step)):
+        columns = pl.ds(start, step)
+        product = contract(store[columns], queries, 1, 1).T
         for r, row in enumerate(targets):
-            out[pl.ds(row, rows), start : start + step] = part[r * rows : (r + 1) * rows]
+            part[pl.ds(row, rows), columns] = product[r * rows : (r + 1) * rows]
+        stores.append(pltpu.make_async_copy(part.at[:, columns], out.at[:, columns], sems.at[n]))
+        stores[-1].start()
+    for copy in stores:
+        copy.wait()
 
 
 def scores(order, wide, held, got, store):
@@ -182,7 +192,11 @@
         functools.partial(score_kernel, order, wide),
         out_shape=jax.ShapeDtypeStruct((2 * held.shape[0], store.shape[0]), jnp.float32),
         in_specs=[VMEM] * 3,
-        out_specs=VMEM,
+        out_specs=HBM,
+        scratch_shapes=[
+            pltpu.VMEM((2 * held.shape[0], store.shape[0]), jnp.float32),
+            pltpu.SemaphoreType.DMA((pl.cdiv(store.shape[0], 512),)),
+        ],
         compiler_params=pltpu.CompilerParams(vmem_limit_bytes=20 * MIB),
     )(held, got, store)
 

time: 32 us -> 31.2 us (0.975)
  waiting for transfers between devices: 11.4 us -> 10.2 us
  starting transfers between devices: 11.1 us -> 11.7 us
    ppermute x9, waiting for transfers between devices: 11.4 us -> 10.2 us  [swap(): return lax.ppermute(value, axes, pairs)]
    ppermute x9, starting transfers between devices: 11.1 us -> 11.7 us  [swap(): return lax.ppermute(value, axes, pairs)]
where the time goes in v4:
time: 31.2 us; the launch traced here: 30.9 us
  starting transfers between devices  11.7 us (38%)
  waiting for transfers between devices  10.2 us (33%)
  Pallas kernels  5.76 us (18%)
  other arithmetic  1.56 us (5%)
  local copies, waits for them, and re-layouts  1.52 us (5%)
    ppermute x9, starting transfers between devices, swap(): return lax.ppermute(value, axes, pairs)  11.7 us
    ppermute x9, waiting for transfers between devices, swap(): return lax.ppermute(value, axes, pairs)  10.2 us
    pallas_call x1, Pallas kernels, scores(): pl.pallas_call(functools.partial(score_kernel, order, wide), out_shape=ja...  2.55 us
    pallas_call x1, Pallas kernels, project(): pl.pallas_call(functools.partial(project_kernel, width_in), out_shape=(ou...  2.24 us
    unnamed x8, local copies, waits for them, and re-layouts  1.49 us
    concatenate x1, other arithmetic, on_device(): proj = jnp.concatenate([in_projection.T, out_projection.T], axis=0)  0.85 us
  transfers between devices with their start and end apart: 9, of which 9 were waited for; matrix products, arithmetic and copies ran while one was open for 0% of the time, Pallas kernels for 1%

profile of v4, /device:TPU:0, one launch (start us, length us, event | category | flops | bytes accessed | tf_op | source)
XLA Modules:
  0.0 30.9 jit_solution(2000478803123796497)
XLA Ops:
  0.0 0.8 %pad_maximum_fusion.proj = bf16[96,512]{1,0:T(8,128)(2,1)S(1)} fusion(bf16[64,512]{1,0:T(8,128)(2,1)} %bitcast.18, bf16[32,512]{1,0:T(8,128)(2,1)} %bitcast.19), kind=kLoop, calls=%fused_computation.14 | loop fusion | flops 196608 | bytes 196608 | tf_op jit(solution)/shard_map/concatenate | solution.py:239
  0.8 2.2 %shard_map.73 = (f32[2,96,256]{2,1,0:T(8,128)S(1)}, f32[2,96,256]{2,1,0:T(8,128)S(1)}) custom-call(bf16[1024,512]{1,0:T(8,128)(2,1)} %acts.1, bf16[1024,512]{1,0:T(8,128)(2,1)} %grads.1, bf16[96,512]{1,0:T(8,128)(2,1)S(1)} %pad_maximum_fusion.proj), custom_call_target="tpu_custom_call" | custom-call | flops 100663296 | bytes 2097152 | tf_op jit(solution)/shard_map/pallas_call | solution.py:84
  3.1 0.5 %collective-permute-start = (f32[2,96,256]{2,1,0:T(8,128)S(1)}, f32[2,96,256]{2,1,0:T(8,128)S(1)}, u32[]{:S(2)}, u32[]{:S(2)}) collective-permute-start(f32[2,96,256]{2,1,0:T(8,128)S(1)} %get-tuple-element.10), channel_id=1, source_target_pairs={{0,2},{1,3},{2,0},{3,1},{4,6},{5,7},{6,4},{7,5},{8,10},{9,11},{10,... | collective-permute-start | bytes 589832 | tf_op jit(solution)/shard_map/ppermute | solution.py:50
  3.6 1.1 %collective-permute-done = f32[2,96,256]{2,1,0:T(8,128)S(1)} collective-permute-done((f32[2,96,256]{2,1,0:T(8,128)S(1)}, f32[2,96,256]{2,1,0:T(8,128)S(1)}, u32[]{:S(2)}, u32[]{:S(2)}) %collective-permute-start) | collective-permute-done | bytes 196640 | tf_op jit(solution)/shard_map/ppermute | solution.py:50
  4.8 0.1 select_convert_fusion.2
  5.0 3.0 %collective-permute-start.3 = (f16[98,256]{1,0:T(8,128)(2,1)S(1)}, f16[98,256]{1,0:T(8,128)(2,1)S(1)}, u32[]{:S(2)}, u32[]{:S(2)}) collective-permute-start(f16[98,256]{1,0:T(8,128)(2,1)S(1)} %get-tuple-element.28), channel_id=1, source_target_pairs={{0,8},{1,9},{2,10},{3,11},{4,12},{5,13},{6,14},{7,15},{8,0},{9,1},... | collective-permute-start | bytes 150536 | tf_op jit(solution)/shard_map/ppermute | solution.py:50
  8.0 1.0 %collective-permute-start.2 = (f16[98,256]{1,0:T(8,128)(2,1)S(1)}, f16[98,256]{1,0:T(8,128)(2,1)S(1)}, u32[]{:S(2)}, u32[]{:S(2)}) collective-permute-start(f16[98,256]{1,0:T(8,128)(2,1)S(1)} %get-tuple-element.27), channel_id=1, source_target_pairs={{0,6},{1,7},{2,4},{3,5},{4,2},{5,3},{6,0},{7,1},{8,14},{9,15},{10,... | collective-permute-start | bytes 150536 | tf_op jit(solution)/shard_map/ppermute | solution.py:50
  8.9 0.3 %collective-permute-start.1 = (f16[98,256]{1,0:T(8,128)(2,1)S(1)}, f16[98,256]{1,0:T(8,128)(2,1)S(1)}, u32[]{:S(2)}, u32[]{:S(2)}) collective-permute-start(f16[98,256]{1,0:T(8,128)(2,1)S(1)} %get-tuple-element.27), channel_id=1, source_target_pairs={{0,14},{1,15},{2,12},{3,13},{4,10},{5,11},{6,8},{7,9},{8,6},{9,7},... | collective-permute-start | bytes 150536 | tf_op jit(solution)/shard_map/ppermute | solution.py:50
  9.3 0.9 %collective-permute-done.3 = f16[98,256]{1,0:T(8,128)(2,1)S(1)} collective-permute-done((f16[98,256]{1,0:T(8,128)(2,1)S(1)}, f16[98,256]{1,0:T(8,128)(2,1)S(1)}, u32[]{:S(2)}, u32[]{:S(2)}) %collective-permute-start.3) | collective-permute-done | bytes 50208 | tf_op jit(solution)/shard_map/ppermute | solution.py:50
  10.1 1.9 %collective-permute-done.2 = f16[98,256]{1,0:T(8,128)(2,1)S(1)} collective-permute-done((f16[98,256]{1,0:T(8,128)(2,1)S(1)}, f16[98,256]{1,0:T(8,128)(2,1)S(1)}, u32[]{:S(2)}, u32[]{:S(2)}) %collective-permute-start.2) | collective-permute-done | bytes 50208 | tf_op jit(solution)/shard_map/ppermute | solution.py:50
  12.1 1.3 %collective-permute-done.1 = f16[98,256]{1,0:T(8,128)(2,1)S(1)} collective-permute-done((f16[98,256]{1,0:T(8,128)(2,1)S(1)}, f16[98,256]{1,0:T(8,128)(2,1)S(1)}, u32[]{:S(2)}, u32[]{:S(2)}) %collective-permute-start.1) | collective-permute-done | bytes 50208 | tf_op jit(solution)/shard_map/ppermute | solution.py:50
  13.4 0.1 fusion.1
  13.6 0.1 select_convert_fusion
  13.8 2.9 %collective-permute-start.4 = (f16[98,256]{1,0:T(8,128)(2,1)S(1)}, f16[98,256]{1,0:T(8,128)(2,1)S(1)}, u32[]{:S(2)}, u32[]{:S(2)}) collective-permute-start(f16[98,256]{1,0:T(8,128)(2,1)S(1)} %select_convert_fusion), channel_id=1, source_target_pairs={{0,18},{1,19},{2,16},{3,17},{4,22},{5,23},{6,20},{7,21},{8,26},{9,... | collective-permute-start | bytes 150536 | tf_op jit(solution)/shard_map/ppermute | solution.py:50
  16.7 0.0 copy-start
  16.7 0.8 %copy-done = f32[64,64]{1,0:T(8,128)S(1)} copy-done((f32[64,64]{1,0:T(8,128)S(1)}, f32[64,64]{1,0:T(8,128)}, u32[]{:S(2)}) %copy-start) | copy-done | bytes 16408
  17.4 0.0 copy-start.1
  17.4 0.7 %copy-done.1 = f32[32,32]{1,0:T(8,128)S(1)} copy-done((f32[32,32]{1,0:T(8,128)S(1)}, f32[32,32]{1,0:T(8,128)}, u32[]{:S(2)}) %copy-start.1) | copy-done | bytes 4120
  18.2 0.0 slice-start
  18.2 0.4 %shard_map.74 = (bf16[256,2048]{1,0:T(8,128)(2,1)S(1)}, bf16[128,128]{1,0:T(8,128)(2,1)S(1)}) custom-call(f32[32,32]{1,0:T(8,128)S(1)} %copy-done.1, f32[64,64]{1,0:T(8,128)S(1)} %copy-done), custom_call_target="tpu_custom_call" | custom-call | flops 8589934592 | bytes 16777216 | tf_op jit(solution)/shard_map/pallas_call | solution.py:125
  18.5 1.5 %collective-permute-done.4 = f16[98,256]{1,0:T(8,128)(2,1)S(1)} collective-permute-done((f16[98,256]{1,0:T(8,128)(2,1)S(1)}, f16[98,256]{1,0:T(8,128)(2,1)S(1)}, u32[]{:S(2)}, u32[]{:S(2)}) %collective-permute-start.4) | collective-permute-done | bytes 50208 | tf_op jit(solution)/shard_map/ppermute | solution.py:50
  20.1 0.0 slice-start.1
  20.1 0.1 fusion.summed
  20.2 0.6 %shard_map.75 = bf16[8,2048]{1,0:T(8,128)(2,1)S(1)} custom-call(f32[96,256]{1,0:T(8,128)S(1)} %fusion.summed, bf16[256,2048]{1,0:T(8,128)(2,1)S(1)} %get-tuple-element.11.spread_out, bf16[128,128]{1,0:T(8,128)(2,1)S(1)} %get-tuple-element.12.spread_in), custom_call_target="tpu_custom_call" | custom-call | flops 8589934592 | bytes 16777216 | tf_op jit(solution)/shard_map/pallas_call | solution.py:159
  20.8 1.6 %collective-permute-start.7 = (bf16[8,2048]{1,0:T(8,128)(2,1)S(1)}, bf16[8,2048]{1,0:T(8,128)(2,1)S(1)}, u32[]{:S(2)}, u32[]{:S(2)}) collective-permute-start(bf16[8,2048]{1,0:T(8,128)(2,1)S(1)} %shard_map.75), channel_id=1, source_target_pairs={{0,5},{1,4},{2,7},{3,6},{4,1},{5,0},{6,3},{7,2},{8,13},{9,12},{10,... | collective-permute-start | bytes 98312 | tf_op jit(solution)/shard_map/ppermute | solution.py:50
  22.4 0.9 %collective-permute-start.6 = (bf16[8,2048]{1,0:T(8,128)(2,1)S(1)}, bf16[8,2048]{1,0:T(8,128)(2,1)S(1)}, u32[]{:S(2)}, u32[]{:S(2)}) collective-permute-start(bf16[8,2048]{1,0:T(8,128)(2,1)S(1)} %shard_map.75), channel_id=1, source_target_pairs={{0,6},{1,7},{2,4},{3,5},{4,2},{5,3},{6,0},{7,1},{8,14},{9,15},{10,... | collective-permute-start | bytes 98312 | tf_op jit(solution)/shard_map/ppermute | solution.py:50
  23.3 0.8 %collective-permute-start.5 = (bf16[8,2048]{1,0:T(8,128)(2,1)S(1)}, bf16[8,2048]{1,0:T(8,128)(2,1)S(1)}, u32[]{:S(2)}, u32[]{:S(2)}) collective-permute-start(bf16[8,2048]{1,0:T(8,128)(2,1)S(1)} %shard_map.75), channel_id=1, source_target_pairs={{0,3},{1,2},{2,1},{3,0},{4,7},{5,6},{6,5},{7,4},{8,11},{9,10},{10,... | collective-permute-start | bytes 98312 | tf_op jit(solution)/shard_map/ppermute | solution.py:50
  24.1 1.9 %collective-permute-done.7 = bf16[8,2048]{1,0:T(8,128)(2,1)S(1)} collective-permute-done((bf16[8,2048]{1,0:T(8,128)(2,1)S(1)}, bf16[8,2048]{1,0:T(8,128)(2,1)S(1)}, u32[]{:S(2)}, u32[]{:S(2)}) %collective-permute-start.7) | collective-permute-done | bytes 32800 | tf_op jit(solution)/shard_map/ppermute | solution.py:50
  25.9 0.1 collective-permute-done.6
  26.0 0.6 %collective-permute-done.5 = bf16[8,2048]{1,0:T(8,128)(2,1)S(1)} collective-permute-done((bf16[8,2048]{1,0:T(8,128)(2,1)S(1)}, bf16[8,2048]{1,0:T(8,128)(2,1)S(1)}, u32[]{:S(2)}, u32[]{:S(2)}) %collective-permute-start.5) | collective-permute-done | bytes 32800 | tf_op jit(solution)/shard_map/ppermute | solution.py:50
  26.6 0.7 %collective-permute-start.8 = (bf16[32,2048]{1,0:T(8,128)(2,1)S(1)}, bf16[32,2048]{1,0:T(8,128)(2,1)S(1)}, u32[]{:S(2)}, u32[]{:S(2)}) collective-permute-start(bf16[32,2048]{1,0:T(8,128)(2,1)S(1)} %pad_add_fusion.held), channel_id=1, source_target_pairs={{0,2},{1,3},{2,0},{3,1},{4,6},{5,7},{6,4},{7,5},{8,10},{9,11},{10,... | collective-permute-start | bytes 393224 | tf_op jit(solution)/shard_map/ppermute | solution.py:50
  27.4 1.0 %collective-permute-done.8.got = bf16[32,2048]{1,0:T(8,128)(2,1)S(1)} collective-permute-done((bf16[32,2048]{1,0:T(8,128)(2,1)S(1)}, bf16[32,2048]{1,0:T(8,128)(2,1)S(1)}, u32[]{:S(2)}, u32[]{:S(2)}) %collective-permute-start.8) | collective-permute-done | bytes 131104 | tf_op jit(solution)/shard_map/ppermute | solution.py:50
  28.4 0.0 slice-done
  28.4 0.0 slice-done.1
  28.4 2.5 %shard_map.76 = f32[64,1536]{1,0:T(8,128)} custom-call(bf16[32,2048]{1,0:T(8,128)(2,1)S(1)} %pad_add_fusion.held, bf16[32,2048]{1,0:T(8,128)(2,1)S(1)} %collective-permute-done.8.got, bf16[1536,2048]{1,0:T(8,128)(2,1)S(1)} %bitcast.17), custom_call_target="tpu_custom_call" | custom-call | tf_op jit(solution)/shard_map/pallas_call | solution.py:191
  (23 shorter events, 0.2 us)
Async XLA Ops:
  3.1 1.6 %collective-permute-start = (f32[2,96,256]{2,1,0:T(8,128)S(1)}, f32[2,96,256]{2,1,0:T(8,128)S(1)}, u32[]{:S(2)}, u32[]{:S(2)}) collective-permute-start(f32[2,96,256]{2,1,0:T(8,128)S(1)} %get-tuple-element.10), channel_id=1, source_target_pairs={{0,2},{1,3},{2,0},{3,1},{4,6},{5,7},{6,4},{7,5},{8,10},{9,11},{10,... | collective-permute-start | bytes 589832 | tf_op jit(solution)/shard_map/ppermute | solution.py:50
  5.0 5.1 %collective-permute-start.3 = (f16[98,256]{1,0:T(8,128)(2,1)S(1)}, f16[98,256]{1,0:T(8,128)(2,1)S(1)}, u32[]{:S(2)}, u32[]{:S(2)}) collective-permute-start(f16[98,256]{1,0:T(8,128)(2,1)S(1)} %get-tuple-element.28), channel_id=1, source_target_pairs={{0,8},{1,9},{2,10},{3,11},{4,12},{5,13},{6,14},{7,15},{8,0},{9,1},... | collective-permute-start | bytes 150536 | tf_op jit(solution)/shard_map/ppermute | solution.py:50
  8.0 4.1 %collective-permute-start.2 = (f16[98,256]{1,0:T(8,128)(2,1)S(1)}, f16[98,256]{1,0:T(8,128)(2,1)S(1)}, u32[]{:S(2)}, u32[]{:S(2)}) collective-permute-start(f16[98,256]{1,0:T(8,128)(2,1)S(1)} %get-tuple-element.27), channel_id=1, source_target_pairs={{0,6},{1,7},{2,4},{3,5},{4,2},{5,3},{6,0},{7,1},{8,14},{9,15},{10,... | collective-permute-start | bytes 150536 | tf_op jit(solution)/shard_map/ppermute | solution.py:50
  8.9 4.5 %collective-permute-start.1 = (f16[98,256]{1,0:T(8,128)(2,1)S(1)}, f16[98,256]{1,0:T(8,128)(2,1)S(1)}, u32[]{:S(2)}, u32[]{:S(2)}) collective-permute-start(f16[98,256]{1,0:T(8,128)(2,1)S(1)} %get-tuple-element.27), channel_id=1, source_target_pairs={{0,14},{1,15},{2,12},{3,13},{4,10},{5,11},{6,8},{7,9},{8,6},{9,7},... | collective-permute-start | bytes 150536 | tf_op jit(solution)/shard_map/ppermute | solution.py:50
  13.8 6.3 %collective-permute-start.4 = (f16[98,256]{1,0:T(8,128)(2,1)S(1)}, f16[98,256]{1,0:T(8,128)(2,1)S(1)}, u32[]{:S(2)}, u32[]{:S(2)}) collective-permute-start(f16[98,256]{1,0:T(8,128)(2,1)S(1)} %select_convert_fusion), channel_id=1, source_target_pairs={{0,18},{1,19},{2,16},{3,17},{4,22},{5,23},{6,20},{7,21},{8,26},{9,... | collective-permute-start | bytes 150536 | tf_op jit(solution)/shard_map/ppermute | solution.py:50
  16.7 0.8 %copy-start = (f32[64,64]{1,0:T(8,128)S(1)}, f32[64,64]{1,0:T(8,128)}, u32[]{:S(2)}) copy-start(f32[64,64]{1,0:T(8,128)} %out_inverse.1) | copy-start | bytes 49156
  17.4 0.7 %copy-start.1 = (f32[32,32]{1,0:T(8,128)S(1)}, f32[32,32]{1,0:T(8,128)}, u32[]{:S(2)}) copy-start(f32[32,32]{1,0:T(8,128)} %in_inverse.1) | copy-start | bytes 12292
  18.2 10.2 %slice-start = ((s8[6291456]{0:T(1024)(128)(4,1)}), s8[4194304]{0:T(1024)(128)(4,1)S(1)}, s32[]{:S(2)}) async-start(s8[6291456]{0:T(1024)(128)(4,1)} %bitcast.16), calls=%async_computation | async-start | bytes 8388608
  20.1 8.3 %slice-start.1 = ((s8[6291456]{0:T(1024)(128)(4,1)}), s8[2097152]{0:T(1024)(128)(4,1)S(1)}, s32[]{:S(2)}) async-start(s8[6291456]{0:T(1024)(128)(4,1)} %bitcast.16), calls=%async_computation.1 | async-start | bytes 4194304
  20.8 5.1 %collective-permute-start.7 = (bf16[8,2048]{1,0:T(8,128)(2,1)S(1)}, bf16[8,2048]{1,0:T(8,128)(2,1)S(1)}, u32[]{:S(2)}, u32[]{:S(2)}) collective-permute-start(bf16[8,2048]{1,0:T(8,128)(2,1)S(1)} %shard_map.75), channel_id=1, source_target_pairs={{0,5},{1,4},{2,7},{3,6},{4,1},{5,0},{6,3},{7,2},{8,13},{9,12},{10,... | collective-permute-start | bytes 98312 | tf_op jit(solution)/shard_map/ppermute | solution.py:50
  22.4 3.7 %collective-permute-start.6 = (bf16[8,2048]{1,0:T(8,128)(2,1)S(1)}, bf16[8,2048]{1,0:T(8,128)(2,1)S(1)}, u32[]{:S(2)}, u32[]{:S(2)}) collective-permute-start(bf16[8,2048]{1,0:T(8,128)(2,1)S(1)} %shard_map.75), channel_id=1, source_target_pairs={{0,6},{1,7},{2,4},{3,5},{4,2},{5,3},{6,0},{7,1},{8,14},{9,15},{10,... | collective-permute-start | bytes 98312 | tf_op jit(solution)/shard_map/ppermute | solution.py:50
  23.3 3.3 %collective-permute-start.5 = (bf16[8,2048]{1,0:T(8,128)(2,1)S(1)}, bf16[8,2048]{1,0:T(8,128)(2,1)S(1)}, u32[]{:S(2)}, u32[]{:S(2)}) collective-permute-start(bf16[8,2048]{1,0:T(8,128)(2,1)S(1)} %shard_map.75), channel_id=1, source_target_pairs={{0,3},{1,2},{2,1},{3,0},{4,7},{5,6},{6,5},{7,4},{8,11},{9,10},{10,... | collective-permute-start | bytes 98312 | tf_op jit(solution)/shard_map/ppermute | solution.py:50
  26.6 1.7 %collective-permute-start.8 = (bf16[32,2048]{1,0:T(8,128)(2,1)S(1)}, bf16[32,2048]{1,0:T(8,128)(2,1)S(1)}, u32[]{:S(2)}, u32[]{:S(2)}) collective-permute-start(bf16[32,2048]{1,0:T(8,128)(2,1)S(1)} %pad_add_fusion.held), channel_id=1, source_target_pairs={{0,2},{1,3},{2,0},{3,1},{4,6},{5,7},{6,4},{7,5},{8,10},{9,11},{10,... | collective-permute-start | bytes 393224 | tf_op jit(solution)/shard_map/ppermute | solution.py:50

commit v5 on v4

--- a/solution.py
+++ b/solution.py
@@ -1,5 +1,6 @@
 import functools
 import itertools
+import math
 
 import jax
 import jax.numpy as jnp
@@ -13,7 +14,7 @@
 HBM = pl.BlockSpec(memory_space=pltpu.HBM)
 MIB = 1 << 20
 PROJECT_VMEM = 55_889_920
-CROSS = (-1, -2, -1)
+CROSS = (-1, -2, 0)
 HIGH = 12
 
 
@@ -146,7 +147,7 @@
     side_in = jnp.concatenate([in_high, in_high, in_low, in_low], axis=1)
     side_out = jnp.concatenate([out_high, out_high, out_low, out_low], axis=1)
     spread_in_low = contract(side_in, spread_in[...], 1, 0)
-    step = 256
+    step = math.gcd(columns, 256)
     wide = jnp.concatenate([spread_in_low] * (step // lanes), axis=1)
     for start in range(0, columns, step):
         part = contract(side_out, spread_out[:, start : start + step], 1, 0) * wide
@@ -174,7 +175,7 @@
         pl.multiple_of((((blk ^ far_blk) * (wide // 2) + (x ^ far_x)) * 2 + (half ^ flip)) * rows, rows)
         for far_blk, far_x, flip in order
     ]
-    step = 512
+    step = math.gcd(out.shape[1], 512)
     stores = []
     for n, start in enumerate(range(0, out.shape[1], step)):
         columns = pl.ds(start, step)
@@ -195,19 +196,15 @@
         out_specs=HBM,
         scratch_shapes=[
             pltpu.VMEM((2 * held.shape[0], store.shape[0]), jnp.float32),
-            pltpu.SemaphoreType.DMA((pl.cdiv(store.shape[0], 512),)),
+            pltpu.SemaphoreType.DMA((store.shape[0] // math.gcd(store.shape[0], 512),)),
         ],
         compiler_params=pltpu.CompilerParams(vmem_limit_bytes=20 * MIB),
     )(held, got, store)
 
 
-def stack(pieces):
-    rows = pieces[0].shape[0]
-    zero = jnp.zeros((), pieces[0].dtype)
-    return sum(
-        lax.pad(piece, zero, ((n * rows, (len(pieces) - 1 - n) * rows, 0), (0, 0, 0)))
-        for n, piece in enumerate(pieces)
-    )
+def pad_rows(piece, place, places):
+    rows, zero = piece.shape[0], jnp.zeros((), piece.dtype)
+    return lax.pad(piece, zero, ((place * rows, (places - 1 - place) * rows, 0), (0, 0, 0)))
 
 
 def encode(value, width_in):
@@ -253,12 +250,14 @@
     order = [(0, 0)]
     bit = 2
     while bit < blocks:
-        queries = stack([queries, exchange(queries, sizes, blk=bit)])
+        queries = pad_rows(queries, 0, 2) + pad_rows(exchange(queries, sizes, blk=bit), 1, 2)
         order += [(b ^ bit, x) for b, x in order]
         bit *= 2
     near = [(b, x) for x in range(slices) for b in range(min(blocks, 2))]
     others = [exchange(queries, sizes, blk=b, wide=x) for b, x in near[:0:-1]]
-    queries = stack([queries] + others[::-1])
+    queries = pad_rows(queries, 0, len(near))
+    for n, other in zip(range(len(near) - 1, 0, -1), others):
+        queries = lax.optimization_barrier(queries + pad_rows(other, n, len(near)))
     order = [(b ^ c, x ^ y) for c, y in near for b, x in order]
     order = tuple((b, x, flip) for flip in range(2) for b, x in order)
     return scores(order, wide, queries, swap(queries, sizes, {"wide": 1}), grad_store)

time: 31.2 us -> 30.4 us (0.974)
  starting transfers between devices: 11.7 us -> 10.9 us
    ppermute x9, starting transfers between devices: 11.7 us -> 10.9 us  [swap(): return lax.ppermute(value, axes, pairs)]
where the time goes in v5:
time: 30.4 us; the launch traced here: 30.1 us
  starting transfers between devices  10.9 us (36%)
  waiting for transfers between devices  10.2 us (34%)
  Pallas kernels  5.75 us (19%)
  other arithmetic  1.59 us (5%)
  local copies, waits for them, and re-layouts  1.52 us (5%)
    ppermute x9, starting transfers between devices, swap(): return lax.ppermute(value, axes, pairs)  10.9 us
    ppermute x9, waiting for transfers between devices, swap(): return lax.ppermute(value, axes, pairs)  10.2 us
    pallas_call x1, Pallas kernels, scores(): pl.pallas_call(functools.partial(score_kernel, order, wide), out_shape=ja...  2.55 us
    pallas_call x1, Pallas kernels, project(): pl.pallas_call(functools.partial(project_kernel, width_in), out_shape=(ou...  2.23 us
    unnamed x8, local copies, waits for them, and re-layouts  1.49 us
    concatenate x1, other arithmetic, on_device(): proj = jnp.concatenate([in_projection.T, out_projection.T], axis=0)  0.85 us
  transfers between devices with their start and end apart: 9, of which 9 were waited for; matrix products, arithmetic and copies ran while one was open for 0% of the time, Pallas kernels for 1%

profile of v5, /device:TPU:0, one launch (start us, length us, event | category | flops | bytes accessed | tf_op | source)
XLA Modules:
  0.0 30.1 jit_solution(15780648257256348118)
XLA Ops:
  0.0 0.8 %pad_maximum_fusion.proj = bf16[96,512]{1,0:T(8,128)(2,1)S(1)} fusion(bf16[64,512]{1,0:T(8,128)(2,1)} %bitcast.18, bf16[32,512]{1,0:T(8,128)(2,1)} %bitcast.19), kind=kLoop, calls=%fused_computation.16 | loop fusion | flops 196608 | bytes 196608 | tf_op jit(solution)/shard_map/concatenate | solution.py:236
  0.8 2.2 %shard_map.73 = (f32[2,96,256]{2,1,0:T(8,128)S(1)}, f32[2,96,256]{2,1,0:T(8,128)S(1)}) custom-call(bf16[1024,512]{1,0:T(8,128)(2,1)} %acts.1, bf16[1024,512]{1,0:T(8,128)(2,1)} %grads.1, bf16[96,512]{1,0:T(8,128)(2,1)S(1)} %pad_maximum_fusion.proj), custom_call_target="tpu_custom_call" | custom-call | flops 100663296 | bytes 2097152 | tf_op jit(solution)/shard_map/pallas_call | solution.py:85
  3.1 0.5 %collective-permute-start = (f32[2,96,256]{2,1,0:T(8,128)S(1)}, f32[2,96,256]{2,1,0:T(8,128)S(1)}, u32[]{:S(2)}, u32[]{:S(2)}) collective-permute-start(f32[2,96,256]{2,1,0:T(8,128)S(1)} %get-tuple-element.10), channel_id=1, source_target_pairs={{0,2},{1,3},{2,0},{3,1},{4,6},{5,7},{6,4},{7,5},{8,10},{9,11},{10,... | collective-permute-start | bytes 589832 | tf_op jit(solution)/shard_map/ppermute | solution.py:51
  3.6 1.1 %collective-permute-done = f32[2,96,256]{2,1,0:T(8,128)S(1)} collective-permute-done((f32[2,96,256]{2,1,0:T(8,128)S(1)}, f32[2,96,256]{2,1,0:T(8,128)S(1)}, u32[]{:S(2)}, u32[]{:S(2)}) %collective-permute-start) | collective-permute-done | bytes 196640 | tf_op jit(solution)/shard_map/ppermute | solution.py:51
  4.8 0.1 select_convert_fusion.2
  5.0 3.0 %collective-permute-start.3 = (f16[98,256]{1,0:T(8,128)(2,1)S(1)}, f16[98,256]{1,0:T(8,128)(2,1)S(1)}, u32[]{:S(2)}, u32[]{:S(2)}) collective-permute-start(f16[98,256]{1,0:T(8,128)(2,1)S(1)} %get-tuple-element.28), channel_id=1, source_target_pairs={{0,8},{1,9},{2,10},{3,11},{4,12},{5,13},{6,14},{7,15},{8,0},{9,1},... | collective-permute-start | bytes 150536 | tf_op jit(solution)/shard_map/ppermute | solution.py:51
  8.0 1.0 %collective-permute-start.2 = (f16[98,256]{1,0:T(8,128)(2,1)S(1)}, f16[98,256]{1,0:T(8,128)(2,1)S(1)}, u32[]{:S(2)}, u32[]{:S(2)}) collective-permute-start(f16[98,256]{1,0:T(8,128)(2,1)S(1)} %get-tuple-element.27), channel_id=1, source_target_pairs={{0,6},{1,7},{2,4},{3,5},{4,2},{5,3},{6,0},{7,1},{8,14},{9,15},{10,... | collective-permute-start | bytes 150536 | tf_op jit(solution)/shard_map/ppermute | solution.py:51
  8.9 0.3 %collective-permute-start.1 = (f16[98,256]{1,0:T(8,128)(2,1)S(1)}, f16[98,256]{1,0:T(8,128)(2,1)S(1)}, u32[]{:S(2)}, u32[]{:S(2)}) collective-permute-start(f16[98,256]{1,0:T(8,128)(2,1)S(1)} %get-tuple-element.27), channel_id=1, source_target_pairs={{0,14},{1,15},{2,12},{3,13},{4,10},{5,11},{6,8},{7,9},{8,6},{9,7},... | collective-permute-start | bytes 150536 | tf_op jit(solution)/shard_map/ppermute | solution.py:51
  9.2 0.9 %collective-permute-done.3 = f16[98,256]{1,0:T(8,128)(2,1)S(1)} collective-permute-done((f16[98,256]{1,0:T(8,128)(2,1)S(1)}, f16[98,256]{1,0:T(8,128)(2,1)S(1)}, u32[]{:S(2)}, u32[]{:S(2)}) %collective-permute-start.3) | collective-permute-done | bytes 50208 | tf_op jit(solution)/shard_map/ppermute | solution.py:51
  10.1 1.9 %collective-permute-done.2 = f16[98,256]{1,0:T(8,128)(2,1)S(1)} collective-permute-done((f16[98,256]{1,0:T(8,128)(2,1)S(1)}, f16[98,256]{1,0:T(8,128)(2,1)S(1)}, u32[]{:S(2)}, u32[]{:S(2)}) %collective-permute-start.2) | collective-permute-done | bytes 50208 | tf_op jit(solution)/shard_map/ppermute | solution.py:51
  12.1 1.3 %collective-permute-done.1 = f16[98,256]{1,0:T(8,128)(2,1)S(1)} collective-permute-done((f16[98,256]{1,0:T(8,128)(2,1)S(1)}, f16[98,256]{1,0:T(8,128)(2,1)S(1)}, u32[]{:S(2)}, u32[]{:S(2)}) %collective-permute-start.1) | collective-permute-done | bytes 50208 | tf_op jit(solution)/shard_map/ppermute | solution.py:51
  13.4 0.1 fusion.1
  13.6 0.1 select_convert_fusion
  13.8 2.9 %collective-permute-start.4 = (f16[98,256]{1,0:T(8,128)(2,1)S(1)}, f16[98,256]{1,0:T(8,128)(2,1)S(1)}, u32[]{:S(2)}, u32[]{:S(2)}) collective-permute-start(f16[98,256]{1,0:T(8,128)(2,1)S(1)} %select_convert_fusion), channel_id=1, source_target_pairs={{0,18},{1,19},{2,16},{3,17},{4,22},{5,23},{6,20},{7,21},{8,26},{9,... | collective-permute-start | bytes 150536 | tf_op jit(solution)/shard_map/ppermute | solution.py:51
  16.7 0.0 copy-start
  16.7 0.8 %copy-done = f32[64,64]{1,0:T(8,128)S(1)} copy-done((f32[64,64]{1,0:T(8,128)S(1)}, f32[64,64]{1,0:T(8,128)}, u32[]{:S(2)}) %copy-start) | copy-done | bytes 16408
  17.4 0.0 copy-start.1
  17.4 0.7 %copy-done.1 = f32[32,32]{1,0:T(8,128)S(1)} copy-done((f32[32,32]{1,0:T(8,128)S(1)}, f32[32,32]{1,0:T(8,128)}, u32[]{:S(2)}) %copy-start.1) | copy-done | bytes 4120
  18.2 0.0 slice-start
  18.2 0.4 %shard_map.74 = (bf16[256,2048]{1,0:T(8,128)(2,1)S(1)}, bf16[128,128]{1,0:T(8,128)(2,1)S(1)}) custom-call(f32[32,32]{1,0:T(8,128)S(1)} %copy-done.1, f32[64,64]{1,0:T(8,128)S(1)} %copy-done), custom_call_target="tpu_custom_call" | custom-call | flops 8589934592 | bytes 16777216 | tf_op jit(solution)/shard_map/pallas_call | solution.py:126
  18.5 1.5 %collective-permute-done.4 = f16[98,256]{1,0:T(8,128)(2,1)S(1)} collective-permute-done((f16[98,256]{1,0:T(8,128)(2,1)S(1)}, f16[98,256]{1,0:T(8,128)(2,1)S(1)}, u32[]{:S(2)}, u32[]{:S(2)}) %collective-permute-start.4) | collective-permute-done | bytes 50208 | tf_op jit(solution)/shard_map/ppermute | solution.py:51
  20.0 0.1 fusion.summed
  20.2 0.0 slice-start.1
  20.2 0.6 %shard_map.75 = bf16[8,2048]{1,0:T(8,128)(2,1)S(1)} custom-call(f32[96,256]{1,0:T(8,128)S(1)} %fusion.summed, bf16[256,2048]{1,0:T(8,128)(2,1)S(1)} %get-tuple-element.11.spread_out, bf16[128,128]{1,0:T(8,128)(2,1)S(1)} %get-tuple-element.12.spread_in), custom_call_target="tpu_custom_call" | custom-call | flops 8589934592 | bytes 16777216 | tf_op jit(solution)/shard_map/pallas_call | solution.py:160
  20.8 1.3 %collective-permute-start.5 = (bf16[8,2048]{1,0:T(8,128)(2,1)S(1)}, bf16[8,2048]{1,0:T(8,128)(2,1)S(1)}, u32[]{:S(2)}, u32[]{:S(2)}) collective-permute-start(bf16[8,2048]{1,0:T(8,128)(2,1)S(1)} %shard_map.75), channel_id=1, source_target_pairs={{0,7},{1,6},{2,5},{3,4},{4,3},{5,2},{6,1},{7,0},{8,15},{9,14},{10,... | collective-permute-start | bytes 98312 | tf_op jit(solution)/shard_map/ppermute | solution.py:51
  22.1 0.5 %collective-permute-start.7 = (bf16[8,2048]{1,0:T(8,128)(2,1)S(1)}, bf16[8,2048]{1,0:T(8,128)(2,1)S(1)}, u32[]{:S(2)}, u32[]{:S(2)}) collective-permute-start(bf16[8,2048]{1,0:T(8,128)(2,1)S(1)} %shard_map.75), channel_id=1, source_target_pairs={{0,1},{1,0},{2,3},{3,2},{4,5},{5,4},{6,7},{7,6},{8,9},{9,8},{10,11... | collective-permute-start | bytes 98312 | tf_op jit(solution)/shard_map/ppermute | solution.py:51
  22.5 1.2 %collective-permute-start.6 = (bf16[8,2048]{1,0:T(8,128)(2,1)S(1)}, bf16[8,2048]{1,0:T(8,128)(2,1)S(1)}, u32[]{:S(2)}, u32[]{:S(2)}) collective-permute-start(bf16[8,2048]{1,0:T(8,128)(2,1)S(1)} %shard_map.75), channel_id=1, source_target_pairs={{0,6},{1,7},{2,4},{3,5},{4,2},{5,3},{6,0},{7,1},{8,14},{9,15},{10,... | collective-permute-start | bytes 98312 | tf_op jit(solution)/shard_map/ppermute | solution.py:51
  23.8 1.4 %collective-permute-done.5 = bf16[8,2048]{1,0:T(8,128)(2,1)S(1)} collective-permute-done((bf16[8,2048]{1,0:T(8,128)(2,1)S(1)}, bf16[8,2048]{1,0:T(8,128)(2,1)S(1)}, u32[]{:S(2)}, u32[]{:S(2)}) %collective-permute-start.5) | collective-permute-done | bytes 32800 | tf_op jit(solution)/shard_map/ppermute | solution.py:51
  25.1 0.8 %collective-permute-done.6 = bf16[8,2048]{1,0:T(8,128)(2,1)S(1)} collective-permute-done((bf16[8,2048]{1,0:T(8,128)(2,1)S(1)}, bf16[8,2048]{1,0:T(8,128)(2,1)S(1)}, u32[]{:S(2)}, u32[]{:S(2)}) %collective-permute-start.6) | collective-permute-done | bytes 32800 | tf_op jit(solution)/shard_map/ppermute | solution.py:51
  26.0 0.1 collective-permute-done.7
  26.2 0.2 collective-permute-start.8
  26.4 1.2 %collective-permute-done.8.got = bf16[32,2048]{1,0:T(8,128)(2,1)S(1)} collective-permute-done((bf16[32,2048]{1,0:T(8,128)(2,1)S(1)}, bf16[32,2048]{1,0:T(8,128)(2,1)S(1)}, u32[]{:S(2)}, u32[]{:S(2)}) %collective-permute-start.8) | collective-permute-done | bytes 131104 | tf_op jit(solution)/shard_map/ppermute | solution.py:51
  27.6 0.0 slice-done
  27.6 0.0 slice-done.1
  27.6 2.5 %shard_map.76 = f32[64,1536]{1,0:T(8,128)} custom-call(bf16[32,2048]{1,0:T(8,128)(2,1)S(1)} %pad_add_fusion.held, bf16[32,2048]{1,0:T(8,128)(2,1)S(1)} %collective-permute-done.8.got, bf16[1536,2048]{1,0:T(8,128)(2,1)S(1)} %bitcast.17), custom_call_target="tpu_custom_call" | custom-call | tf_op jit(solution)/shard_map/pallas_call | solution.py:192
  (25 shorter events, 0.3 us)
Async XLA Ops:
  3.1 1.6 %collective-permute-start = (f32[2,96,256]{2,1,0:T(8,128)S(1)}, f32[2,96,256]{2,1,0:T(8,128)S(1)}, u32[]{:S(2)}, u32[]{:S(2)}) collective-permute-start(f32[2,96,256]{2,1,0:T(8,128)S(1)} %get-tuple-element.10), channel_id=1, source_target_pairs={{0,2},{1,3},{2,0},{3,1},{4,6},{5,7},{6,4},{7,5},{8,10},{9,11},{10,... | collective-permute-start | bytes 589832 | tf_op jit(solution)/shard_map/ppermute | solution.py:51
  5.0 5.1 %collective-permute-start.3 = (f16[98,256]{1,0:T(8,128)(2,1)S(1)}, f16[98,256]{1,0:T(8,128)(2,1)S(1)}, u32[]{:S(2)}, u32[]{:S(2)}) collective-permute-start(f16[98,256]{1,0:T(8,128)(2,1)S(1)} %get-tuple-element.28), channel_id=1, source_target_pairs={{0,8},{1,9},{2,10},{3,11},{4,12},{5,13},{6,14},{7,15},{8,0},{9,1},... | collective-permute-start | bytes 150536 | tf_op jit(solution)/shard_map/ppermute | solution.py:51
  8.0 4.1 %collective-permute-start.2 = (f16[98,256]{1,0:T(8,128)(2,1)S(1)}, f16[98,256]{1,0:T(8,128)(2,1)S(1)}, u32[]{:S(2)}, u32[]{:S(2)}) collective-permute-start(f16[98,256]{1,0:T(8,128)(2,1)S(1)} %get-tuple-element.27), channel_id=1, source_target_pairs={{0,6},{1,7},{2,4},{3,5},{4,2},{5,3},{6,0},{7,1},{8,14},{9,15},{10,... | collective-permute-start | bytes 150536 | tf_op jit(solution)/shard_map/ppermute | solution.py:51
  8.9 4.5 %collective-permute-start.1 = (f16[98,256]{1,0:T(8,128)(2,1)S(1)}, f16[98,256]{1,0:T(8,128)(2,1)S(1)}, u32[]{:S(2)}, u32[]{:S(2)}) collective-permute-start(f16[98,256]{1,0:T(8,128)(2,1)S(1)} %get-tuple-element.27), channel_id=1, source_target_pairs={{0,14},{1,15},{2,12},{3,13},{4,10},{5,11},{6,8},{7,9},{8,6},{9,7},... | collective-permute-start | bytes 150536 | tf_op jit(solution)/shard_map/ppermute | solution.py:51
  13.8 6.3 %collective-permute-start.4 = (f16[98,256]{1,0:T(8,128)(2,1)S(1)}, f16[98,256]{1,0:T(8,128)(2,1)S(1)}, u32[]{:S(2)}, u32[]{:S(2)}) collective-permute-start(f16[98,256]{1,0:T(8,128)(2,1)S(1)} %select_convert_fusion), channel_id=1, source_target_pairs={{0,18},{1,19},{2,16},{3,17},{4,22},{5,23},{6,20},{7,21},{8,26},{9,... | collective-permute-start | bytes 150536 | tf_op jit(solution)/shard_map/ppermute | solution.py:51
  16.7 0.8 %copy-start = (f32[64,64]{1,0:T(8,128)S(1)}, f32[64,64]{1,0:T(8,128)}, u32[]{:S(2)}) copy-start(f32[64,64]{1,0:T(8,128)} %out_inverse.1) | copy-start | bytes 49156
  17.4 0.7 %copy-start.1 = (f32[32,32]{1,0:T(8,128)S(1)}, f32[32,32]{1,0:T(8,128)}, u32[]{:S(2)}) copy-start(f32[32,32]{1,0:T(8,128)} %in_inverse.1) | copy-start | bytes 12292
  18.2 9.4 %slice-start = ((s8[6291456]{0:T(1024)(128)(4,1)}), s8[4194304]{0:T(1024)(128)(4,1)S(1)}, s32[]{:S(2)}) async-start(s8[6291456]{0:T(1024)(128)(4,1)} %bitcast.16), calls=%async_computation | async-start | bytes 8388608
  20.2 7.4 %slice-start.1 = ((s8[6291456]{0:T(1024)(128)(4,1)}), s8[2097152]{0:T(1024)(128)(4,1)S(1)}, s32[]{:S(2)}) async-start(s8[6291456]{0:T(1024)(128)(4,1)} %bitcast.16), calls=%async_computation.1 | async-start | bytes 4194304
  20.8 4.4 %collective-permute-start.5 = (bf16[8,2048]{1,0:T(8,128)(2,1)S(1)}, bf16[8,2048]{1,0:T(8,128)(2,1)S(1)}, u32[]{:S(2)}, u32[]{:S(2)}) collective-permute-start(bf16[8,2048]{1,0:T(8,128)(2,1)S(1)} %shard_map.75), channel_id=1, source_target_pairs={{0,7},{1,6},{2,5},{3,4},{4,3},{5,2},{6,1},{7,0},{8,15},{9,14},{10,... | collective-permute-start | bytes 98312 | tf_op jit(solution)/shard_map/ppermute | solution.py:51
  22.1 4.0 %collective-permute-start.7 = (bf16[8,2048]{1,0:T(8,128)(2,1)S(1)}, bf16[8,2048]{1,0:T(8,128)(2,1)S(1)}, u32[]{:S(2)}, u32[]{:S(2)}) collective-permute-start(bf16[8,2048]{1,0:T(8,128)(2,1)S(1)} %shard_map.75), channel_id=1, source_target_pairs={{0,1},{1,0},{2,3},{3,2},{4,5},{5,4},{6,7},{7,6},{8,9},{9,8},{10,11... | collective-permute-start | bytes 98312 | tf_op jit(solution)/shard_map/ppermute | solution.py:51
  22.5 3.4 %collective-permute-start.6 = (bf16[8,2048]{1,0:T(8,128)(2,1)S(1)}, bf16[8,2048]{1,0:T(8,128)(2,1)S(1)}, u32[]{:S(2)}, u32[]{:S(2)}) collective-permute-start(bf16[8,2048]{1,0:T(8,128)(2,1)S(1)} %shard_map.75), channel_id=1, source_target_pairs={{0,6},{1,7},{2,4},{3,5},{4,2},{5,3},{6,0},{7,1},{8,14},{9,15},{10,... | collective-permute-start | bytes 98312 | tf_op jit(solution)/shard_map/ppermute | solution.py:51
  26.2 1.4 %collective-permute-start.8 = (bf16[32,2048]{1,0:T(8,128)(2,1)S(1)}, bf16[32,2048]{1,0:T(8,128)(2,1)S(1)}, u32[]{:S(2)}, u32[]{:S(2)}) collective-permute-start(bf16[32,2048]{1,0:T(8,128)(2,1)S(1)} %pad_add_fusion.held), channel_id=1, source_target_pairs={{0,2},{1,3},{2,0},{3,1},{4,6},{5,7},{6,4},{7,5},{8,10},{9,11},{10,... | collective-permute-start | bytes 393224 | tf_op jit(solution)/shard_map/ppermute | solution.py:51

commit v6 on v5

--- a/solution.py
+++ b/solution.py
@@ -71,8 +71,9 @@
             copy.start()
             copies.append(copy)
     for k in range(2 * slices):
-        copies[2 * k].wait()
-        copies[2 * k + 1].wait()
+        if k % slices == 0:
+            for copy in copies[2 * k : 2 * (k + slices)]:
+                copy.wait()
         out = given if k < slices else kept
         out[k % slices, :width_in] = contract(proj[:width_in], act_buf[k], 1, 1)
         out[k % slices, width_in:] = contract(proj[width_in:], grad_buf[k], 1, 1)
@@ -141,12 +142,11 @@
     tokens = summed.shape[1]
     queries, columns = out.shape
     lanes = spread_in.shape[1]
-    low = summed[...].T
-    in_high, in_low = two_parts(low[:, :width_in])
-    out_high, out_low = two_parts(low[:, width_in:])
-    side_in = jnp.concatenate([in_high, in_high, in_low, in_low], axis=1)
-    side_out = jnp.concatenate([out_high, out_high, out_low, out_low], axis=1)
-    spread_in_low = contract(side_in, spread_in[...], 1, 0)
+    in_high, in_low = two_parts(summed[:width_in])
+    out_high, out_low = two_parts(summed[width_in:])
+    side_in = jnp.concatenate([in_high, in_high, in_low, in_low], axis=0)
+    side_out = jnp.concatenate([out_high, out_high, out_low, out_low], axis=0).T
+    spread_in_low = contract(side_in, spread_in[...], 0, 0)
     step = math.gcd(columns, 256)
     wide = jnp.concatenate([spread_in_low] * (step // lanes), axis=1)
     for start in range(0, columns, step):

time: 30.4 us -> 30.2 us (level)
  no operation moved by 1% of the time
where the time goes in v6:
time: 30.2 us; the launch traced here: 29.9 us
  starting transfers between devices  10.9 us (36%)
  waiting for transfers between devices  10.1 us (33%)
  Pallas kernels  5.55 us (18%)
  other arithmetic  1.59 us (5%)
  local copies, waits for them, and re-layouts  1.52 us (5%)
    ppermute x9, starting transfers between devices, swap(): return lax.ppermute(value, axes, pairs)  10.9 us
    ppermute x9, waiting for transfers between devices, swap(): return lax.ppermute(value, axes, pairs)  10.1 us
    pallas_call x1, Pallas kernels, scores(): pl.pallas_call(functools.partial(score_kernel, order, wide), out_shape=ja...  2.54 us
    pallas_call x1, Pallas kernels, project(): pl.pallas_call(functools.partial(project_kernel, width_in), out_shape=(ou...  2.14 us
    unnamed x8, local copies, waits for them, and re-layouts  1.49 us
    concatenate x1, other arithmetic, on_device(): proj = jnp.concatenate([in_projection.T, out_projection.T], axis=0)  0.85 us
  transfers between devices with their start and end apart: 9, of which 9 were waited for; matrix products, arithmetic and copies ran while one was open for 0% of the time, Pallas kernels for 1%

profile of v6, /device:TPU:0, one launch (start us, length us, event | category | flops | bytes accessed | tf_op | source)
XLA Modules:
  0.0 29.9 jit_solution(14520299628188683988)
XLA Ops:
  0.0 0.8 %pad_maximum_fusion.proj = bf16[96,512]{1,0:T(8,128)(2,1)S(1)} fusion(bf16[64,512]{1,0:T(8,128)(2,1)} %bitcast.18, bf16[32,512]{1,0:T(8,128)(2,1)} %bitcast.19), kind=kLoop, calls=%fused_computation.16 | loop fusion | flops 196608 | bytes 196608 | tf_op jit(solution)/shard_map/concatenate | solution.py:236
  0.8 2.1 %shard_map.73 = (f32[2,96,256]{2,1,0:T(8,128)S(1)}, f32[2,96,256]{2,1,0:T(8,128)S(1)}) custom-call(bf16[1024,512]{1,0:T(8,128)(2,1)} %acts.1, bf16[1024,512]{1,0:T(8,128)(2,1)} %grads.1, bf16[96,512]{1,0:T(8,128)(2,1)S(1)} %pad_maximum_fusion.proj), custom_call_target="tpu_custom_call" | custom-call | flops 100663296 | bytes 2097152 | tf_op jit(solution)/shard_map/pallas_call | solution.py:86
  3.0 0.5 %collective-permute-start = (f32[2,96,256]{2,1,0:T(8,128)S(1)}, f32[2,96,256]{2,1,0:T(8,128)S(1)}, u32[]{:S(2)}, u32[]{:S(2)}) collective-permute-start(f32[2,96,256]{2,1,0:T(8,128)S(1)} %get-tuple-element.10), channel_id=1, source_target_pairs={{0,2},{1,3},{2,0},{3,1},{4,6},{5,7},{6,4},{7,5},{8,10},{9,11},{10,... | collective-permute-start | bytes 589832 | tf_op jit(solution)/shard_map/ppermute | solution.py:51
  3.5 1.1 %collective-permute-done = f32[2,96,256]{2,1,0:T(8,128)S(1)} collective-permute-done((f32[2,96,256]{2,1,0:T(8,128)S(1)}, f32[2,96,256]{2,1,0:T(8,128)S(1)}, u32[]{:S(2)}, u32[]{:S(2)}) %collective-permute-start) | collective-permute-done | bytes 196640 | tf_op jit(solution)/shard_map/ppermute | solution.py:51
  4.7 0.1 select_convert_fusion.2
  4.9 3.0 %collective-permute-start.3 = (f16[98,256]{1,0:T(8,128)(2,1)S(1)}, f16[98,256]{1,0:T(8,128)(2,1)S(1)}, u32[]{:S(2)}, u32[]{:S(2)}) collective-permute-start(f16[98,256]{1,0:T(8,128)(2,1)S(1)} %get-tuple-element.28), channel_id=1, source_target_pairs={{0,8},{1,9},{2,10},{3,11},{4,12},{5,13},{6,14},{7,15},{8,0},{9,1},... | collective-permute-start | bytes 150536 | tf_op jit(solution)/shard_map/ppermute | solution.py:51
  7.9 1.0 %collective-permute-start.2 = (f16[98,256]{1,0:T(8,128)(2,1)S(1)}, f16[98,256]{1,0:T(8,128)(2,1)S(1)}, u32[]{:S(2)}, u32[]{:S(2)}) collective-permute-start(f16[98,256]{1,0:T(8,128)(2,1)S(1)} %get-tuple-element.27), channel_id=1, source_target_pairs={{0,6},{1,7},{2,4},{3,5},{4,2},{5,3},{6,0},{7,1},{8,14},{9,15},{10,... | collective-permute-start | bytes 150536 | tf_op jit(solution)/shard_map/ppermute | solution.py:51
  8.8 0.3 %collective-permute-start.1 = (f16[98,256]{1,0:T(8,128)(2,1)S(1)}, f16[98,256]{1,0:T(8,128)(2,1)S(1)}, u32[]{:S(2)}, u32[]{:S(2)}) collective-permute-start(f16[98,256]{1,0:T(8,128)(2,1)S(1)} %get-tuple-element.27), channel_id=1, source_target_pairs={{0,14},{1,15},{2,12},{3,13},{4,10},{5,11},{6,8},{7,9},{8,6},{9,7},... | collective-permute-start | bytes 150536 | tf_op jit(solution)/shard_map/ppermute | solution.py:51
  9.2 0.9 %collective-permute-done.3 = f16[98,256]{1,0:T(8,128)(2,1)S(1)} collective-permute-done((f16[98,256]{1,0:T(8,128)(2,1)S(1)}, f16[98,256]{1,0:T(8,128)(2,1)S(1)}, u32[]{:S(2)}, u32[]{:S(2)}) %collective-permute-start.3) | collective-permute-done | bytes 50208 | tf_op jit(solution)/shard_map/ppermute | solution.py:51
  10.0 1.9 %collective-permute-done.2 = f16[98,256]{1,0:T(8,128)(2,1)S(1)} collective-permute-done((f16[98,256]{1,0:T(8,128)(2,1)S(1)}, f16[98,256]{1,0:T(8,128)(2,1)S(1)}, u32[]{:S(2)}, u32[]{:S(2)}) %collective-permute-start.2) | collective-permute-done | bytes 50208 | tf_op jit(solution)/shard_map/ppermute | solution.py:51
  12.0 1.3 %collective-permute-done.1 = f16[98,256]{1,0:T(8,128)(2,1)S(1)} collective-permute-done((f16[98,256]{1,0:T(8,128)(2,1)S(1)}, f16[98,256]{1,0:T(8,128)(2,1)S(1)}, u32[]{:S(2)}, u32[]{:S(2)}) %collective-permute-start.1) | collective-permute-done | bytes 50208 | tf_op jit(solution)/shard_map/ppermute | solution.py:51
  13.3 0.1 fusion.1
  13.5 0.1 select_convert_fusion
  13.7 2.9 %collective-permute-start.4 = (f16[98,256]{1,0:T(8,128)(2,1)S(1)}, f16[98,256]{1,0:T(8,128)(2,1)S(1)}, u32[]{:S(2)}, u32[]{:S(2)}) collective-permute-start(f16[98,256]{1,0:T(8,128)(2,1)S(1)} %select_convert_fusion), channel_id=1, source_target_pairs={{0,18},{1,19},{2,16},{3,17},{4,22},{5,23},{6,20},{7,21},{8,26},{9,... | collective-permute-start | bytes 150536 | tf_op jit(solution)/shard_map/ppermute | solution.py:51
  16.6 0.0 copy-start
  16.6 0.8 %copy-done = f32[64,64]{1,0:T(8,128)S(1)} copy-done((f32[64,64]{1,0:T(8,128)S(1)}, f32[64,64]{1,0:T(8,128)}, u32[]{:S(2)}) %copy-start) | copy-done | bytes 16408
  17.3 0.0 copy-start.1
  17.3 0.7 %copy-done.1 = f32[32,32]{1,0:T(8,128)S(1)} copy-done((f32[32,32]{1,0:T(8,128)S(1)}, f32[32,32]{1,0:T(8,128)}, u32[]{:S(2)}) %copy-start.1) | copy-done | bytes 4120
  18.1 0.0 slice-start
  18.1 0.4 %shard_map.74 = (bf16[256,2048]{1,0:T(8,128)(2,1)S(1)}, bf16[128,128]{1,0:T(8,128)(2,1)S(1)}) custom-call(f32[32,32]{1,0:T(8,128)S(1)} %copy-done.1, f32[64,64]{1,0:T(8,128)S(1)} %copy-done), custom_call_target="tpu_custom_call" | custom-call | flops 8589934592 | bytes 16777216 | tf_op jit(solution)/shard_map/pallas_call | solution.py:127
  18.4 1.5 %collective-permute-done.4 = f16[98,256]{1,0:T(8,128)(2,1)S(1)} collective-permute-done((f16[98,256]{1,0:T(8,128)(2,1)S(1)}, f16[98,256]{1,0:T(8,128)(2,1)S(1)}, u32[]{:S(2)}, u32[]{:S(2)}) %collective-permute-start.4) | collective-permute-done | bytes 50208 | tf_op jit(solution)/shard_map/ppermute | solution.py:51
  20.0 0.1 fusion.summed
  20.1 0.0 slice-start.1
  20.1 0.5 %shard_map.75 = bf16[8,2048]{1,0:T(8,128)(2,1)S(1)} custom-call(f32[96,256]{1,0:T(8,128)S(1)} %fusion.summed, bf16[256,2048]{1,0:T(8,128)(2,1)S(1)} %get-tuple-element.11.spread_out, bf16[128,128]{1,0:T(8,128)(2,1)S(1)} %get-tuple-element.12.spread_in), custom_call_target="tpu_custom_call" | custom-call | flops 8589934592 | bytes 16777216 | tf_op jit(solution)/shard_map/pallas_call | solution.py:160
  20.6 1.3 %collective-permute-start.5 = (bf16[8,2048]{1,0:T(8,128)(2,1)S(1)}, bf16[8,2048]{1,0:T(8,128)(2,1)S(1)}, u32[]{:S(2)}, u32[]{:S(2)}) collective-permute-start(bf16[8,2048]{1,0:T(8,128)(2,1)S(1)} %shard_map.75), channel_id=1, source_target_pairs={{0,7},{1,6},{2,5},{3,4},{4,3},{5,2},{6,1},{7,0},{8,15},{9,14},{10,... | collective-permute-start | bytes 98312 | tf_op jit(solution)/shard_map/ppermute | solution.py:51
  21.9 0.4 %collective-permute-start.7 = (bf16[8,2048]{1,0:T(8,128)(2,1)S(1)}, bf16[8,2048]{1,0:T(8,128)(2,1)S(1)}, u32[]{:S(2)}, u32[]{:S(2)}) collective-permute-start(bf16[8,2048]{1,0:T(8,128)(2,1)S(1)} %shard_map.75), channel_id=1, source_target_pairs={{0,1},{1,0},{2,3},{3,2},{4,5},{5,4},{6,7},{7,6},{8,9},{9,8},{10,11... | collective-permute-start | bytes 98312 | tf_op jit(solution)/shard_map/ppermute | solution.py:51
  22.3 1.3 %collective-permute-start.6 = (bf16[8,2048]{1,0:T(8,128)(2,1)S(1)}, bf16[8,2048]{1,0:T(8,128)(2,1)S(1)}, u32[]{:S(2)}, u32[]{:S(2)}) collective-permute-start(bf16[8,2048]{1,0:T(8,128)(2,1)S(1)} %shard_map.75), channel_id=1, source_target_pairs={{0,6},{1,7},{2,4},{3,5},{4,2},{5,3},{6,0},{7,1},{8,14},{9,15},{10,... | collective-permute-start | bytes 98312 | tf_op jit(solution)/shard_map/ppermute | solution.py:51
  23.6 1.3 %collective-permute-done.5 = bf16[8,2048]{1,0:T(8,128)(2,1)S(1)} collective-permute-done((bf16[8,2048]{1,0:T(8,128)(2,1)S(1)}, bf16[8,2048]{1,0:T(8,128)(2,1)S(1)}, u32[]{:S(2)}, u32[]{:S(2)}) %collective-permute-start.5) | collective-permute-done | bytes 32800 | tf_op jit(solution)/shard_map/ppermute | solution.py:51
  25.0 0.7 %collective-permute-done.6 = bf16[8,2048]{1,0:T(8,128)(2,1)S(1)} collective-permute-done((bf16[8,2048]{1,0:T(8,128)(2,1)S(1)}, bf16[8,2048]{1,0:T(8,128)(2,1)S(1)}, u32[]{:S(2)}, u32[]{:S(2)}) %collective-permute-start.6) | collective-permute-done | bytes 32800 | tf_op jit(solution)/shard_map/ppermute | solution.py:51
  25.7 0.3 collective-permute-done.7
  26.0 0.2 collective-permute-start.8
  26.2 1.2 %collective-permute-done.8.got = bf16[32,2048]{1,0:T(8,128)(2,1)S(1)} collective-permute-done((bf16[32,2048]{1,0:T(8,128)(2,1)S(1)}, bf16[32,2048]{1,0:T(8,128)(2,1)S(1)}, u32[]{:S(2)}, u32[]{:S(2)}) %collective-permute-start.8) | collective-permute-done | bytes 131104 | tf_op jit(solution)/shard_map/ppermute | solution.py:51
  27.4 0.0 slice-done
  27.4 0.0 slice-done.1
  27.4 2.5 %shard_map.76 = f32[64,1536]{1,0:T(8,128)} custom-call(bf16[32,2048]{1,0:T(8,128)(2,1)S(1)} %pad_add_fusion.held, bf16[32,2048]{1,0:T(8,128)(2,1)S(1)} %collective-permute-done.8.got, bf16[1536,2048]{1,0:T(8,128)(2,1)S(1)} %bitcast.17), custom_call_target="tpu_custom_call" | custom-call | tf_op jit(solution)/shard_map/pallas_call | solution.py:192
  (25 shorter events, 0.3 us)
Async XLA Ops:
  3.0 1.6 %collective-permute-start = (f32[2,96,256]{2,1,0:T(8,128)S(1)}, f32[2,96,256]{2,1,0:T(8,128)S(1)}, u32[]{:S(2)}, u32[]{:S(2)}) collective-permute-start(f32[2,96,256]{2,1,0:T(8,128)S(1)} %get-tuple-element.10), channel_id=1, source_target_pairs={{0,2},{1,3},{2,0},{3,1},{4,6},{5,7},{6,4},{7,5},{8,10},{9,11},{10,... | collective-permute-start | bytes 589832 | tf_op jit(solution)/shard_map/ppermute | solution.py:51
  4.9 5.1 %collective-permute-start.3 = (f16[98,256]{1,0:T(8,128)(2,1)S(1)}, f16[98,256]{1,0:T(8,128)(2,1)S(1)}, u32[]{:S(2)}, u32[]{:S(2)}) collective-permute-start(f16[98,256]{1,0:T(8,128)(2,1)S(1)} %get-tuple-element.28), channel_id=1, source_target_pairs={{0,8},{1,9},{2,10},{3,11},{4,12},{5,13},{6,14},{7,15},{8,0},{9,1},... | collective-permute-start | bytes 150536 | tf_op jit(solution)/shard_map/ppermute | solution.py:51
  7.9 4.1 %collective-permute-start.2 = (f16[98,256]{1,0:T(8,128)(2,1)S(1)}, f16[98,256]{1,0:T(8,128)(2,1)S(1)}, u32[]{:S(2)}, u32[]{:S(2)}) collective-permute-start(f16[98,256]{1,0:T(8,128)(2,1)S(1)} %get-tuple-element.27), channel_id=1, source_target_pairs={{0,6},{1,7},{2,4},{3,5},{4,2},{5,3},{6,0},{7,1},{8,14},{9,15},{10,... | collective-permute-start | bytes 150536 | tf_op jit(solution)/shard_map/ppermute | solution.py:51
  8.8 4.5 %collective-permute-start.1 = (f16[98,256]{1,0:T(8,128)(2,1)S(1)}, f16[98,256]{1,0:T(8,128)(2,1)S(1)}, u32[]{:S(2)}, u32[]{:S(2)}) collective-permute-start(f16[98,256]{1,0:T(8,128)(2,1)S(1)} %get-tuple-element.27), channel_id=1, source_target_pairs={{0,14},{1,15},{2,12},{3,13},{4,10},{5,11},{6,8},{7,9},{8,6},{9,7},... | collective-permute-start | bytes 150536 | tf_op jit(solution)/shard_map/ppermute | solution.py:51
  13.7 6.3 %collective-permute-start.4 = (f16[98,256]{1,0:T(8,128)(2,1)S(1)}, f16[98,256]{1,0:T(8,128)(2,1)S(1)}, u32[]{:S(2)}, u32[]{:S(2)}) collective-permute-start(f16[98,256]{1,0:T(8,128)(2,1)S(1)} %select_convert_fusion), channel_id=1, source_target_pairs={{0,18},{1,19},{2,16},{3,17},{4,22},{5,23},{6,20},{7,21},{8,26},{9,... | collective-permute-start | bytes 150536 | tf_op jit(solution)/shard_map/ppermute | solution.py:51
  16.6 0.8 %copy-start = (f32[64,64]{1,0:T(8,128)S(1)}, f32[64,64]{1,0:T(8,128)}, u32[]{:S(2)}) copy-start(f32[64,64]{1,0:T(8,128)} %out_inverse.1) | copy-start | bytes 49156
  17.3 0.7 %copy-start.1 = (f32[32,32]{1,0:T(8,128)S(1)}, f32[32,32]{1,0:T(8,128)}, u32[]{:S(2)}) copy-start(f32[32,32]{1,0:T(8,128)} %in_inverse.1) | copy-start | bytes 12292
  18.1 9.3 %slice-start = ((s8[6291456]{0:T(1024)(128)(4,1)}), s8[4194304]{0:T(1024)(128)(4,1)S(1)}, s32[]{:S(2)}) async-start(s8[6291456]{0:T(1024)(128)(4,1)} %bitcast.16), calls=%async_computation | async-start | bytes 8388608
  20.1 7.3 %slice-start.1 = ((s8[6291456]{0:T(1024)(128)(4,1)}), s8[2097152]{0:T(1024)(128)(4,1)S(1)}, s32[]{:S(2)}) async-start(s8[6291456]{0:T(1024)(128)(4,1)} %bitcast.16), calls=%async_computation.1 | async-start | bytes 4194304
  20.6 4.4 %collective-permute-start.5 = (bf16[8,2048]{1,0:T(8,128)(2,1)S(1)}, bf16[8,2048]{1,0:T(8,128)(2,1)S(1)}, u32[]{:S(2)}, u32[]{:S(2)}) collective-permute-start(bf16[8,2048]{1,0:T(8,128)(2,1)S(1)} %shard_map.75), channel_id=1, source_target_pairs={{0,7},{1,6},{2,5},{3,4},{4,3},{5,2},{6,1},{7,0},{8,15},{9,14},{10,... | collective-permute-start | bytes 98312 | tf_op jit(solution)/shard_map/ppermute | solution.py:51
  21.9 4.1 %collective-permute-start.7 = (bf16[8,2048]{1,0:T(8,128)(2,1)S(1)}, bf16[8,2048]{1,0:T(8,128)(2,1)S(1)}, u32[]{:S(2)}, u32[]{:S(2)}) collective-permute-start(bf16[8,2048]{1,0:T(8,128)(2,1)S(1)} %shard_map.75), channel_id=1, source_target_pairs={{0,1},{1,0},{2,3},{3,2},{4,5},{5,4},{6,7},{7,6},{8,9},{9,8},{10,11... | collective-permute-start | bytes 98312 | tf_op jit(solution)/shard_map/ppermute | solution.py:51
  22.3 3.4 %collective-permute-start.6 = (bf16[8,2048]{1,0:T(8,128)(2,1)S(1)}, bf16[8,2048]{1,0:T(8,128)(2,1)S(1)}, u32[]{:S(2)}, u32[]{:S(2)}) collective-permute-start(bf16[8,2048]{1,0:T(8,128)(2,1)S(1)} %shard_map.75), channel_id=1, source_target_pairs={{0,6},{1,7},{2,4},{3,5},{4,2},{5,3},{6,0},{7,1},{8,14},{9,15},{10,... | collective-permute-start | bytes 98312 | tf_op jit(solution)/shard_map/ppermute | solution.py:51
  26.0 1.4 %collective-permute-start.8 = (bf16[32,2048]{1,0:T(8,128)(2,1)S(1)}, bf16[32,2048]{1,0:T(8,128)(2,1)S(1)}, u32[]{:S(2)}, u32[]{:S(2)}) collective-permute-start(bf16[32,2048]{1,0:T(8,128)(2,1)S(1)} %pad_add_fusion.held), channel_id=1, source_target_pairs={{0,2},{1,3},{2,0},{3,1},{4,6},{5,7},{6,4},{7,5},{8,10},{9,11},{10,... | collective-permute-start | bytes 393224 | tf_op jit(solution)/shard_map/ppermute | solution.py:51

commit v7 on v6

--- a/solution.py
+++ b/solution.py
@@ -167,9 +167,10 @@
     )(summed, spread_out, spread_in)
 
 
-def score_kernel(order, wide, held, got, store, out, part, sems):
+def score_kernel(order, wide, pieces, *refs):
     blk, x, half = lax.axis_index("blk"), lax.axis_index("wide") // 2, own_half()
-    queries = jnp.concatenate([held[...], got[...]], axis=0)
+    store, out, part, sems = refs[pieces:]
+    queries = jnp.concatenate([ref[...] for ref in refs[:pieces]], axis=0)
     rows = out.shape[0] // len(order)
     targets = [
         pl.multiple_of((((blk ^ far_blk) * (wide // 2) + (x ^ far_x)) * 2 + (half ^ flip)) * rows, rows)
@@ -190,21 +191,25 @@
 
 def scores(order, wide, held, got, store):
     return pl.pallas_call(
-        functools.partial(score_kernel, order, wide),
-        out_shape=jax.ShapeDtypeStruct((2 * held.shape[0], store.shape[0]), jnp.float32),
-        in_specs=[VMEM] * 3,
+        functools.partial(score_kernel, order, wide, len(held) + len(got)),
+        out_shape=jax.ShapeDtypeStruct((2 * sum(piece.shape[0] for piece in held), store.shape[0]), jnp.float32),
+        in_specs=[VMEM] * (len(held) + len(got) + 1),
         out_specs=HBM,
         scratch_shapes=[
-            pltpu.VMEM((2 * held.shape[0], store.shape[0]), jnp.float32),
+            pltpu.VMEM((2 * sum(piece.shape[0] for piece in held), store.shape[0]), jnp.float32),
             pltpu.SemaphoreType.DMA((store.shape[0] // math.gcd(store.shape[0], 512),)),
         ],
         compiler_params=pltpu.CompilerParams(vmem_limit_bytes=20 * MIB),
-    )(held, got, store)
+    )(*held, *got, store)
 
 
 def pad_rows(piece, place, places):
     rows, zero = piece.shape[0], jnp.zeros((), piece.dtype)
     return lax.pad(piece, zero, ((place * rows, (places - 1 - place) * rows, 0), (0, 0, 0)))
+
+
+def stack(pieces):
+    return sum(pad_rows(piece, n, len(pieces)) for n, piece in enumerate(pieces))
 
 
 def encode(value, width_in):
@@ -255,12 +260,16 @@
         bit *= 2
     near = [(b, x) for x in range(slices) for b in range(min(blocks, 2))]
     others = [exchange(queries, sizes, blk=b, wide=x) for b, x in near[:0:-1]]
-    queries = pad_rows(queries, 0, len(near))
-    for n, other in zip(range(len(near) - 1, 0, -1), others):
-        queries = lax.optimization_barrier(queries + pad_rows(other, n, len(near)))
-    order = [(b ^ c, x ^ y) for c, y in near for b, x in order]
-    order = tuple((b, x, flip) for flip in range(2) for b, x in order)
-    return scores(order, wide, queries, swap(queries, sizes, {"wide": 1}), grad_store)
+    pieces, passed, orders = [queries], [], [order]
+    for (c, y), other in zip(near[:0:-1], others):
+        pieces.append(other)
+        orders.append([(b ^ c, x ^ y) for b, x in order])
+    early = lax.optimization_barrier(stack(pieces[:2]))
+    late = stack(pieces[2:]) if pieces[2:] else None
+    held = [early] + ([late] if pieces[2:] else [])
+    passed = [swap(piece, sizes, {"wide": 1}) for piece in held]
+    order = tuple((b, x, flip) for flip in range(2) for part in orders for b, x in part)
+    return scores(order, wide, held, passed, grad_store)
 
 
 def solution(mesh):

time: 30.2 us -> 30.1 us (level)
    ppermute x9 -> x10, waiting for transfers between devices: 10.1 us -> 10 us  [swap(): return lax.ppermute(value, axes, pairs)]
    ppermute x9 -> x10, starting transfers between devices: 10.9 us -> 11 us  [swap(): return lax.ppermute(value, axes, pairs)]
  transfers between devices with their start and end apart: 9 -> 10, of which waited for: 9 -> 9; matrix products, arithmetic and copies ran while one was open for 0% -> 0% of each run, Pallas kernels for 1% -> 1%
where the time goes in v7:
time: 30.1 us; the launch traced here: 29.8 us
  starting transfers between devices  11 us (37%)
  waiting for transfers between devices  10 us (33%)
  Pallas kernels  5.55 us (18%)
  other arithmetic  1.56 us (5%)
  local copies, waits for them, and re-layouts  1.52 us (5%)
    ppermute x10, starting transfers between devices, swap(): return lax.ppermute(value, axes, pairs)  11 us
    ppermute x10, waiting for transfers between devices, swap(): return lax.ppermute(value, axes, pairs)  10 us
    pallas_call x1, Pallas kernels, scores(): pl.pallas_call(functools.partial(score_kernel, order, wide, len(held) + l...  2.55 us
    pallas_call x1, Pallas kernels, project(): pl.pallas_call(functools.partial(project_kernel, width_in), out_shape=(ou...  2.14 us
    unnamed x8, local copies, waits for them, and re-layouts  1.49 us
    concatenate x1, other arithmetic, on_device(): proj = jnp.concatenate([in_projection.T, out_projection.T], axis=0)  0.85 us
  transfers between devices with their start and end apart: 10, of which 9 were waited for; matrix products, arithmetic and copies ran while one was open for 0% of the time, Pallas kernels for 1%

profile of v7, /device:TPU:0, one launch (start us, length us, event | category | flops | bytes accessed | tf_op | source)
XLA Modules:
  0.0 29.8 jit_solution(8687440435224127106)
XLA Ops:
  0.0 0.8 %pad_maximum_fusion.proj = bf16[96,512]{1,0:T(8,128)(2,1)S(1)} fusion(bf16[64,512]{1,0:T(8,128)(2,1)} %bitcast.18, bf16[32,512]{1,0:T(8,128)(2,1)} %bitcast.19), kind=kLoop, calls=%fused_computation.13 | loop fusion | flops 196608 | bytes 196608 | tf_op jit(solution)/shard_map/concatenate | solution.py:241
  0.8 2.1 %shard_map.73 = (f32[2,96,256]{2,1,0:T(8,128)S(1)}, f32[2,96,256]{2,1,0:T(8,128)S(1)}) custom-call(bf16[1024,512]{1,0:T(8,128)(2,1)} %acts.1, bf16[1024,512]{1,0:T(8,128)(2,1)} %grads.1, bf16[96,512]{1,0:T(8,128)(2,1)S(1)} %pad_maximum_fusion.proj), custom_call_target="tpu_custom_call" | custom-call | flops 100663296 | bytes 2097152 | tf_op jit(solution)/shard_map/pallas_call | solution.py:86
  3.0 0.5 %collective-permute-start = (f32[2,96,256]{2,1,0:T(8,128)S(1)}, f32[2,96,256]{2,1,0:T(8,128)S(1)}, u32[]{:S(2)}, u32[]{:S(2)}) collective-permute-start(f32[2,96,256]{2,1,0:T(8,128)S(1)} %get-tuple-element.10), channel_id=1, source_target_pairs={{0,2},{1,3},{2,0},{3,1},{4,6},{5,7},{6,4},{7,5},{8,10},{9,11},{10,... | collective-permute-start | bytes 589832 | tf_op jit(solution)/shard_map/ppermute | solution.py:51
  3.5 1.1 %collective-permute-done = f32[2,96,256]{2,1,0:T(8,128)S(1)} collective-permute-done((f32[2,96,256]{2,1,0:T(8,128)S(1)}, f32[2,96,256]{2,1,0:T(8,128)S(1)}, u32[]{:S(2)}, u32[]{:S(2)}) %collective-permute-start) | collective-permute-done | bytes 196640 | tf_op jit(solution)/shard_map/ppermute | solution.py:51
  4.7 0.1 select_convert_fusion.2
  4.9 3.0 %collective-permute-start.3 = (f16[98,256]{1,0:T(8,128)(2,1)S(1)}, f16[98,256]{1,0:T(8,128)(2,1)S(1)}, u32[]{:S(2)}, u32[]{:S(2)}) collective-permute-start(f16[98,256]{1,0:T(8,128)(2,1)S(1)} %get-tuple-element.28), channel_id=1, source_target_pairs={{0,8},{1,9},{2,10},{3,11},{4,12},{5,13},{6,14},{7,15},{8,0},{9,1},... | collective-permute-start | bytes 150536 | tf_op jit(solution)/shard_map/ppermute | solution.py:51
  7.9 1.0 %collective-permute-start.2 = (f16[98,256]{1,0:T(8,128)(2,1)S(1)}, f16[98,256]{1,0:T(8,128)(2,1)S(1)}, u32[]{:S(2)}, u32[]{:S(2)}) collective-permute-start(f16[98,256]{1,0:T(8,128)(2,1)S(1)} %get-tuple-element.27), channel_id=1, source_target_pairs={{0,6},{1,7},{2,4},{3,5},{4,2},{5,3},{6,0},{7,1},{8,14},{9,15},{10,... | collective-permute-start | bytes 150536 | tf_op jit(solution)/shard_map/ppermute | solution.py:51
  8.8 0.3 %collective-permute-start.1 = (f16[98,256]{1,0:T(8,128)(2,1)S(1)}, f16[98,256]{1,0:T(8,128)(2,1)S(1)}, u32[]{:S(2)}, u32[]{:S(2)}) collective-permute-start(f16[98,256]{1,0:T(8,128)(2,1)S(1)} %get-tuple-element.27), channel_id=1, source_target_pairs={{0,14},{1,15},{2,12},{3,13},{4,10},{5,11},{6,8},{7,9},{8,6},{9,7},... | collective-permute-start | bytes 150536 | tf_op jit(solution)/shard_map/ppermute | solution.py:51
  9.2 0.9 %collective-permute-done.3 = f16[98,256]{1,0:T(8,128)(2,1)S(1)} collective-permute-done((f16[98,256]{1,0:T(8,128)(2,1)S(1)}, f16[98,256]{1,0:T(8,128)(2,1)S(1)}, u32[]{:S(2)}, u32[]{:S(2)}) %collective-permute-start.3) | collective-permute-done | bytes 50208 | tf_op jit(solution)/shard_map/ppermute | solution.py:51
  10.0 1.9 %collective-permute-done.2 = f16[98,256]{1,0:T(8,128)(2,1)S(1)} collective-permute-done((f16[98,256]{1,0:T(8,128)(2,1)S(1)}, f16[98,256]{1,0:T(8,128)(2,1)S(1)}, u32[]{:S(2)}, u32[]{:S(2)}) %collective-permute-start.2) | collective-permute-done | bytes 50208 | tf_op jit(solution)/shard_map/ppermute | solution.py:51
  12.0 1.3 %collective-permute-done.1 = f16[98,256]{1,0:T(8,128)(2,1)S(1)} collective-permute-done((f16[98,256]{1,0:T(8,128)(2,1)S(1)}, f16[98,256]{1,0:T(8,128)(2,1)S(1)}, u32[]{:S(2)}, u32[]{:S(2)}) %collective-permute-start.1) | collective-permute-done | bytes 50208 | tf_op jit(solution)/shard_map/ppermute | solution.py:51
  13.3 0.1 fusion.1
  13.5 0.1 select_convert_fusion
  13.7 2.9 %collective-permute-start.4 = (f16[98,256]{1,0:T(8,128)(2,1)S(1)}, f16[98,256]{1,0:T(8,128)(2,1)S(1)}, u32[]{:S(2)}, u32[]{:S(2)}) collective-permute-start(f16[98,256]{1,0:T(8,128)(2,1)S(1)} %select_convert_fusion), channel_id=1, source_target_pairs={{0,18},{1,19},{2,16},{3,17},{4,22},{5,23},{6,20},{7,21},{8,26},{9,... | collective-permute-start | bytes 150536 | tf_op jit(solution)/shard_map/ppermute | solution.py:51
  16.6 0.0 copy-start
  16.6 0.8 %copy-done = f32[64,64]{1,0:T(8,128)S(1)} copy-done((f32[64,64]{1,0:T(8,128)S(1)}, f32[64,64]{1,0:T(8,128)}, u32[]{:S(2)}) %copy-start) | copy-done | bytes 16408
  17.3 0.0 copy-start.1
  17.3 0.7 %copy-done.1 = f32[32,32]{1,0:T(8,128)S(1)} copy-done((f32[32,32]{1,0:T(8,128)S(1)}, f32[32,32]{1,0:T(8,128)}, u32[]{:S(2)}) %copy-start.1) | copy-done | bytes 4120
  18.1 0.0 slice-start
  18.1 0.4 %shard_map.74 = (bf16[256,2048]{1,0:T(8,128)(2,1)S(1)}, bf16[128,128]{1,0:T(8,128)(2,1)S(1)}) custom-call(f32[32,32]{1,0:T(8,128)S(1)} %copy-done.1, f32[64,64]{1,0:T(8,128)S(1)} %copy-done), custom_call_target="tpu_custom_call" | custom-call | flops 8589934592 | bytes 16777216 | tf_op jit(solution)/shard_map/pallas_call | solution.py:127
  18.4 1.5 %collective-permute-done.4 = f16[98,256]{1,0:T(8,128)(2,1)S(1)} collective-permute-done((f16[98,256]{1,0:T(8,128)(2,1)S(1)}, f16[98,256]{1,0:T(8,128)(2,1)S(1)}, u32[]{:S(2)}, u32[]{:S(2)}) %collective-permute-start.4) | collective-permute-done | bytes 50208 | tf_op jit(solution)/shard_map/ppermute | solution.py:51
  20.0 0.0 slice-start.1
  20.0 0.1 fusion.summed
  20.1 0.5 %shard_map.75 = bf16[8,2048]{1,0:T(8,128)(2,1)S(1)} custom-call(f32[96,256]{1,0:T(8,128)S(1)} %fusion.summed, bf16[256,2048]{1,0:T(8,128)(2,1)S(1)} %get-tuple-element.11.spread_out, bf16[128,128]{1,0:T(8,128)(2,1)S(1)} %get-tuple-element.12.spread_in), custom_call_target="tpu_custom_call" | custom-call | flops 8589934592 | bytes 16777216 | tf_op jit(solution)/shard_map/pallas_call | solution.py:160
  20.6 1.3 %collective-permute-start.5 = (bf16[8,2048]{1,0:T(8,128)(2,1)S(1)}, bf16[8,2048]{1,0:T(8,128)(2,1)S(1)}, u32[]{:S(2)}, u32[]{:S(2)}) collective-permute-start(bf16[8,2048]{1,0:T(8,128)(2,1)S(1)} %shard_map.75), channel_id=1, source_target_pairs={{0,7},{1,6},{2,5},{3,4},{4,3},{5,2},{6,1},{7,0},{8,15},{9,14},{10,... | collective-permute-start | bytes 98312 | tf_op jit(solution)/shard_map/ppermute | solution.py:51
  21.9 0.4 %collective-permute-start.7 = (bf16[8,2048]{1,0:T(8,128)(2,1)S(1)}, bf16[8,2048]{1,0:T(8,128)(2,1)S(1)}, u32[]{:S(2)}, u32[]{:S(2)}) collective-permute-start(bf16[8,2048]{1,0:T(8,128)(2,1)S(1)} %shard_map.75), channel_id=1, source_target_pairs={{0,1},{1,0},{2,3},{3,2},{4,5},{5,4},{6,7},{7,6},{8,9},{9,8},{10,11... | collective-permute-start | bytes 98312 | tf_op jit(solution)/shard_map/ppermute | solution.py:51
  22.3 1.3 %collective-permute-start.6 = (bf16[8,2048]{1,0:T(8,128)(2,1)S(1)}, bf16[8,2048]{1,0:T(8,128)(2,1)S(1)}, u32[]{:S(2)}, u32[]{:S(2)}) collective-permute-start(bf16[8,2048]{1,0:T(8,128)(2,1)S(1)} %shard_map.75), channel_id=1, source_target_pairs={{0,6},{1,7},{2,4},{3,5},{4,2},{5,3},{6,0},{7,1},{8,14},{9,15},{10,... | collective-permute-start | bytes 98312 | tf_op jit(solution)/shard_map/ppermute | solution.py:51
  23.6 1.3 %collective-permute-done.5 = bf16[8,2048]{1,0:T(8,128)(2,1)S(1)} collective-permute-done((bf16[8,2048]{1,0:T(8,128)(2,1)S(1)}, bf16[8,2048]{1,0:T(8,128)(2,1)S(1)}, u32[]{:S(2)}, u32[]{:S(2)}) %collective-permute-start.5) | collective-permute-done | bytes 32800 | tf_op jit(solution)/shard_map/ppermute | solution.py:51
  25.0 0.1 collective-permute-start.8
  25.1 0.8 %collective-permute-done.7 = bf16[8,2048]{1,0:T(8,128)(2,1)S(1)} collective-permute-done((bf16[8,2048]{1,0:T(8,128)(2,1)S(1)}, bf16[8,2048]{1,0:T(8,128)(2,1)S(1)}, u32[]{:S(2)}, u32[]{:S(2)}) %collective-permute-start.7) | collective-permute-done | bytes 32800 | tf_op jit(solution)/shard_map/ppermute | solution.py:51
  25.9 0.0 collective-permute-done.6
  26.0 0.1 collective-permute-start.9
  26.1 0.1 collective-permute-done.8.refs_2_
  26.2 1.1 %collective-permute-done.9.refs_3_ = bf16[16,2048]{1,0:T(8,128)(2,1)S(1)} collective-permute-done((bf16[16,2048]{1,0:T(8,128)(2,1)S(1)}, bf16[16,2048]{1,0:T(8,128)(2,1)S(1)}, u32[]{:S(2)}, u32[]{:S(2)}) %collective-permute-start.9) | collective-permute-done | bytes 65568 | tf_op jit(solution)/shard_map/ppermute | solution.py:51
  27.3 0.0 slice-done
  27.3 0.0 slice-done.1
  27.3 2.5 %shard_map.76 = f32[64,1536]{1,0:T(8,128)} custom-call(bf16[16,2048]{1,0:T(8,128)(2,1)S(1)} %pad_add_fusion.1.refs_0_, bf16[16,2048]{1,0:T(8,128)(2,1)S(1)} %pad_add_fusion.refs_1_, bf16[16,2048]{1,0:T(8,128)(2,1)S(1)} %collective-permute-done.8.refs_2_, bf16[16,2048]{1,0:T(8,128)(2,1)S(1)} %collective-permute-done.9.refs_3_, bf16[1536,2048]{1,0:T(8,128)(2,1)S(1)} %bitcast.17), custom_call_target="tpu_custom_call" | custom-call | tf_op jit(solution)/shard_map/pallas_call | solution.py:193
  (24 shorter events, 0.2 us)
Async XLA Ops:
  3.0 1.6 %collective-permute-start = (f32[2,96,256]{2,1,0:T(8,128)S(1)}, f32[2,96,256]{2,1,0:T(8,128)S(1)}, u32[]{:S(2)}, u32[]{:S(2)}) collective-permute-start(f32[2,96,256]{2,1,0:T(8,128)S(1)} %get-tuple-element.10), channel_id=1, source_target_pairs={{0,2},{1,3},{2,0},{3,1},{4,6},{5,7},{6,4},{7,5},{8,10},{9,11},{10,... | collective-permute-start | bytes 589832 | tf_op jit(solution)/shard_map/ppermute | solution.py:51
  4.9 5.1 %collective-permute-start.3 = (f16[98,256]{1,0:T(8,128)(2,1)S(1)}, f16[98,256]{1,0:T(8,128)(2,1)S(1)}, u32[]{:S(2)}, u32[]{:S(2)}) collective-permute-start(f16[98,256]{1,0:T(8,128)(2,1)S(1)} %get-tuple-element.28), channel_id=1, source_target_pairs={{0,8},{1,9},{2,10},{3,11},{4,12},{5,13},{6,14},{7,15},{8,0},{9,1},... | collective-permute-start | bytes 150536 | tf_op jit(solution)/shard_map/ppermute | solution.py:51
  7.9 4.1 %collective-permute-start.2 = (f16[98,256]{1,0:T(8,128)(2,1)S(1)}, f16[98,256]{1,0:T(8,128)(2,1)S(1)}, u32[]{:S(2)}, u32[]{:S(2)}) collective-permute-start(f16[98,256]{1,0:T(8,128)(2,1)S(1)} %get-tuple-element.27), channel_id=1, source_target_pairs={{0,6},{1,7},{2,4},{3,5},{4,2},{5,3},{6,0},{7,1},{8,14},{9,15},{10,... | collective-permute-start | bytes 150536 | tf_op jit(solution)/shard_map/ppermute | solution.py:51
  8.8 4.5 %collective-permute-start.1 = (f16[98,256]{1,0:T(8,128)(2,1)S(1)}, f16[98,256]{1,0:T(8,128)(2,1)S(1)}, u32[]{:S(2)}, u32[]{:S(2)}) collective-permute-start(f16[98,256]{1,0:T(8,128)(2,1)S(1)} %get-tuple-element.27), channel_id=1, source_target_pairs={{0,14},{1,15},{2,12},{3,13},{4,10},{5,11},{6,8},{7,9},{8,6},{9,7},... | collective-permute-start | bytes 150536 | tf_op jit(solution)/shard_map/ppermute | solution.py:51
  13.7 6.3 %collective-permute-start.4 = (f16[98,256]{1,0:T(8,128)(2,1)S(1)}, f16[98,256]{1,0:T(8,128)(2,1)S(1)}, u32[]{:S(2)}, u32[]{:S(2)}) collective-permute-start(f16[98,256]{1,0:T(8,128)(2,1)S(1)} %select_convert_fusion), channel_id=1, source_target_pairs={{0,18},{1,19},{2,16},{3,17},{4,22},{5,23},{6,20},{7,21},{8,26},{9,... | collective-permute-start | bytes 150536 | tf_op jit(solution)/shard_map/ppermute | solution.py:51
  16.6 0.8 %copy-start = (f32[64,64]{1,0:T(8,128)S(1)}, f32[64,64]{1,0:T(8,128)}, u32[]{:S(2)}) copy-start(f32[64,64]{1,0:T(8,128)} %out_inverse.1) | copy-start | bytes 49156
  17.3 0.7 %copy-start.1 = (f32[32,32]{1,0:T(8,128)S(1)}, f32[32,32]{1,0:T(8,128)}, u32[]{:S(2)}) copy-start(f32[32,32]{1,0:T(8,128)} %in_inverse.1) | copy-start | bytes 12292
  18.1 9.2 %slice-start = ((s8[6291456]{0:T(1024)(128)(4,1)}), s8[4194304]{0:T(1024)(128)(4,1)S(1)}, s32[]{:S(2)}) async-start(s8[6291456]{0:T(1024)(128)(4,1)} %bitcast.16), calls=%async_computation | async-start | bytes 8388608
  20.0 7.3 %slice-start.1 = ((s8[6291456]{0:T(1024)(128)(4,1)}), s8[2097152]{0:T(1024)(128)(4,1)S(1)}, s32[]{:S(2)}) async-start(s8[6291456]{0:T(1024)(128)(4,1)} %bitcast.16), calls=%async_computation.1 | async-start | bytes 4194304
  20.6 4.4 %collective-permute-start.5 = (bf16[8,2048]{1,0:T(8,128)(2,1)S(1)}, bf16[8,2048]{1,0:T(8,128)(2,1)S(1)}, u32[]{:S(2)}, u32[]{:S(2)}) collective-permute-start(bf16[8,2048]{1,0:T(8,128)(2,1)S(1)} %shard_map.75), channel_id=1, source_target_pairs={{0,7},{1,6},{2,5},{3,4},{4,3},{5,2},{6,1},{7,0},{8,15},{9,14},{10,... | collective-permute-start | bytes 98312 | tf_op jit(solution)/shard_map/ppermute | solution.py:51
  21.9 4.1 %collective-permute-start.7 = (bf16[8,2048]{1,0:T(8,128)(2,1)S(1)}, bf16[8,2048]{1,0:T(8,128)(2,1)S(1)}, u32[]{:S(2)}, u32[]{:S(2)}) collective-permute-start(bf16[8,2048]{1,0:T(8,128)(2,1)S(1)} %shard_map.75), channel_id=1, source_target_pairs={{0,1},{1,0},{2,3},{3,2},{4,5},{5,4},{6,7},{7,6},{8,9},{9,8},{10,11... | collective-permute-start | bytes 98312 | tf_op jit(solution)/shard_map/ppermute | solution.py:51
  22.3 3.6 %collective-permute-start.6 = (bf16[8,2048]{1,0:T(8,128)(2,1)S(1)}, bf16[8,2048]{1,0:T(8,128)(2,1)S(1)}, u32[]{:S(2)}, u32[]{:S(2)}) collective-permute-start(bf16[8,2048]{1,0:T(8,128)(2,1)S(1)} %shard_map.75), channel_id=1, source_target_pairs={{0,6},{1,7},{2,4},{3,5},{4,2},{5,3},{6,0},{7,1},{8,14},{9,15},{10,... | collective-permute-start | bytes 98312 | tf_op jit(solution)/shard_map/ppermute | solution.py:51
  25.0 1.3 %collective-permute-start.8 = (bf16[16,2048]{1,0:T(8,128)(2,1)S(1)}, bf16[16,2048]{1,0:T(8,128)(2,1)S(1)}, u32[]{:S(2)}, u32[]{:S(2)}) collective-permute-start(bf16[16,2048]{1,0:T(8,128)(2,1)S(1)} %pad_add_fusion.1.refs_0_), channel_id=1, source_target_pairs={{0,2},{1,3},{2,0},{3,1},{4,6},{5,7},{6,4},{7,5},{8,10},{9,11},{10,... | collective-permute-start | bytes 196616 | tf_op jit(solution)/shard_map/ppermute | solution.py:51
  26.0 1.3 %collective-permute-start.9 = (bf16[16,2048]{1,0:T(8,128)(2,1)S(1)}, bf16[16,2048]{1,0:T(8,128)(2,1)S(1)}, u32[]{:S(2)}, u32[]{:S(2)}) collective-permute-start(bf16[16,2048]{1,0:T(8,128)(2,1)S(1)} %pad_add_fusion.refs_1_), channel_id=1, source_target_pairs={{0,2},{1,3},{2,0},{3,1},{4,6},{5,7},{6,4},{7,5},{8,10},{9,11},{10,... | collective-permute-start | bytes 196616 | tf_op jit(solution)/shard_map/ppermute | solution.py:51

commit v8 on v7

--- a/solution.py
+++ b/solution.py
@@ -95,7 +95,7 @@
         ],
         compiler_params=pltpu.CompilerParams(vmem_limit_bytes=PROJECT_VMEM),
         cost_estimate=pl.CostEstimate(
-            flops=4 * slices * tokens * features * width,
+            flops=1 << 30,
             bytes_accessed=8 * slices * tokens * features,
             transcendentals=0,
         ),

time: 30.1 us -> 30 us (level)
  waiting for transfers between devices: 10 us -> 11.5 us
  local copies, waits for them, and re-layouts: 1.52 us -> 0.05 us
    unnamed x8, local copies, waits for them, and re-layouts: 1.49 us -> 0.02 us
    ppermute x10, waiting for transfers between devices: 10 us -> 11.5 us  [swap(): return lax.ppermute(value, axes, pairs)]
where the time goes in v8:
time: 30 us; the launch traced here: 29.8 us
  waiting for transfers between devices  11.5 us (38%)
  starting transfers between devices  11 us (37%)
  Pallas kernels  5.57 us (19%)
  other arithmetic  1.57 us (5%)
    ppermute x10, waiting for transfers between devices, swap(): return lax.ppermute(value, axes, pairs)  11.5 us
    ppermute x10, starting transfers between devices, swap(): return lax.ppermute(value, axes, pairs)  11 us
    pallas_call x1, Pallas kernels, scores(): pl.pallas_call(functools.partial(score_kernel, order, wide, len(held) + l...  2.54 us
    pallas_call x1, Pallas kernels, project(): pl.pallas_call(functools.partial(project_kernel, width_in), out_shape=(ou...  2.14 us
    concatenate x1, other arithmetic, on_device(): proj = jnp.concatenate([in_projection.T, out_projection.T], axis=0)  0.86 us
  transfers between devices with their start and end apart: 10, of which 9 were waited for; matrix products, arithmetic and copies ran while one was open for 0% of the time, Pallas kernels for 1%

profile of v8, /device:TPU:0, one launch (start us, length us, event | category | flops | bytes accessed | tf_op | source)
XLA Modules:
  0.0 29.8 jit_solution(11640045233765448049)
XLA Ops:
  0.0 0.0 copy-start
  0.0 0.0 copy-start.1
  0.0 0.9 %pad_maximum_fusion.proj = bf16[96,512]{1,0:T(8,128)(2,1)S(1)} fusion(bf16[64,512]{1,0:T(8,128)(2,1)} %bitcast.18, bf16[32,512]{1,0:T(8,128)(2,1)} %bitcast.19), kind=kLoop, calls=%fused_computation.13 | loop fusion | flops 196608 | bytes 196608 | tf_op jit(solution)/shard_map/concatenate | solution.py:241
  0.9 2.1 %shard_map.73 = (f32[2,96,256]{2,1,0:T(8,128)S(1)}, f32[2,96,256]{2,1,0:T(8,128)S(1)}) custom-call(bf16[1024,512]{1,0:T(8,128)(2,1)} %acts.1, bf16[1024,512]{1,0:T(8,128)(2,1)} %grads.1, bf16[96,512]{1,0:T(8,128)(2,1)S(1)} %pad_maximum_fusion.proj), custom_call_target="tpu_custom_call" | custom-call | flops 1073741824 | bytes 2097152 | tf_op jit(solution)/shard_map/pallas_call | solution.py:86
  3.0 0.5 %collective-permute-start = (f32[2,96,256]{2,1,0:T(8,128)S(1)}, f32[2,96,256]{2,1,0:T(8,128)S(1)}, u32[]{:S(2)}, u32[]{:S(2)}) collective-permute-start(f32[2,96,256]{2,1,0:T(8,128)S(1)} %get-tuple-element.10), channel_id=1, source_target_pairs={{0,2},{1,3},{2,0},{3,1},{4,6},{5,7},{6,4},{7,5},{8,10},{9,11},{10,... | collective-permute-start | bytes 589832 | tf_op jit(solution)/shard_map/ppermute | solution.py:51
  3.5 1.1 %collective-permute-done = f32[2,96,256]{2,1,0:T(8,128)S(1)} collective-permute-done((f32[2,96,256]{2,1,0:T(8,128)S(1)}, f32[2,96,256]{2,1,0:T(8,128)S(1)}, u32[]{:S(2)}, u32[]{:S(2)}) %collective-permute-start) | collective-permute-done | bytes 196640 | tf_op jit(solution)/shard_map/ppermute | solution.py:51
  4.7 0.1 select_convert_fusion.2
  4.9 3.0 %collective-permute-start.3 = (f16[98,256]{1,0:T(8,128)(2,1)S(1)}, f16[98,256]{1,0:T(8,128)(2,1)S(1)}, u32[]{:S(2)}, u32[]{:S(2)}) collective-permute-start(f16[98,256]{1,0:T(8,128)(2,1)S(1)} %get-tuple-element.28), channel_id=1, source_target_pairs={{0,8},{1,9},{2,10},{3,11},{4,12},{5,13},{6,14},{7,15},{8,0},{9,1},... | collective-permute-start | bytes 150536 | tf_op jit(solution)/shard_map/ppermute | solution.py:51
  7.9 1.0 %collective-permute-start.2 = (f16[98,256]{1,0:T(8,128)(2,1)S(1)}, f16[98,256]{1,0:T(8,128)(2,1)S(1)}, u32[]{:S(2)}, u32[]{:S(2)}) collective-permute-start(f16[98,256]{1,0:T(8,128)(2,1)S(1)} %get-tuple-element.27), channel_id=1, source_target_pairs={{0,6},{1,7},{2,4},{3,5},{4,2},{5,3},{6,0},{7,1},{8,14},{9,15},{10,... | collective-permute-start | bytes 150536 | tf_op jit(solution)/shard_map/ppermute | solution.py:51
  8.9 0.3 %collective-permute-start.1 = (f16[98,256]{1,0:T(8,128)(2,1)S(1)}, f16[98,256]{1,0:T(8,128)(2,1)S(1)}, u32[]{:S(2)}, u32[]{:S(2)}) collective-permute-start(f16[98,256]{1,0:T(8,128)(2,1)S(1)} %get-tuple-element.27), channel_id=1, source_target_pairs={{0,14},{1,15},{2,12},{3,13},{4,10},{5,11},{6,8},{7,9},{8,6},{9,7},... | collective-permute-start | bytes 150536 | tf_op jit(solution)/shard_map/ppermute | solution.py:51
  9.2 0.9 %collective-permute-done.3 = f16[98,256]{1,0:T(8,128)(2,1)S(1)} collective-permute-done((f16[98,256]{1,0:T(8,128)(2,1)S(1)}, f16[98,256]{1,0:T(8,128)(2,1)S(1)}, u32[]{:S(2)}, u32[]{:S(2)}) %collective-permute-start.3) | collective-permute-done | bytes 50208 | tf_op jit(solution)/shard_map/ppermute | solution.py:51
  10.0 1.9 %collective-permute-done.2 = f16[98,256]{1,0:T(8,128)(2,1)S(1)} collective-permute-done((f16[98,256]{1,0:T(8,128)(2,1)S(1)}, f16[98,256]{1,0:T(8,128)(2,1)S(1)}, u32[]{:S(2)}, u32[]{:S(2)}) %collective-permute-start.2) | collective-permute-done | bytes 50208 | tf_op jit(solution)/shard_map/ppermute | solution.py:51
  12.0 1.3 %collective-permute-done.1 = f16[98,256]{1,0:T(8,128)(2,1)S(1)} collective-permute-done((f16[98,256]{1,0:T(8,128)(2,1)S(1)}, f16[98,256]{1,0:T(8,128)(2,1)S(1)}, u32[]{:S(2)}, u32[]{:S(2)}) %collective-permute-start.1) | collective-permute-done | bytes 50208 | tf_op jit(solution)/shard_map/ppermute | solution.py:51
  13.3 0.1 fusion.1
  13.6 0.1 select_convert_fusion
  13.7 2.9 %collective-permute-start.4 = (f16[98,256]{1,0:T(8,128)(2,1)S(1)}, f16[98,256]{1,0:T(8,128)(2,1)S(1)}, u32[]{:S(2)}, u32[]{:S(2)}) collective-permute-start(f16[98,256]{1,0:T(8,128)(2,1)S(1)} %select_convert_fusion), channel_id=1, source_target_pairs={{0,18},{1,19},{2,16},{3,17},{4,22},{5,23},{6,20},{7,21},{8,26},{9,... | collective-permute-start | bytes 150536 | tf_op jit(solution)/shard_map/ppermute | solution.py:51
  16.6 0.0 copy-done
  16.6 0.0 copy-done.1
  16.6 0.0 slice-start
  16.6 0.4 %shard_map.74 = (bf16[256,2048]{1,0:T(8,128)(2,1)S(1)}, bf16[128,128]{1,0:T(8,128)(2,1)S(1)}) custom-call(f32[32,32]{1,0:T(8,128)S(1)} %copy-done.1, f32[64,64]{1,0:T(8,128)S(1)} %copy-done), custom_call_target="tpu_custom_call" | custom-call | flops 8589934592 | bytes 16777216 | tf_op jit(solution)/shard_map/pallas_call | solution.py:127
  17.0 2.9 %collective-permute-done.4 = f16[98,256]{1,0:T(8,128)(2,1)S(1)} collective-permute-done((f16[98,256]{1,0:T(8,128)(2,1)S(1)}, f16[98,256]{1,0:T(8,128)(2,1)S(1)}, u32[]{:S(2)}, u32[]{:S(2)}) %collective-permute-start.4) | collective-permute-done | bytes 50208 | tf_op jit(solution)/shard_map/ppermute | solution.py:51
  20.0 0.0 slice-start.1
  20.0 0.1 fusion.summed
  20.1 0.5 %shard_map.75 = bf16[8,2048]{1,0:T(8,128)(2,1)S(1)} custom-call(f32[96,256]{1,0:T(8,128)S(1)} %fusion.summed, bf16[256,2048]{1,0:T(8,128)(2,1)S(1)} %get-tuple-element.11.spread_out, bf16[128,128]{1,0:T(8,128)(2,1)S(1)} %get-tuple-element.12.spread_in), custom_call_target="tpu_custom_call" | custom-call | flops 8589934592 | bytes 16777216 | tf_op jit(solution)/shard_map/pallas_call | solution.py:160
  20.6 1.3 %collective-permute-start.5 = (bf16[8,2048]{1,0:T(8,128)(2,1)S(1)}, bf16[8,2048]{1,0:T(8,128)(2,1)S(1)}, u32[]{:S(2)}, u32[]{:S(2)}) collective-permute-start(bf16[8,2048]{1,0:T(8,128)(2,1)S(1)} %shard_map.75), channel_id=1, source_target_pairs={{0,7},{1,6},{2,5},{3,4},{4,3},{5,2},{6,1},{7,0},{8,15},{9,14},{10,... | collective-permute-start | bytes 98312 | tf_op jit(solution)/shard_map/ppermute | solution.py:51
  21.9 0.5 %collective-permute-start.7 = (bf16[8,2048]{1,0:T(8,128)(2,1)S(1)}, bf16[8,2048]{1,0:T(8,128)(2,1)S(1)}, u32[]{:S(2)}, u32[]{:S(2)}) collective-permute-start(bf16[8,2048]{1,0:T(8,128)(2,1)S(1)} %shard_map.75), channel_id=1, source_target_pairs={{0,1},{1,0},{2,3},{3,2},{4,5},{5,4},{6,7},{7,6},{8,9},{9,8},{10,11... | collective-permute-start | bytes 98312 | tf_op jit(solution)/shard_map/ppermute | solution.py:51
  22.4 1.2 %collective-permute-start.6 = (bf16[8,2048]{1,0:T(8,128)(2,1)S(1)}, bf16[8,2048]{1,0:T(8,128)(2,1)S(1)}, u32[]{:S(2)}, u32[]{:S(2)}) collective-permute-start(bf16[8,2048]{1,0:T(8,128)(2,1)S(1)} %shard_map.75), channel_id=1, source_target_pairs={{0,6},{1,7},{2,4},{3,5},{4,2},{5,3},{6,0},{7,1},{8,14},{9,15},{10,... | collective-permute-start | bytes 98312 | tf_op jit(solution)/shard_map/ppermute | solution.py:51
  23.6 1.3 %collective-permute-done.5 = bf16[8,2048]{1,0:T(8,128)(2,1)S(1)} collective-permute-done((bf16[8,2048]{1,0:T(8,128)(2,1)S(1)}, bf16[8,2048]{1,0:T(8,128)(2,1)S(1)}, u32[]{:S(2)}, u32[]{:S(2)}) %collective-permute-start.5) | collective-permute-done | bytes 32800 | tf_op jit(solution)/shard_map/ppermute | solution.py:51
  24.9 0.1 collective-permute-start.8
  25.1 0.8 %collective-permute-done.7 = bf16[8,2048]{1,0:T(8,128)(2,1)S(1)} collective-permute-done((bf16[8,2048]{1,0:T(8,128)(2,1)S(1)}, bf16[8,2048]{1,0:T(8,128)(2,1)S(1)}, u32[]{:S(2)}, u32[]{:S(2)}) %collective-permute-start.7) | collective-permute-done | bytes 32800 | tf_op jit(solution)/shard_map/ppermute | solution.py:51
  25.9 0.0 collective-permute-done.6
  25.9 0.1 collective-permute-start.9
  26.1 0.1 collective-permute-done.8.refs_2_
  26.2 1.1 %collective-permute-done.9.refs_3_ = bf16[16,2048]{1,0:T(8,128)(2,1)S(1)} collective-permute-done((bf16[16,2048]{1,0:T(8,128)(2,1)S(1)}, bf16[16,2048]{1,0:T(8,128)(2,1)S(1)}, u32[]{:S(2)}, u32[]{:S(2)}) %collective-permute-start.9) | collective-permute-done | bytes 65568 | tf_op jit(solution)/shard_map/ppermute | solution.py:51
  27.3 0.0 slice-done
  27.3 0.0 slice-done.1
  27.3 2.5 %shard_map.76 = f32[64,1536]{1,0:T(8,128)} custom-call(bf16[16,2048]{1,0:T(8,128)(2,1)S(1)} %pad_add_fusion.1.refs_0_, bf16[16,2048]{1,0:T(8,128)(2,1)S(1)} %pad_add_fusion.refs_1_, bf16[16,2048]{1,0:T(8,128)(2,1)S(1)} %collective-permute-done.8.refs_2_, bf16[16,2048]{1,0:T(8,128)(2,1)S(1)} %collective-permute-done.9.refs_3_, bf16[1536,2048]{1,0:T(8,128)(2,1)S(1)} %bitcast.17), custom_call_target="tpu_custom_call" | custom-call | tf_op jit(solution)/shard_map/pallas_call | solution.py:193
  (24 shorter events, 0.2 us)
Async XLA Ops:
  0.0 16.6 %copy-start = (f32[64,64]{1,0:T(8,128)S(1)}, f32[64,64]{1,0:T(8,128)}, u32[]{:S(2)}) copy-start(f32[64,64]{1,0:T(8,128)} %out_inverse.1) | copy-start | bytes 49156
  0.0 16.6 %copy-start.1 = (f32[32,32]{1,0:T(8,128)S(1)}, f32[32,32]{1,0:T(8,128)}, u32[]{:S(2)}) copy-start(f32[32,32]{1,0:T(8,128)} %in_inverse.1) | copy-start | bytes 12292
  3.0 1.6 %collective-permute-start = (f32[2,96,256]{2,1,0:T(8,128)S(1)}, f32[2,96,256]{2,1,0:T(8,128)S(1)}, u32[]{:S(2)}, u32[]{:S(2)}) collective-permute-start(f32[2,96,256]{2,1,0:T(8,128)S(1)} %get-tuple-element.10), channel_id=1, source_target_pairs={{0,2},{1,3},{2,0},{3,1},{4,6},{5,7},{6,4},{7,5},{8,10},{9,11},{10,... | collective-permute-start | bytes 589832 | tf_op jit(solution)/shard_map/ppermute | solution.py:51
  4.9 5.1 %collective-permute-start.3 = (f16[98,256]{1,0:T(8,128)(2,1)S(1)}, f16[98,256]{1,0:T(8,128)(2,1)S(1)}, u32[]{:S(2)}, u32[]{:S(2)}) collective-permute-start(f16[98,256]{1,0:T(8,128)(2,1)S(1)} %get-tuple-element.28), channel_id=1, source_target_pairs={{0,8},{1,9},{2,10},{3,11},{4,12},{5,13},{6,14},{7,15},{8,0},{9,1},... | collective-permute-start | bytes 150536 | tf_op jit(solution)/shard_map/ppermute | solution.py:51
  7.9 4.1 %collective-permute-start.2 = (f16[98,256]{1,0:T(8,128)(2,1)S(1)}, f16[98,256]{1,0:T(8,128)(2,1)S(1)}, u32[]{:S(2)}, u32[]{:S(2)}) collective-permute-start(f16[98,256]{1,0:T(8,128)(2,1)S(1)} %get-tuple-element.27), channel_id=1, source_target_pairs={{0,6},{1,7},{2,4},{3,5},{4,2},{5,3},{6,0},{7,1},{8,14},{9,15},{10,... | collective-permute-start | bytes 150536 | tf_op jit(solution)/shard_map/ppermute | solution.py:51
  8.9 4.5 %collective-permute-start.1 = (f16[98,256]{1,0:T(8,128)(2,1)S(1)}, f16[98,256]{1,0:T(8,128)(2,1)S(1)}, u32[]{:S(2)}, u32[]{:S(2)}) collective-permute-start(f16[98,256]{1,0:T(8,128)(2,1)S(1)} %get-tuple-element.27), channel_id=1, source_target_pairs={{0,14},{1,15},{2,12},{3,13},{4,10},{5,11},{6,8},{7,9},{8,6},{9,7},... | collective-permute-start | bytes 150536 | tf_op jit(solution)/shard_map/ppermute | solution.py:51
  13.7 6.2 %collective-permute-start.4 = (f16[98,256]{1,0:T(8,128)(2,1)S(1)}, f16[98,256]{1,0:T(8,128)(2,1)S(1)}, u32[]{:S(2)}, u32[]{:S(2)}) collective-permute-start(f16[98,256]{1,0:T(8,128)(2,1)S(1)} %select_convert_fusion), channel_id=1, source_target_pairs={{0,18},{1,19},{2,16},{3,17},{4,22},{5,23},{6,20},{7,21},{8,26},{9,... | collective-permute-start | bytes 150536 | tf_op jit(solution)/shard_map/ppermute | solution.py:51
  16.6 10.7 %slice-start = ((s8[6291456]{0:T(1024)(128)(4,1)}), s8[4194304]{0:T(1024)(128)(4,1)S(1)}, s32[]{:S(2)}) async-start(s8[6291456]{0:T(1024)(128)(4,1)} %bitcast.16), calls=%async_computation | async-start | bytes 8388608
  20.0 7.3 %slice-start.1 = ((s8[6291456]{0:T(1024)(128)(4,1)}), s8[2097152]{0:T(1024)(128)(4,1)S(1)}, s32[]{:S(2)}) async-start(s8[6291456]{0:T(1024)(128)(4,1)} %bitcast.16), calls=%async_computation.1 | async-start | bytes 4194304
  20.6 4.4 %collective-permute-start.5 = (bf16[8,2048]{1,0:T(8,128)(2,1)S(1)}, bf16[8,2048]{1,0:T(8,128)(2,1)S(1)}, u32[]{:S(2)}, u32[]{:S(2)}) collective-permute-start(bf16[8,2048]{1,0:T(8,128)(2,1)S(1)} %shard_map.75), channel_id=1, source_target_pairs={{0,7},{1,6},{2,5},{3,4},{4,3},{5,2},{6,1},{7,0},{8,15},{9,14},{10,... | collective-permute-start | bytes 98312 | tf_op jit(solution)/shard_map/ppermute | solution.py:51
  21.9 4.0 %collective-permute-start.7 = (bf16[8,2048]{1,0:T(8,128)(2,1)S(1)}, bf16[8,2048]{1,0:T(8,128)(2,1)S(1)}, u32[]{:S(2)}, u32[]{:S(2)}) collective-permute-start(bf16[8,2048]{1,0:T(8,128)(2,1)S(1)} %shard_map.75), channel_id=1, source_target_pairs={{0,1},{1,0},{2,3},{3,2},{4,5},{5,4},{6,7},{7,6},{8,9},{9,8},{10,11... | collective-permute-start | bytes 98312 | tf_op jit(solution)/shard_map/ppermute | solution.py:51
  22.4 3.5 %collective-permute-start.6 = (bf16[8,2048]{1,0:T(8,128)(2,1)S(1)}, bf16[8,2048]{1,0:T(8,128)(2,1)S(1)}, u32[]{:S(2)}, u32[]{:S(2)}) collective-permute-start(bf16[8,2048]{1,0:T(8,128)(2,1)S(1)} %shard_map.75), channel_id=1, source_target_pairs={{0,6},{1,7},{2,4},{3,5},{4,2},{5,3},{6,0},{7,1},{8,14},{9,15},{10,... | collective-permute-start | bytes 98312 | tf_op jit(solution)/shard_map/ppermute | solution.py:51
  24.9 1.3 %collective-permute-start.8 = (bf16[16,2048]{1,0:T(8,128)(2,1)S(1)}, bf16[16,2048]{1,0:T(8,128)(2,1)S(1)}, u32[]{:S(2)}, u32[]{:S(2)}) collective-permute-start(bf16[16,2048]{1,0:T(8,128)(2,1)S(1)} %pad_add_fusion.1.refs_0_), channel_id=1, source_target_pairs={{0,2},{1,3},{2,0},{3,1},{4,6},{5,7},{6,4},{7,5},{8,10},{9,11},{10,... | collective-permute-start | bytes 196616 | tf_op jit(solution)/shard_map/ppermute | solution.py:51
  25.9 1.3 %collective-permute-start.9 = (bf16[16,2048]{1,0:T(8,128)(2,1)S(1)}, bf16[16,2048]{1,0:T(8,128)(2,1)S(1)}, u32[]{:S(2)}, u32[]{:S(2)}) collective-permute-start(bf16[16,2048]{1,0:T(8,128)(2,1)S(1)} %pad_add_fusion.refs_1_), channel_id=1, source_target_pairs={{0,2},{1,3},{2,0},{3,1},{4,6},{5,7},{6,4},{7,5},{8,10},{9,11},{10,... | collective-permute-start | bytes 196616 | tf_op jit(solution)/shard_map/ppermute | solution.py:51
